TPU v7x, 32 devices: a whole 2x2x4 slice. The times are simulated.
32 devices in a mesh: group: 8 (over z, x), batch: 4 (over y, core).
Axes of the slice: x: 2, y: 2, z: 4, core: 2. Of those that a mesh axis runs over, the one named last changes fastest.
Arguments:
- mixed_input: bfloat16 [8192, 2816], P(('batch', 'group')), parts along dimension 0, may hold values from -6 to 6
- conv_weight: float32 [4, 2816], replicated, may hold values from -3 to 3
- conv_bias: float32 [2816], replicated, may hold values from -3 to 3
- gate_input: bfloat16 [8192, 2560], P(('batch', 'group')), parts along dimension 0, may hold values from -6 to 6
- log_decay: float32 [40, 8192], P(None, ('batch', 'group')), parts along dimension 1, may hold values from -0.76 to 0, as said below
- level_weights: float32 [40, 20, 8192], P(None, None, ('batch', 'group')), parts along dimension 2, may hold values from 0.2 to 2
- skip_gain: float32 [40], replicated, may hold values from 0.3 to 3
- norm_gain: float32 [2560], replicated, may hold values from 0.25 to 1.75
- seg_lengths: int32 [12], P('batch'), parts along dimension 0, may hold values from 1 to 1280, 2048 in all
Outputs:
- output: bfloat16 [8192, 2560], P(('batch', 'group')), parts along dimension 0
There are 4 independent parts, one for each index of `batch`. A program takes and returns all parts, laid end to end along the dimension named above; an argument that names none is the same for every part. Nothing has to cross between parts.
Inputs may be any that keep to these rules, and one draw needn't show every extreme that they name: `seg_lengths`: the recordings' lengths in order; they sum to 2048 and the longest is exactly 1280. `log_decay`: every entry is negative.
All inputs are finite; a program needn't handle non-finite values.
Results may differ from a plain program's by a relative error of at most 0.0034.
Values may be sent and summed in bfloat16 or wider, within the bound.
No kernel may reach another device: no remote copies, remote signals or barrier semaphores. Data moves between devices by JAX's collectives and lax.ppermute only.
A program may use at most 128 MiB of HBM per device.

v0:
```python
import jax
import jax.numpy as jnp
from jax import lax
from jax.sharding import PartitionSpec as P

eps_norm = 1e-05


def shifted(array, axis, by):
    peers = lax.axis_size(axis)
    pairs = [(i, i + by) for i in range(peers) if 0 <= i + by < peers]
    return lax.ppermute(array, axis, pairs)


def partner(value, axis, apart):
    mask = 2**apart
    pairs = [(source, source ^ mask) for source in range(lax.axis_size(axis))]
    return lax.ppermute(value, axis, pairs)


def segment_of(positions, seg_lengths):
    bounds = jnp.cumsum(seg_lengths)[:-1]
    found = jnp.sum((positions[:, None] >= bounds[None, :]).astype(jnp.int32), axis=1)
    return jnp.where(positions >= 0, found, -1)


def pair_levels(count, low_bits):
    index = jnp.arange(count, dtype=jnp.int32)
    diff = jnp.bitwise_xor(index[:, None], index[None, :])
    levels = jnp.zeros((count, count), jnp.int32)
    for bit_index in range(low_bits):
        levels = levels + (diff >= 2**bit_index).astype(jnp.int32)
    return levels


def convolve(rows, segs, conv_weight, conv_bias, taps):
    count = rows.shape[0] - (taps - 1)
    total = jnp.zeros((count, rows.shape[1]), jnp.float32) + conv_bias[None, :]
    for tap in range(taps):
        begin = taps - 1 - tap
        piece = rows[begin : begin + count].astype(jnp.float32)
        same = (segs[begin : begin + count] == segs[taps - 1 :]).astype(jnp.float32)
        total = total + conv_weight[tap][None, :] * piece * same[:, None]
    return jax.nn.silu(total)


def head_block():
    for block_try in (8, 5, 4, 2):
        return block_try
    return 1


def per_device(
    mixed_input,
    conv_weight,
    conv_bias,
    gate_input,
    log_decay,
    level_weights,
    skip_gain,
    norm_gain,
    seg_lengths,
):
    tok_rows = mixed_input.shape[0]
    width = gate_input.shape[1]
    head_count = log_decay.shape[0]
    head_dim = width // head_count
    state_dim = (mixed_input.shape[1] - width) // 2
    taps = conv_weight.shape[0]
    low_bits = tok_rows.bit_length() - 1
    group_count = lax.axis_size("group")
    high_bits = group_count.bit_length() - 1
    group_index = lax.axis_index("group")
    first_pos = group_index * tok_rows
    positions = first_pos + jnp.arange(tok_rows, dtype=jnp.int32)
    segments = segment_of(positions, seg_lengths)
    rim_segs = segment_of(
        first_pos - (taps - 1) + jnp.arange(taps - 1, dtype=jnp.int32), seg_lengths
    )
    rim_rows = shifted(mixed_input[tok_rows - (taps - 1) :], "group", 1)
    activated = convolve(
        jnp.concatenate([rim_rows, mixed_input], axis=0),
        jnp.concatenate([rim_segs, segments], axis=0),
        conv_weight,
        conv_bias,
        taps,
    )
    xs = activated[:, :width].astype(jnp.bfloat16)
    keys = activated[:, width : width + state_dim].astype(jnp.bfloat16)
    queries = activated[:, width + state_dim :].astype(jnp.bfloat16)
    cum = jnp.cumsum(log_decay, axis=1)
    prev_seg = segment_of(jnp.reshape(first_pos - 1, (1,)), seg_lengths)[0]
    entry = jnp.exp(cum) * (segments == prev_seg).astype(jnp.float32)[None, :]
    same_end = (segments == segments[-1]).astype(jnp.float32)
    end_weight = jnp.exp(cum[:, -1:] - cum) * same_end[None, :]
    scaled = (
        (xs.astype(jnp.float32).reshape(tok_rows, head_count, head_dim) * end_weight.T[:, :, None])
        .astype(jnp.bfloat16)
        .reshape(tok_rows, width)
    )
    end_state = lax.dot_general(
        keys, scaled, (((0,), (0,)), ((), ())), preferred_element_type=jnp.float32
    )
    through = jnp.exp(cum[:, -1]) * (segments[-1] == prev_seg).astype(jnp.float32)
    through_cols = jnp.repeat(through, head_dim)
    scores = jnp.dot(queries, keys.T, preferred_element_type=jnp.float32)
    pair_level = pair_levels(tok_rows, low_bits)
    row_ids = jnp.arange(tok_rows, dtype=jnp.int32)
    valid = (row_ids[None, :] <= row_ids[:, None]) & (segments[:, None] == segments[None, :])
    per_block = head_block()
    pieces = []
    for block_start in range(0, head_count, per_block):
        cum_block = cum[block_start : block_start + per_block]
        gap = jnp.where(valid[None], cum_block[:, :, None] - cum_block[:, None, :], 0.0)
        decay = jnp.exp(gap) * valid[None].astype(jnp.float32)
        picked = jnp.zeros_like(decay)
        for level_index in range(low_bits + 1):
            picked = jnp.where(
                pair_level[None] == level_index,
                level_weights[block_start : block_start + per_block, level_index, :, None],
                picked,
            )
        mixing = (scores[None] * picked * decay).astype(jnp.bfloat16)
        values = xs[:, block_start * head_dim : (block_start + per_block) * head_dim].reshape(
            tok_rows, per_block, head_dim
        )
        pieces.append(
            jnp.einsum("hts,shp->thp", mixing, values, preferred_element_type=jnp.float32)
        )
    local_part = jnp.concatenate(pieces, axis=1)
    far_part = jnp.zeros((tok_rows, head_count, head_dim), jnp.float32)
    running = end_state
    block_total = through_cols
    before = jnp.ones_like(through_cols)
    for bit_index in range(high_bits):
        far_state, far_total = partner((running, block_total), "group", bit_index)
        on_top = group_index // 2**bit_index % 2 == 1
        level_state = jnp.where(on_top, far_state * before[None, :], 0.0)
        read = jnp.dot(
            queries, level_state.astype(jnp.bfloat16), preferred_element_type=jnp.float32
        )
        factor = level_weights[:, low_bits + 1 + bit_index, :] * entry
        far_part = far_part + read.reshape(tok_rows, head_count, head_dim) * factor.T[:, :, None]
        if bit_index + 1 < high_bits:
            running = jnp.where(
                on_top,
                far_state * block_total[None, :] + running,
                running * far_total[None, :] + far_state,
            )
            before = jnp.where(on_top, far_total * before, before)
            block_total = block_total * far_total
    mixed_sum = (
        local_part
        + far_part
        + skip_gain[None, :, None] * xs.astype(jnp.float32).reshape(tok_rows, head_count, head_dim)
    )
    flat = mixed_sum.reshape(tok_rows, width)
    gated = flat * jax.nn.silu(gate_input.astype(jnp.float32))
    scale = lax.rsqrt(jnp.mean(gated * gated, axis=1, keepdims=True) + eps_norm)
    return (gated * scale * norm_gain[None, :]).astype(jnp.bfloat16)


def solution(mesh):
    in_specs = (
        P(("batch", "group"), None),
        P(),
        P(),
        P(("batch", "group"), None),
        P(None, ("batch", "group")),
        P(None, None, ("batch", "group")),
        P(),
        P(),
        P("batch"),
    )
    out_specs = P(("batch", "group"), None)
    return jax.shard_map(
        per_device, mesh=mesh, in_specs=in_specs, out_specs=out_specs, check_vma=False
    )
```

profile of v0, /device:TPU:0, one launch (start us, length us, event | category | flops | bytes accessed | tf_op | source)
XLA Modules:
  0.0 155.0 jit_solution(11975011083033121906)
XLA Ops:
  0.8 4.8 %collective-permute-start = (bf16[3,2816]{1,0:T(4,128)(2,1)S(1)}, bf16[3,2816]{1,0:T(4,128)(2,1)S(1)}, u32[]{:S(2)}, u32[]{:S(2)}) collective-permute-start(bf16[3,2816]{1,0:T(4,128)(2,1)S(1)} %slice.251), channel_id=1, source_target_pairs={{0,4},{4,8},{8,12},{12,16},{16,20},{20,24},{24,28},{1,5},{5,9},{9,... | collective-permute-start | bytes 50696 | tf_op jit(solution)/shard_map/ppermute | solution.py:12
  10.4 1.6 %collective-permute-start.2 = (f32[2560]{0:T(1024)S(1)}, f32[2560]{0:T(1024)S(1)}, u32[]{:S(2)}, u32[]{:S(2)}) collective-permute-start(f32[2560]{0:T(1024)S(1)} %mul.370), channel_id=1, source_target_pairs={{0,4},{4,0},{8,12},{12,8},{16,20},{20,16},{24,28},{28,24},{1,5},{5... | collective-permute-start | bytes 30728 | tf_op jit(solution)/shard_map/ppermute | solution.py:18
  14.8 1.4 slice_bitcast_fusion.49
  17.9 1.7 %mul.359 = f32[256,40,64]{0,2,1:T(8,128)} broadcast(f32[256,40]{0,1:T(8,128)S(1)} %get-tuple-element.66), dimensions={0,1} | broadcast | bytes 2662400 | tf_op jit(solution)/shard_map/mul | solution.py:97
  19.5 3.3 %copy.40 = f32[256,2560]{1,0:T(8,128)} copy(f32[256,2560]{0,1:T(8,128)} %bitcast.178) | data formatting | bytes 5242880 | tf_op jit(solution)/shard_map/mul | solution.py:97
  22.9 2.7 %multiply_convert_fusion = bf16[256,2816]{1,0:T(8,128)(2,1)S(1)} fusion(bf16[256,2816]{1,0:T(8,128)(2,1)S(1)} %copy-done.6, bf16[3,2816]{1,0:T(4,128)(2,1)S(1)} %collective-permute-done, f32[256]{0:T(256)S(1)} %get-tuple-element.73, f32[2816]{0:T(1024)S(1)} %get-tuple-element.7, f32[256]{0:T(256)S(1)} %get-tuple-element.74, f32[2816]{0:T(1024)S(1)} %get-tuple-element.8, ...), kind=kLoop, calls=%fused_computation.12 | loop fusion | flops 20905984 | bytes 2959872 | tf_op jit(solution)/shard_map/convert.2
  27.5 1.6 %slice_bitcast_fusion.31 = (f32[8,256]{1,0:T(8,128)}, f32[8,256]{1,0:T(8,128)}, f32[8,256]{1,0:T(8,128)}, f32[8,256]{1,0:T(8,128)}, f32[8,256]{1,0:T(8,128)}, /*...) fusion(f32[40,20,256]{2,0,1:T(8,128)} %param.14), kind=kLoop, calls=%fused_computation.251 | loop fusion | bytes 311296 | tf_op jit(solution)/shard_map/jit(_where)/broadcast_in_dim | solution.py:118
  29.0 1.6 %slice_bitcast_fusion.13 = (f32[8,256]{1,0:T(8,128)}, f32[8,256]{1,0:T(8,128)}, f32[8,256]{1,0:T(8,128)}, f32[8,256]{1,0:T(8,128)}, f32[8,256]{1,0:T(8,128)}, /*...) fusion(f32[40,20,256]{2,0,1:T(8,128)} %param.14), kind=kLoop, calls=%fused_computation.233 | loop fusion | bytes 311296 | tf_op jit(solution)/shard_map/jit(_where)/broadcast_in_dim | solution.py:118
  32.4 1.7 %mul.390 = f32[256,40,64]{0,2,1:T(8,128)} broadcast(f32[256,40]{0,1:T(8,128)S(1)} %get-tuple-element.19), dimensions={0,1} | broadcast | bytes 2662400 | tf_op jit(solution)/shard_map/mul | solution.py:143
  34.1 3.2 %copy.43 = f32[256,2560]{1,0:T(8,128)} copy(f32[256,2560]{0,1:T(8,128)} %bitcast.179) | data formatting | bytes 5242880 | tf_op jit(solution)/shard_map/mul | solution.py:143
  37.3 1.8 %mul.378 = f32[256,40,64]{0,2,1:T(8,128)} broadcast(f32[256,40]{0,1:T(8,128)S(1)} %get-tuple-element.20), dimensions={0,1} | broadcast | bytes 2662400 | tf_op jit(solution)/shard_map/mul | solution.py:143
  39.0 3.2 %copy.42 = f32[256,2560]{1,0:T(8,128)} copy(f32[256,2560]{0,1:T(8,128)} %bitcast.180) | data formatting | bytes 5242880 | tf_op jit(solution)/shard_map/mul | solution.py:143
  42.3 1.8 %mul.365 = f32[256,40,64]{0,2,1:T(8,128)} broadcast(f32[256,40]{0,1:T(8,128)S(1)} %get-tuple-element.18), dimensions={0,1} | broadcast | bytes 2662400 | tf_op jit(solution)/shard_map/mul | solution.py:143
  44.0 3.3 %copy.41 = f32[256,2560]{1,0:T(8,128)} copy(f32[256,2560]{0,1:T(8,128)} %bitcast.181) | data formatting | bytes 5242880 | tf_op jit(solution)/shard_map/mul | solution.py:143
  48.7 1.6 %collective-permute-start.4 = (f32[2560]{0:T(1024)}, f32[2560]{0:T(1024)S(1)}, u32[]{:S(2)}, u32[]{:S(2)}) collective-permute-start(f32[2560]{0:T(1024)} %mul.381), channel_id=1, source_target_pairs={{0,8},{4,12},{8,0},{12,4},{16,24},{20,28},{24,16},{28,20},{1,9},{5... | collective-permute-start | bytes 30728 | tf_op jit(solution)/shard_map/ppermute | solution.py:18
  51.2 1.8 %copy.33 = bf16[256,512]{0,1:T(8,128)(2,1)} copy(bf16[256,512]{1,0:T(8,128)(2,1)} %get-tuple-element.17) | data formatting | bytes 524288 | tf_op jit(solution)/shard_map/slice | solution.py:124
  53.0 1.8 %copy.35 = bf16[256,512]{0,1:T(8,128)(2,1)} copy(bf16[256,512]{1,0:T(8,128)(2,1)} %get-tuple-element.16) | data formatting | bytes 524288 | tf_op jit(solution)/shard_map/slice | solution.py:124
  54.8 1.8 %copy.36 = bf16[256,512]{0,1:T(8,128)(2,1)} copy(bf16[256,512]{1,0:T(8,128)(2,1)} %get-tuple-element.15) | data formatting | bytes 524288 | tf_op jit(solution)/shard_map/slice | solution.py:124
  57.0 2.1 %add_select_fusion.1 = f32[128,2560]{1,0:T(8,128)S(1)} fusion(f32[128,2560]{1,0:T(8,128)} %collective-permute-done.1, f32[128,2560]{1,0:T(8,128)} %copy-done.3, f32[2560]{0:T(1024)S(1)} %collective-permute-done.2, f32[2560]{0:T(1024)S(1)} %mul.370, pred[]{:T(512)S(6)} %eq.260), kind=kLoop, calls=%fused_computation.33 | loop fusion | flops 1638400 | bytes 3952641 | tf_op jit(solution)/shard_map/jit(_where)/select_n | solution.py:145
  60.1 4.1 %fusion.17 = f32[256,40,64]{0,2,1:T(8,128)} fusion(bf16[256,8,64]{0,2,1:T(8,128)(2,1)S(1)} %bitcast.184, f32[256,256]{1,0:T(8,128)S(1)} %copy-done.7, f32[8,256]{1,0:T(8,128)S(1)} %copy-done.43, f32[8,256]{1,0:T(8,128)S(1)} %copy-done.71, f32[8,256]{1,0:T(8,128)S(1)} %copy-done.72, f32[8,256]{1,0:T(8,128)S(1)} %copy-done.33, f32[8,256]{1,0:T(8,128)S(1)} %copy-done.34, ...), kind=kOutput, calls=%fused_computation.44 | convolution fusion | flops 74973184 | bytes 2056192 | tf_op jit(solution)/shard_map/hts,shp->thp/dot_general | solution.py:128
  64.4 4.1 %fusion.16 = f32[256,40,64]{0,2,1:T(8,128)} fusion(f32[256,40,64]{0,2,1:T(8,128)} %fusion.17, bf16[256,8,64]{0,2,1:T(8,128)(2,1)S(1)} %bitcast.183, f32[8,256]{1,0:T(8,128)S(1)} %copy-done.42, f32[8,256]{1,0:T(8,128)S(1)} %copy-done.62, f32[8,256]{1,0:T(8,128)S(1)} %copy-done.63, f32[8,256]{1,0:T(8,128)S(1)} %copy-done.64, f32[8,256]{1,0:T(8,128)S(1)} %copy-done.65, ...), kind=kOutput, calls=%fused_computation.42 | convolution fusion | flops 74973184 | bytes 2056192 | tf_op jit(solution)/shard_map/hts,shp->thp/dot_general | solution.py:128
  68.6 4.1 %fusion.15 = f32[256,40,64]{0,2,1:T(8,128)} fusion(f32[256,40,64]{0,2,1:T(8,128)} %fusion.16, bf16[256,8,64]{0,2,1:T(8,128)(2,1)S(1)} %bitcast.182, f32[8,256]{1,0:T(8,128)S(1)} %copy-done.41, f32[8,256]{1,0:T(8,128)S(1)} %copy-done.61, f32[8,256]{1,0:T(8,128)S(1)} %copy-done.54, f32[8,256]{1,0:T(8,128)S(1)} %copy-done.55, f32[8,256]{1,0:T(8,128)S(1)} %copy-done.56, ...), kind=kOutput, calls=%fused_computation.40 | convolution fusion | flops 74973184 | bytes 2056192 | tf_op jit(solution)/shard_map/hts,shp->thp/dot_general | solution.py:128
  73.7 15.0 %collective-permute-done.3 = f32[128,2560]{1,0:T(8,128)} collective-permute-done((f32[128,2560]{1,0:T(8,128)S(1)}, f32[128,2560]{1,0:T(8,128)}, u32[]{:S(2)}, u32[]{:S(2)}) %collective-permute-start.3) | collective-permute-done | bytes 1310752 | tf_op jit(solution)/shard_map/ppermute | solution.py:18
  88.7 2.7 %add_select_fusion = f32[128,2560]{1,0:T(8,128)} fusion(f32[128,2560]{1,0:T(8,128)} %collective-permute-done.3, f32[128,2560]{1,0:T(8,128)S(1)} %add_select_fusion.1, f32[2560]{0:T(1024)S(1)} %collective-permute-done.4, f32[2560]{0:T(1024)} %mul.381, pred[]{:T(512)S(6)} %eq.265), kind=kLoop, calls=%fused_computation.31 | loop fusion | flops 1638400 | bytes 3952641 | tf_op jit(solution)/shard_map/jit(_where)/select_n | solution.py:145
  91.4 2.6 %collective-permute-start.5 = (f32[128,2560]{1,0:T(8,128)}, f32[128,2560]{1,0:T(8,128)S(1)}, u32[]{:S(2)}, u32[]{:S(2)}) collective-permute-start(f32[128,2560]{1,0:T(8,128)} %add_select_fusion), channel_id=1, source_target_pairs={{0,16},{4,20},{8,24},{12,28},{16,0},{20,4},{24,8},{28,12},{1,17},{... | collective-permute-start | bytes 3932168 | tf_op jit(solution)/shard_map/ppermute | solution.py:18
  94.2 4.2 %fusion.14 = f32[256,40,64]{0,2,1:T(8,128)} fusion(f32[256,40,64]{0,2,1:T(8,128)} %fusion.15, bf16[256,8,64]{0,2,1:T(8,128)(2,1)S(1)} %bitcast.186, f32[8,256]{1,0:T(8,128)S(1)} %copy-done.40, f32[8,256]{1,0:T(8,128)S(1)} %copy-done.44, f32[8,256]{1,0:T(8,128)S(1)} %copy-done.45, f32[8,256]{1,0:T(8,128)S(1)} %copy-done.46, f32[8,256]{1,0:T(8,128)S(1)} %copy-done.47, ...), kind=kOutput, calls=%fused_computation.38 | convolution fusion | flops 74973184 | bytes 2056192 | tf_op jit(solution)/shard_map/hts,shp->thp/dot_general | solution.py:128
  99.2 5.3 %fusion.13 = f32[256,40,64]{0,2,1:T(8,128)} fusion(f32[256,40,64]{0,2,1:T(8,128)} %fusion.14, bf16[256,8,64]{0,2,1:T(8,128)(2,1)} %bitcast.185, f32[8,256]{1,0:T(8,128)S(1)} %copy-done.39, f32[8,256]{1,0:T(8,128)} %get-tuple-element.22, f32[8,256]{1,0:T(8,128)} %get-tuple-element.23, f32[8,256]{1,0:T(8,128)} %get-tuple-element.24, ...), kind=kOutput, calls=%fused_computation.36 | convolution fusion | flops 74973184 | bytes 2056192 | tf_op jit(solution)/shard_map/hts,shp->thp/dot_general | solution.py:128
  104.4 3.3 %copy.44 = f32[256,2560]{1,0:T(8,128)} copy(f32[256,2560]{0,1:T(8,128)} %bitcast.62) | data formatting | bytes 5242880 | tf_op jit(solution)/shard_map/concatenate | solution.py:130
  107.8 2.8 %convolution_multiply_fusion.1 = f32[256,2560]{1,0:T(8,128)S(1)} fusion(f32[256,2560]{1,0:T(8,128)} %copy.42, f32[128,2560]{1,0:T(8,128)} %collective-permute-done.3, f32[2560]{0:T(1024)S(1)} %get-tuple-element.10, pred[]{:T(512)S(6)} %eq.265, bf16[256,2816]{1,0:T(8,128)(2,1)S(1)} %multiply_convert_fusion), kind=kOutput, calls=%fused_computation.1 | convolution fusion | flops 169410560 | bytes 6631425 | tf_op jit(solution)/shard_map/dot_general | solution.py:139
  110.6 38.3 %collective-permute-done.5 = f32[128,2560]{1,0:T(8,128)S(1)} collective-permute-done((f32[128,2560]{1,0:T(8,128)}, f32[128,2560]{1,0:T(8,128)S(1)}, u32[]{:S(2)}, u32[]{:S(2)}) %collective-permute-start.5) | collective-permute-done | bytes 1310752 | tf_op jit(solution)/shard_map/ppermute | solution.py:18
  151.8 1.8 %multiply_reduce_fusion = (f32[256]{0:T(256)S(1)}, f32[256,2560]{1,0:T(8,128)S(1)}) fusion(bf16[256,2560]{1,0:T(8,128)(2,1)S(1)} %copy-done.74, bf16[256,2816]{1,0:T(8,128)(2,1)S(1)} %multiply_convert_fusion, f32[2560]{0:T(1024)S(1)} %copy-done.31, f32[256,2560]{1,0:T(8,128)S(1)} %copy-done.5, f32[256,2560]{1,0:T(8,128)S(1)} %convolution_multiply_fusion, ...), kind=kOutput, calls=%fused_computation.18 | convolution fusion | flops 177929984 | bytes 17118208 | tf_op jit(solution)/shard_map/dot_general | solution.py:139
  153.7 1.3 multiply_convert_fusion.1
  (198 shorter events, 20.2 us)
Async XLA Ops:
  0.0 8.5 %copy-start = (f32[40,256]{1,0:T(8,128)S(1)}, f32[40,256]{1,0:T(8,128)}, u32[]{:S(2)}) copy-start(f32[40,256]{1,0:T(8,128)} %param.13) | copy-start | bytes 122884
  0.8 22.1 %collective-permute-start = (bf16[3,2816]{1,0:T(4,128)(2,1)S(1)}, bf16[3,2816]{1,0:T(4,128)(2,1)S(1)}, u32[]{:S(2)}, u32[]{:S(2)}) collective-permute-start(bf16[3,2816]{1,0:T(4,128)(2,1)S(1)} %slice.251), channel_id=1, source_target_pairs={{0,4},{4,8},{8,12},{12,16},{16,20},{20,24},{24,28},{1,5},{5,9},{9,... | collective-permute-start | bytes 50696 | tf_op jit(solution)/shard_map/ppermute | solution.py:12
  10.4 37.7 %collective-permute-start.2 = (f32[2560]{0:T(1024)S(1)}, f32[2560]{0:T(1024)S(1)}, u32[]{:S(2)}, u32[]{:S(2)}) collective-permute-start(f32[2560]{0:T(1024)S(1)} %mul.370), channel_id=1, source_target_pairs={{0,4},{4,0},{8,12},{12,8},{16,20},{20,16},{24,28},{28,24},{1,5},{5... | collective-permute-start | bytes 30728 | tf_op jit(solution)/shard_map/ppermute | solution.py:18
  26.1 11.2 %copy-start.3 = (f32[128,2560]{1,0:T(8,128)}, f32[128,2560]{1,0:T(8,128)S(1)}, u32[]{:S(2)}) copy-start(f32[128,2560]{1,0:T(8,128)S(1)} %fusion.11) | copy-start | bytes 3932164
  26.1 30.8 %collective-permute-start.1 = (f32[128,2560]{1,0:T(8,128)S(1)}, f32[128,2560]{1,0:T(8,128)}, u32[]{:S(2)}, u32[]{:S(2)}) collective-permute-start(f32[128,2560]{1,0:T(8,128)S(1)} %fusion.11), channel_id=1, source_target_pairs={{0,4},{4,0},{8,12},{12,8},{16,20},{20,16},{24,28},{28,24},{1,5},{5... | collective-permute-start | bytes 3932168 | tf_op jit(solution)/shard_map/ppermute | solution.py:18
  48.7 25.0 %collective-permute-start.4 = (f32[2560]{0:T(1024)}, f32[2560]{0:T(1024)S(1)}, u32[]{:S(2)}, u32[]{:S(2)}) collective-permute-start(f32[2560]{0:T(1024)} %mul.381), channel_id=1, source_target_pairs={{0,8},{4,12},{8,0},{12,4},{16,24},{20,28},{24,16},{28,20},{1,9},{5... | collective-permute-start | bytes 30728 | tf_op jit(solution)/shard_map/ppermute | solution.py:18
  56.8 11.7 %copy-start.9 = (f32[256,256]{1,0:T(8,128)}, f32[256,256]{1,0:T(8,128)S(1)}, u32[]{:S(2)}) copy-start(f32[256,256]{1,0:T(8,128)S(1)} %fusion.157) | copy-start | bytes 786436
  59.1 29.6 %collective-permute-start.3 = (f32[128,2560]{1,0:T(8,128)S(1)}, f32[128,2560]{1,0:T(8,128)}, u32[]{:S(2)}, u32[]{:S(2)}) collective-permute-start(f32[128,2560]{1,0:T(8,128)S(1)} %add_select_fusion.1), channel_id=1, source_target_pairs={{0,8},{4,12},{8,0},{12,4},{16,24},{20,28},{24,16},{28,20},{1,9},{5... | collective-permute-start | bytes 3932168 | tf_op jit(solution)/shard_map/ppermute | solution.py:18
  60.0 4.2 %copy-start.12 = (bf16[256,512]{0,1:T(8,128)(2,1)S(1)}, bf16[256,512]{0,1:T(8,128)(2,1)}, u32[]{:S(2)}) copy-start(bf16[256,512]{0,1:T(8,128)(2,1)} %copy.35) | copy-start | bytes 786436
  73.5 20.4 %copy-start.8 = (f32[256,256]{1,0:T(8,128)S(1)}, f32[256,256]{1,0:T(8,128)}, u32[]{:S(2)}) copy-start(f32[256,256]{1,0:T(8,128)} %get-tuple-element.77) | copy-start | bytes 786436
  73.5 20.4 %copy-start.10 = (f32[256,256]{1,0:T(8,128)S(1)}, f32[256,256]{1,0:T(8,128)}, u32[]{:S(2)}) copy-start(f32[256,256]{1,0:T(8,128)} %copy-done.9) | copy-start | bytes 786436
  73.5 20.4 %copy-start.14 = (bf16[256,512]{0,1:T(8,128)(2,1)S(1)}, bf16[256,512]{0,1:T(8,128)(2,1)}, u32[]{:S(2)}) copy-start(bf16[256,512]{0,1:T(8,128)(2,1)} %copy.37) | copy-start | bytes 786436
  73.5 20.4 %copy-start.16 = (pred[256,256]{1,0:T(8,128)(4,1)S(1)}, pred[256,256]{1,0:T(8,128)(4,1)}, u32[]{:S(2)}) copy-start(pred[256,256]{1,0:T(8,128)(4,1)} %get-tuple-element.86) | copy-start | bytes 196612
  73.5 20.4 %copy-start.18 = (pred[256,256]{1,0:T(8,128)(4,1)S(1)}, pred[256,256]{1,0:T(8,128)(4,1)}, u32[]{:S(2)}) copy-start(pred[256,256]{1,0:T(8,128)(4,1)} %get-tuple-element.87) | copy-start | bytes 196612
  73.6 20.4 %copy-start.20 = (pred[256,256]{1,0:T(8,128)(4,1)S(1)}, pred[256,256]{1,0:T(8,128)(4,1)}, u32[]{:S(2)}) copy-start(pred[256,256]{1,0:T(8,128)(4,1)} %get-tuple-element.88) | copy-start | bytes 196612
  73.6 20.4 %copy-start.22 = (pred[256,256]{1,0:T(8,128)(4,1)S(1)}, pred[256,256]{1,0:T(8,128)(4,1)}, u32[]{:S(2)}) copy-start(pred[256,256]{1,0:T(8,128)(4,1)} %get-tuple-element.89) | copy-start | bytes 196612
  73.6 20.4 %copy-start.24 = (pred[256,256]{1,0:T(8,128)(4,1)S(1)}, pred[256,256]{1,0:T(8,128)(4,1)}, u32[]{:S(2)}) copy-start(pred[256,256]{1,0:T(8,128)(4,1)} %get-tuple-element.90) | copy-start | bytes 196612
  73.6 20.4 %copy-start.26 = (pred[256,256]{1,0:T(8,128)(4,1)S(1)}, pred[256,256]{1,0:T(8,128)(4,1)}, u32[]{:S(2)}) copy-start(pred[256,256]{1,0:T(8,128)(4,1)} %get-tuple-element.76) | copy-start | bytes 196612
  73.6 20.4 %copy-start.28 = (pred[256,256]{1,0:T(8,128)(4,1)S(1)}, pred[256,256]{1,0:T(8,128)(4,1)}, u32[]{:S(2)}) copy-start(pred[256,256]{1,0:T(8,128)(4,1)} %get-tuple-element.82) | copy-start | bytes 196612
  73.6 20.4 %copy-start.40 = (f32[8,256]{1,0:T(8,128)S(1)}, f32[8,256]{1,0:T(8,128)}, u32[]{:S(2)}) copy-start(f32[8,256]{1,0:T(8,128)} %get-tuple-element.68) | copy-start | bytes 24580
  73.6 20.4 %copy-start.44 = (f32[8,256]{1,0:T(8,128)S(1)}, f32[8,256]{1,0:T(8,128)}, u32[]{:S(2)}) copy-start(f32[8,256]{1,0:T(8,128)} %get-tuple-element.30) | copy-start | bytes 24580
  73.6 20.4 %copy-start.45 = (f32[8,256]{1,0:T(8,128)S(1)}, f32[8,256]{1,0:T(8,128)}, u32[]{:S(2)}) copy-start(f32[8,256]{1,0:T(8,128)} %get-tuple-element.31) | copy-start | bytes 24580
  73.6 20.4 %copy-start.46 = (f32[8,256]{1,0:T(8,128)S(1)}, f32[8,256]{1,0:T(8,128)}, u32[]{:S(2)}) copy-start(f32[8,256]{1,0:T(8,128)} %get-tuple-element.32) | copy-start | bytes 24580
  73.7 20.4 %copy-start.47 = (f32[8,256]{1,0:T(8,128)S(1)}, f32[8,256]{1,0:T(8,128)}, u32[]{:S(2)}) copy-start(f32[8,256]{1,0:T(8,128)} %get-tuple-element.33) | copy-start | bytes 24580
  73.7 20.4 %copy-start.48 = (f32[8,256]{1,0:T(8,128)S(1)}, f32[8,256]{1,0:T(8,128)}, u32[]{:S(2)}) copy-start(f32[8,256]{1,0:T(8,128)} %get-tuple-element.34) | copy-start | bytes 24580
  73.7 20.4 %copy-start.49 = (f32[8,256]{1,0:T(8,128)S(1)}, f32[8,256]{1,0:T(8,128)}, u32[]{:S(2)}) copy-start(f32[8,256]{1,0:T(8,128)} %get-tuple-element.35) | copy-start | bytes 24580
  73.7 20.4 %copy-start.50 = (f32[8,256]{1,0:T(8,128)S(1)}, f32[8,256]{1,0:T(8,128)}, u32[]{:S(2)}) copy-start(f32[8,256]{1,0:T(8,128)} %get-tuple-element.36) | copy-start | bytes 24580
  73.7 20.4 %copy-start.51 = (f32[8,256]{1,0:T(8,128)S(1)}, f32[8,256]{1,0:T(8,128)}, u32[]{:S(2)}) copy-start(f32[8,256]{1,0:T(8,128)} %get-tuple-element.37) | copy-start | bytes 24580
  73.7 20.4 %copy-start.52 = (f32[8,256]{1,0:T(8,128)S(1)}, f32[8,256]{1,0:T(8,128)}, u32[]{:S(2)}) copy-start(f32[8,256]{1,0:T(8,128)} %get-tuple-element.38) | copy-start | bytes 24580
  91.4 57.5 %collective-permute-start.5 = (f32[128,2560]{1,0:T(8,128)}, f32[128,2560]{1,0:T(8,128)S(1)}, u32[]{:S(2)}, u32[]{:S(2)}) collective-permute-start(f32[128,2560]{1,0:T(8,128)} %add_select_fusion), channel_id=1, source_target_pairs={{0,16},{4,20},{8,24},{12,28},{16,0},{20,4},{24,8},{28,12},{1,17},{... | collective-permute-start | bytes 3932168 | tf_op jit(solution)/shard_map/ppermute | solution.py:18
  94.1 5.0 %copy-start.39 = (f32[8,256]{1,0:T(8,128)S(1)}, f32[8,256]{1,0:T(8,128)}, u32[]{:S(2)}) copy-start(f32[8,256]{1,0:T(8,128)} %get-tuple-element.67) | copy-start | bytes 24580
  107.8 41.2 %copy-start.1 = (f32[256,2560]{1,0:T(8,128)S(1)}, f32[256,2560]{1,0:T(8,128)}, u32[]{:S(2)}) copy-start(f32[256,2560]{1,0:T(8,128)} %copy.43) | copy-start | bytes 7864324
  (49 other events, 170.4 us)
where the time goes:
time: 156 us; the launch traced here: 155 us
  waiting for transfers between devices  53.3 us (34%)
  local copies, waits for them, and re-layouts  42.9 us (28%)
  matrix products  27.5 us (18%)
  other arithmetic  17 us (11%)
  starting transfers between devices  11.8 us (8%)
  between operations  2.4 us (2%)
    ppermute x5, waiting for transfers between devices, partner(): return lax.ppermute(value, axis, pairs)  53.3 us
    dot_general x5, matrix products, per_device(): jnp.einsum('hts,shp->thp', mixing, values, preferred_element_type=jnp.flo...  21.7 us
    mul x6, local copies, waits for them, and re-layouts, per_device(): read.reshape(tok_rows, head_count, head_dim) * factor.T[:, :, None]  15 us
    slice x6, local copies, waits for them, and re-layouts, per_device(): xs[:, block_start * head_dim:(block_start + per_block) * head_dim]  7.96 us
    ppermute x5, starting transfers between devices, partner(): return lax.ppermute(value, axis, pairs)  7 us
    dot_general x3, matrix products, per_device(): jnp.dot(queries, level_state.astype(jnp.bfloat16), preferred_element_type...  5.16 us
    mul x2, local copies, waits for them, and re-layouts, per_device(): xs.astype(jnp.float32).reshape(tok_rows, head_count, head_dim)  5.01 us
    select_n x2, other arithmetic, per_device(): jnp.where(on_top, far_state * block_total[None, :] + running, running * f...  4.85 us
  transfers between devices with their start and end apart: 6, of which 2 were waited for; matrix products, arithmetic and copies ran while one was open for 50% of the time, Pallas kernels for 0%

commit v1 on v0

v1 whole, which is shorter than its diff:
```python
import functools

import jax
import jax.numpy as jnp
from jax import lax
from jax.experimental import pallas as pl
from jax.experimental.pallas import tpu as pltpu
from jax.sharding import PartitionSpec as P

eps_norm = 1e-05
bf16 = jnp.bfloat16
f32 = jnp.float32
HALO = 16
PLACES = 4
LANES = 128
EXACT = lax.Precision.HIGHEST


def iota(shape, dim):
    return lax.broadcasted_iota(jnp.int32, shape, dim)


def dot(a, b, contract, precision=None):
    return lax.dot_general(
        a, b, (contract, ((), ())), precision=precision, preferred_element_type=f32
    )


def silu(v):
    return v * (0.5 * jnp.tanh(0.5 * v) + 0.5)


def segment_bounds(info, recordings):
    bounds, total = [], 0
    for index in range(recordings - 1):
        total = total + info[index]
        bounds.append(total)
    return bounds


def segment_of(pos, bounds):
    found = jnp.where(pos >= 0, 0, -1)
    for bound in bounds:
        found = found + jnp.where(pos >= bound, 1, 0)
    return found


def same_segment(pos, other, bounds):
    return (segment_of(pos, bounds) == segment_of(other, bounds)).astype(f32)


def two_parts(value):
    high = value.astype(bf16).astype(f32)
    return high, value - high


def spread(rows, first_head, columns, head_dim, repeats):
    row = lax.rem(iota((rows * repeats, columns), 0), rows)
    head = first_head + iota((rows * repeats, columns), 1) // head_dim
    return (row == head).astype(bf16)


def conv_taps(shifts, weight_ref, bias_ref, lo, hi):
    total = bias_ref[0:1, lo:hi]
    for tap, piece in enumerate(shifts):
        total = total + weight_ref[tap : tap + 1, lo:hi] * piece
    return silu(total)


def features_kernel(
    dims, info, x_ref, kq_in_ref, w_ref, b_ref, wkq_ref, bkq_ref, decay_ref,
    xs_ref, kq_ref, part_ref, cum_ref, cumt_ref, ewt_ref, same_ref, keys_ref,
):
    tok, heads, head_dim, taps, recordings, block = dims
    state = keys_ref.shape[0]
    step = pl.program_id(0)

    def features(rows_ref, weight_ref, bias_ref):
        width = rows_ref.shape[1]
        halves = []
        for lo in range(0, width, LANES):
            x = rows_ref[:, lo : lo + LANES].astype(f32)
            shifts = [x] + [
                pltpu.roll(x, tap, 0) * same_ref[tap - 1] for tap in range(1, taps)
            ]
            halves.append(conv_taps(shifts, weight_ref, bias_ref, lo, lo + LANES))
        return jnp.concatenate(halves, axis=1)

    @pl.when(step == 0)
    def _():
        bounds = segment_bounds(info, recordings)
        first = info[recordings] * tok
        pos = first + iota((tok, LANES), 0)
        for tap in range(1, taps):
            same_ref[tap - 1] = same_segment(pos, pos - tap, bounds)
        decay = jnp.concatenate(
            [decay_ref[...], jnp.zeros((LANES - heads, tok), f32)], axis=0
        )
        upper = (iota((tok, tok), 0) <= iota((tok, tok), 1)).astype(f32)
        lower = (iota((tok, tok), 0) >= iota((tok, tok), 1)).astype(f32)
        cum_ref[...] = dot(decay_ref[...], upper, ((1,), (0,)), EXACT)
        cumt = dot(lower, decay, ((1,), (1,)), EXACT)
        cumt_ref[...] = cumt
        end = cumt[tok - 1 : tok, :]
        ewt_ref[...] = jnp.exp(end - cumt) * same_segment(
            pos, jnp.zeros_like(pos) + (first + tok - 1), bounds
        )
        kq = features(kq_in_ref, wkq_ref, bkq_ref)
        kq_ref[...] = kq.astype(bf16)
        keys = jnp.transpose(kq[:, :state])
        keys_ref[...] = jnp.where(iota((state, tok), 1) >= HALO, keys, 0.0).astype(bf16)

    xs = features(x_ref, w_ref, b_ref).astype(bf16)
    xs_ref[...] = xs
    high, low = two_parts(ewt_ref[...])
    weight = dot(
        jnp.concatenate([high, low], axis=1).astype(bf16),
        spread(LANES, step * (block // head_dim), block, head_dim, 2),
        ((1,), (0,)),
    )
    scaled = (xs.astype(f32) * weight).astype(bf16)
    part_ref[...] = dot(keys_ref[...], scaled, ((1,), (0,)))


def join_kernel(
    dims, info, halo_ref, head_ref, w_ref, b_ref, ewt_ref, cumt_ref, part_ref,
    px_ref, pkq_ref, own_ref, one_ref, two_ref, three_ref, rest_ref, scaled_ref,
):
    tok, heads, head_dim, taps, recordings, width, state = dims
    bounds = segment_bounds(info, recordings)
    group = info[recordings]
    first = group * tok
    pos = first + iota((HALO, LANES), 0)
    same = [same_segment(pos, pos - tap, bounds) for tap in range(1, taps)]
    high, low = two_parts(ewt_ref[...])
    split = jnp.concatenate([high, low], axis=1).astype(bf16)

    def features(lo):
        hi = lo + LANES
        both = jnp.concatenate(
            [halo_ref[:, lo:hi].astype(f32), head_ref[:, lo:hi].astype(f32)], axis=0
        )
        shifts = [both[HALO:]] + [
            pltpu.roll(both, tap, 0)[HALO:] * same[tap - 1] for tap in range(1, taps)
        ]
        return conv_taps(shifts, w_ref, b_ref, lo, hi)

    keys = None
    for lo in range(width, width + 2 * state, LANES):
        part = features(lo).astype(bf16)
        pkq_ref[:, lo - width : lo - width + LANES] = part
        if lo == width:
            keys = part
    block = 4 * LANES
    for lo in range(0, width, block):
        xs = jnp.concatenate(
            [features(lo + at) for at in range(0, block, LANES)], axis=1
        ).astype(bf16)
        px_ref[:, lo : lo + block] = xs
        weight = dot(
            split, spread(LANES, lo // head_dim, block, head_dim, 2), ((1,), (0,))
        )
        scaled_ref[:, lo : lo + block] = (xs.astype(f32) * weight).astype(bf16)

    end = cumt_ref[HALO - 1 : HALO, :]
    alive = same_segment(first + tok - 1 + 0 * pos[:1], first - 1 + 0 * pos[:1], bounds)
    through = jnp.exp(end) * alive
    high, rest = two_parts(through)
    mid, low = two_parts(rest)
    row = iota((HALO, LANES), 0)
    tail = jnp.where(row == 0, high, jnp.where(row == 1, mid, jnp.where(row == 2, low, 0.0)))
    place = lax.rem(group, PLACES)
    cols = width // PLACES
    for mask, out_ref in enumerate((own_ref, one_ref, two_ref, three_ref)):
        where = pl.multiple_of(jnp.bitwise_xor(place, mask) * cols, LANES)
        value = part_ref[:, pl.ds(where, cols)] + dot(
            keys, scaled_ref[:, pl.ds(where, cols)], ((0,), (0,))
        )
        value = value.astype(bf16)
        out_ref[:state, :] = value
        out_ref[state:, :LANES] = tail.astype(bf16)
        out_ref[state:, LANES:] = jnp.zeros((HALO, cols - LANES), bf16)
        if mask != 1:
            rest_ref[max(mask - 1, 0)] = value


def combine_kernel(
    dims, info, own_ref, one_ref, two_ref, three_ref, quad_ref, pair_ref, scale_ref
):
    state, head_dim, recordings = dims
    cols = quad_ref.shape[1]
    place = lax.rem(info[recordings], PLACES)
    refs = (own_ref, one_ref, two_ref, three_ref)
    got = []
    for ref in refs:
        tail = ref[state:, :LANES].astype(f32)
        got.append(tail[0:1] + tail[1:2] + tail[2:3])
    through = []
    for at in range(PLACES):
        total = jnp.zeros((1, LANES), f32)
        for mask in range(PLACES):
            total = total + jnp.where(jnp.bitwise_xor(place, mask) == at, got[mask], 0.0)
        through.append(total)
    ones = jnp.ones((1, LANES), f32)
    rows = []
    for mask in range(PLACES):
        at = jnp.bitwise_xor(place, mask)
        product = ones
        for later in range(1, PLACES):
            product = product * jnp.where(later > at, through[later], ones)
        rows.append(product)
    for mask in range(PLACES):
        at = jnp.bitwise_xor(place, mask)
        rows.append(jnp.where(at == 0, through[1], jnp.where(at == 1, ones, 0.0 * ones)))
    before_quad = ones
    for earlier in range(PLACES - 1):
        before_quad = before_quad * jnp.where(earlier < place, through[earlier], ones)
    everything = through[0] * through[1] * through[2] * through[3]
    row = iota((8, LANES), 0)
    scale = jnp.where(row == 1, jnp.where(place == 3, through[2], ones), ones)
    scale = jnp.where(row == 2, before_quad, scale)
    scale_ref[...] = jnp.where(row == 3, everything, scale)
    weights = jnp.concatenate(rows, axis=0)
    high, low = two_parts(weights)
    weights = dot(
        jnp.concatenate([high, low], axis=1).astype(bf16),
        spread(LANES, place * (cols // head_dim), cols, head_dim, 2),
        ((1,), (0,)),
    )
    quad = jnp.zeros((state, cols), f32)
    pair = jnp.zeros((state, cols), f32)
    for mask, ref in enumerate(refs):
        value = ref[:state, :].astype(f32)
        quad = quad + value * weights[mask : mask + 1]
        pair = pair + value * weights[PLACES + mask : PLACES + mask + 1]
    quad_ref[...] = quad.astype(bf16)
    pair_ref[...] = pair.astype(bf16)


def with_head(patch_ref, body_ref):
    return jnp.concatenate([patch_ref[...], body_ref[HALO:, :]], axis=0)


def local_kernel(
    dims, info, xs_ref, px_ref, kq_ref, pkq_ref, cum_ref, level_ref, skip_ref,
    out_ref, scores_ref, mixing_ref,
):
    tok, head_dim, recordings, state, low_bits = dims
    per_step = cum_ref.shape[0]
    rows = 32
    row_bits = rows.bit_length() - 1

    @pl.when(pl.program_id(0) == 0)
    def _():
        bounds = segment_bounds(info, recordings)
        first = info[recordings] * tok
        kq = with_head(pkq_ref, kq_ref)
        s_pos = iota((tok, tok), 0)
        t_pos = iota((tok, tok), 1)
        valid = same_segment(first + s_pos, first + t_pos, bounds) * (s_pos <= t_pos)
        scores_ref[...] = dot(kq[:, :state], kq[:, state:], ((1,), (1,))) * valid

    xs = with_head(px_ref, xs_ref)
    cum = cum_ref[...]
    cumt = jnp.transpose(cum)
    diff = jnp.bitwise_xor(iota((rows, tok), 0), lax.rem(iota((rows, tok), 1), rows))
    near = jnp.zeros((rows, tok), jnp.int32)
    for bit in range(row_bits):
        near = near + (diff >= 2**bit).astype(jnp.int32)
    token = iota((1, tok), 1) // rows
    pieces = []
    for head in range(per_step):
        levels = level_ref[head]
        inner = jnp.broadcast_to(levels[0:1], (rows, tok))
        for level in range(1, row_bits + 1):
            inner = jnp.where(near == level, levels[level : level + 1], inner)
        for s in range(0, tok, rows):
            at = s // rows
            start = s // LANES * LANES
            outer = jnp.zeros((1, tok), f32)
            apart = jnp.bitwise_xor(token, at)
            for level in range(row_bits + 1, low_bits + 1):
                outer = jnp.where(
                    apart >= 2 ** (level - row_bits - 1), levels[level : level + 1], outer
                )
            picked = jnp.where(token == at, inner, outer)[:, start:]
            gap = cum[head : head + 1, start:] - cumt[s : s + rows, head : head + 1]
            value = jnp.exp(jnp.minimum(gap, 0.0)) * picked
            mixing_ref[s : s + rows, start:] = (
                value * scores_ref[s : s + rows, start:]
            ).astype(bf16)
            if start:
                mixing_ref[s : s + rows, :start] = jnp.zeros((rows, start), bf16)
        x_head = xs[:, head * head_dim : (head + 1) * head_dim].astype(f32)
        xt = jnp.transpose(x_head).astype(bf16)
        pieces.append(dot(xt, mixing_ref[...], ((1,), (0,))))
    skip = skip_ref[...]
    for at in range(0, per_step, 2):
        lo = at * head_dim
        both = jnp.transpose(jnp.concatenate(pieces[at : at + 2], axis=0))
        hi = lo + 2 * head_dim
        out_ref[:, lo:hi] = both + skip[:, lo:hi] * xs[:, lo:hi].astype(f32)


def spread_rows(coef, cols, head_dim, first_head):
    high, low = two_parts(coef)
    heads = coef.shape[0]
    return dot(
        jnp.concatenate([high, low], axis=0).astype(bf16),
        spread(heads, first_head, cols, head_dim, 2),
        ((0,), (0,)),
    )


def far_kernel(
    dims, mask, info, sum_ref, kq_ref, pkq_ref, coef_ref, low_ref, pair_ref, gate_ref,
    out_ref, next_ref,
):
    head_dim, recordings, state = dims
    cols = sum_ref.shape[1]
    place = lax.rem(info[recordings], PLACES)
    first = jnp.bitwise_xor(place, mask) * (cols // head_dim)
    queries = with_head(pkq_ref, kq_ref)[:, state:]
    total = sum_ref[...]
    for bit, ref in enumerate((low_ref, pair_ref)):
        read = dot(queries, ref[:state, :], ((1,), (0,)))
        total = total + read * spread_rows(coef_ref[bit], cols, head_dim, first)
    gate = silu(gate_ref[...].astype(f32))
    out_ref[...] = total * gate
    next_ref[...] = spread_rows(coef_ref[2], cols, head_dim, first) * gate


def final_kernel(dims, count, info, *refs):
    recordings, state = dims
    sums = refs[:PLACES]
    factors = refs[PLACES : 2 * PLACES]
    queries_ref = refs[2 * PLACES]
    states = refs[2 * PLACES + 1 : 3 * PLACES + 1]
    gain_ref, out_ref = refs[3 * PLACES + 1 :]
    place = lax.rem(info[recordings], PLACES)
    cols = sums[0].shape[1]
    queries = queries_ref[...]
    gated, squares = [], 0.0
    for mask in range(PLACES):
        read = dot(queries, states[mask][...], ((1,), (0,)))
        value = sums[mask][...] + read * factors[mask][...]
        gated.append(value)
        squares = squares + jnp.sum(value * value, axis=1, keepdims=True)
    scale = lax.rsqrt(squares / count + eps_norm)
    for mask in range(PLACES):
        where = pl.multiple_of(jnp.bitwise_xor(place, mask) * cols, LANES)
        out_ref[:, pl.ds(where, cols)] = (
            gated[mask] * scale * gain_ref[:, pl.ds(where, cols)]
        ).astype(bf16)


def whole(shape):
    zeros = (0,) * len(shape)
    return pl.BlockSpec(shape, lambda *_: zeros)


def call(kernel, info, operands, in_specs, outs, out_specs, grid, scratch=(), flops=0, mb=64):
    moved = sum(a.size * a.dtype.itemsize for a in operands)
    moved += sum(o.size * o.dtype.itemsize for o in outs)
    return pl.pallas_call(
        kernel,
        grid_spec=pltpu.PrefetchScalarGridSpec(
            num_scalar_prefetch=1,
            grid=grid,
            in_specs=in_specs,
            out_specs=out_specs,
            scratch_shapes=list(scratch),
        ),
        out_shape=outs,
        compiler_params=pltpu.CompilerParams(vmem_limit_bytes=mb * 2**20 * 3 // 4),
        cost_estimate=pl.CostEstimate(
            flops=flops, bytes_accessed=moved, transcendentals=0
        ),
    )(info, *operands)


def shape(dims, dtype):
    return jax.ShapeDtypeStruct(dims, dtype)


def per_device(
    mixed_input,
    conv_weight,
    conv_bias,
    gate_input,
    log_decay,
    level_weights,
    skip_gain,
    norm_gain,
    seg_lengths,
):
    tok, channels = mixed_input.shape
    width = gate_input.shape[1]
    heads = log_decay.shape[0]
    head_dim = width // heads
    state = (channels - width) // 2
    taps = conv_weight.shape[0]
    recordings = seg_lengths.shape[0]
    low_bits = tok.bit_length() - 1
    groups = lax.axis_size("group")
    high_bits = groups.bit_length() - 1
    group = lax.axis_index("group")
    place = group % PLACES
    cols = width // PLACES
    info = jnp.concatenate([seg_lengths, group[None].astype(jnp.int32)])

    def send(value, pairs):
        return lax.ppermute(value, "group", pairs)

    def quad_send(value, mask, wanted=lambda target: True):
        pairs = [(g, g ^ mask) for g in range(groups) if wanted(g ^ mask)]
        return send(value, pairs)

    halo = send(mixed_input[tok - HALO :], [(g, g + 1) for g in range(groups - 1)])

    block = 2 * state
    bias = conv_bias[None, :]
    xs, kq, part, cum, cumt, ewt = call(
        functools.partial(
            features_kernel, (tok, heads, head_dim, taps, recordings, block)
        ),
        info,
        (mixed_input, mixed_input, conv_weight, bias, conv_weight, bias, log_decay),
        [
            pl.BlockSpec((tok, block), lambda i, *_: (0, i)),
            pl.BlockSpec((tok, block), lambda i, *_: (0, width // block)),
            pl.BlockSpec((taps, block), lambda i, *_: (0, i)),
            pl.BlockSpec((1, block), lambda i, *_: (0, i)),
            pl.BlockSpec((taps, block), lambda i, *_: (0, width // block)),
            pl.BlockSpec((1, block), lambda i, *_: (0, width // block)),
            whole(log_decay.shape),
        ],
        [
            shape((tok, width), bf16),
            shape((tok, block), bf16),
            shape((state, width), f32),
            shape((heads, tok), f32),
            shape((tok, LANES), f32),
            shape((tok, LANES), f32),
        ],
        [
            pl.BlockSpec((tok, block), lambda i, *_: (0, i)),
            whole((tok, block)),
            pl.BlockSpec((state, block), lambda i, *_: (0, i)),
            whole((heads, tok)),
            whole((tok, LANES)),
            whole((tok, LANES)),
        ],
        (width // block,),
        [pltpu.VMEM((taps - 1, tok, LANES), f32), pltpu.VMEM((state, tok), bf16)],
        flops=2 * tok * width * state,
    )

    payload = shape((state + HALO, cols), bf16)
    px, pkq, own, one, two, three, rest = call(
        functools.partial(
            join_kernel, (tok, heads, head_dim, taps, recordings, width, state)
        ),
        info,
        (halo, mixed_input, conv_weight, bias, ewt, cumt, part),
        [
            whole((HALO, channels)),
            whole((HALO, channels)),
            whole(conv_weight.shape),
            whole(bias.shape),
            whole((HALO, LANES)),
            pl.BlockSpec((HALO, LANES), lambda i, *_: (tok // HALO - 1, 0)),
            whole(part.shape),
        ],
        [
            shape((HALO, width), bf16),
            shape((HALO, block), bf16),
            payload,
            payload,
            payload,
            payload,
            shape((PLACES - 1, state, cols), bf16),
        ],
        [
            whole((HALO, width)),
            whole((HALO, block)),
            whole(payload.shape),
            whole(payload.shape),
            whole(payload.shape),
            whole(payload.shape),
            whole((PLACES - 1, state, cols)),
        ],
        (1,),
        [pltpu.VMEM((HALO, width), bf16)],
        flops=2 * HALO * width * state,
    )

    got_one = quad_send(one, 1)
    got_two = quad_send(two, 2)
    got_three = quad_send(three, 3)
    quad, pair, scale = call(
        functools.partial(combine_kernel, (state, head_dim, recordings)),
        info,
        (own, got_one, got_two, got_three),
        [whole(payload.shape)] * PLACES,
        [shape((state, cols), bf16), shape((state, cols), bf16), shape((8, LANES), f32)],
        [whole((state, cols)), whole((state, cols)), whole((8, LANES))],
        (1,),
        flops=4 * state * cols,
    )

    befores = [scale[0, :heads], scale[1, :heads], scale[2, :heads]]
    crossed = []
    running, total = quad, scale[3, :heads]
    for bit in range(2, high_bits):
        mask = 2**bit
        last = bit + 1 == high_bits
        far = quad_send(running, mask, lambda target: not last or target & mask)
        crossed.append(far)
        if not last:
            on_top = group // mask % 2 == 1
            far_total = quad_send(total, mask)

            def columns(value):
                mine = lax.dynamic_slice(value, (place * (cols // head_dim),), (cols // head_dim,))
                return jnp.repeat(mine, head_dim)[None, :]

            running = jnp.where(
                on_top,
                far.astype(f32) * columns(total) + running.astype(f32),
                running.astype(f32) * columns(far_total) + far.astype(f32),
            ).astype(bf16)
            befores.append(jnp.where(on_top, far_total * befores[-1], befores[-1]))
            total = total * far_total

    rests = quad_send(rest, 1, lambda target: target & 1)
    lows = [got_one, rests[0], rests[2], rests[1]]
    pairs = [pair] + [
        quad_send(pair, mask, lambda target: target & 2) for mask in range(1, PLACES)
    ]

    def all_quarters(value, bit):
        return [value] + [
            quad_send(value, mask, lambda target: target & 2**bit)
            for mask in range(1, PLACES)
        ]

    per_step = 8
    skip_cols = jnp.repeat(skip_gain, head_dim)[None, :]
    sums = call(
        functools.partial(
            local_kernel, (tok, head_dim, recordings, state, low_bits)
        ),
        info,
        (xs, px, kq, pkq, cum, level_weights, skip_cols),
        [
            pl.BlockSpec((tok, per_step * head_dim), lambda i, *_: (0, i)),
            pl.BlockSpec((HALO, per_step * head_dim), lambda i, *_: (0, i)),
            whole(kq.shape),
            whole(pkq.shape),
            pl.BlockSpec((per_step, tok), lambda i, *_: (i, 0)),
            pl.BlockSpec((per_step,) + level_weights.shape[1:], lambda i, *_: (i, 0, 0)),
            pl.BlockSpec((1, per_step * head_dim), lambda i, *_: (0, i)),
        ],
        [shape((tok, width), f32)],
        [pl.BlockSpec((tok, per_step * head_dim), lambda i, *_: (0, i))],
        (heads // per_step,),
        [pltpu.VMEM((tok, tok), f32), pltpu.VMEM((tok, tok), bf16)],
        flops=2 * heads * tok * tok * head_dim,
    )[0]

    positions = group * tok + jnp.arange(tok, dtype=jnp.int32)
    bounds = segment_bounds(seg_lengths, recordings)
    alive = segment_of(positions, bounds) == segment_of(positions[:1] - 1, bounds)
    entry = jnp.exp(cum) * alive.astype(f32)[None, :]
    coefs = jnp.stack(
        [
            level_weights[:, low_bits + 1 + bit, :]
            * entry
            * jnp.where(group // 2**bit % 2 == 1, befores[bit], 0.0)[:, None]
            for bit in range(high_bits)
        ]
    )

    halves = []
    for mask in range(PLACES):
        halves.append(
            list(call(
                functools.partial(far_kernel, (head_dim, recordings, state), mask),
                info,
                (sums, kq, pkq, coefs, lows[mask], pairs[mask], gate_input),
                [
                    pl.BlockSpec((tok, cols), functools.partial(quarter, recordings, mask)),
                    whole(kq.shape),
                    whole(pkq.shape),
                    whole(coefs.shape),
                    whole(lows[mask].shape),
                    whole(pairs[mask].shape),
                    pl.BlockSpec((tok, cols), functools.partial(quarter, recordings, mask)),
                ],
                [shape((tok, cols), f32), shape((tok, cols), f32)],
                [whole((tok, cols)), whole((tok, cols))],
                (1,),
                flops=4 * tok * cols * state,
            ))
        )
    queries = jnp.concatenate([pkq[:, state:], kq[HALO:, state:]], axis=0)
    tops = [all_quarters(value, bit + 2) for bit, value in enumerate(crossed)]
    for bit in range(3, high_bits):
        for mask in range(PLACES):
            first = (place ^ mask) * (cols // head_dim)
            coef = lax.dynamic_slice_in_dim(coefs[bit], first, cols // head_dim, axis=0)
            gate = lax.dynamic_slice_in_dim(gate_input, (place ^ mask) * cols, cols, axis=1)
            read = jnp.dot(queries, tops[bit - 2][mask], preferred_element_type=f32)
            read = read * jnp.repeat(coef, head_dim, axis=0).T
            halves[mask][0] = halves[mask][0] + read * jax.nn.silu(gate.astype(f32))

    rows = 64
    return call(
        functools.partial(final_kernel, (recordings, state), float(width)),
        info,
        [h[0] for h in halves] + [h[1] for h in halves] + [queries] + tops[0] + [norm_gain[None, :]],
        [pl.BlockSpec((rows, cols), lambda i, *_: (i, 0))] * (2 * PLACES)
        + [pl.BlockSpec((rows, state), lambda i, *_: (i, 0))]
        + [whole((state, cols))] * PLACES
        + [whole((1, width))],
        [shape((tok, width), bf16)],
        [pl.BlockSpec((rows, width), lambda i, *_: (i, 0))],
        (tok // rows,),
        flops=2 * tok * width * state,
    )[0]


def quarter(recordings, mask, i, info):
    return 0, jnp.bitwise_xor(lax.rem(info[recordings], PLACES), mask)


def solution(mesh):
    in_specs = (
        P(("batch", "group"), None),
        P(),
        P(),
        P(("batch", "group"), None),
        P(None, ("batch", "group")),
        P(None, None, ("batch", "group")),
        P(),
        P(),
        P("batch"),
    )
    out_specs = P(("batch", "group"), None)
    return jax.shard_map(
        per_device, mesh=mesh, in_specs=in_specs, out_specs=out_specs, check_vma=False
    )
```

time: 156 us -> 72.8 us (0.47)
  the two profiles are of different devices: /device:TPU:0 before, /device:TPU:24 now
where the time goes in v1:
time: 72.8 us; the launch traced here: 72.1 us
  starting transfers between devices  26.6 us (37%)
  Pallas kernels  24.1 us (33%)
  local copies, waits for them, and re-layouts  8.8 us (12%)
  waiting for transfers between devices  7.19 us (10%)
  between operations  3.07 us (4%)
  other arithmetic  2.35 us (3%)
    ppermute x12, starting transfers between devices, send(): return lax.ppermute(value, 'group', pairs)  26.6 us
    pallas_call x9, Pallas kernels, call(): pl.pallas_call(kernel, grid_spec=pltpu.PrefetchScalarGridSpec(num_scalar_...  24.1 us
    ppermute x12, waiting for transfers between devices, send(): return lax.ppermute(value, 'group', pairs)  7.19 us
    unnamed x15, local copies, waits for them, and re-layouts  5.14 us
  transfers between devices with their start and end apart: 12, of which 2 were waited for; matrix products, arithmetic and copies ran while one was open for 9% of the time, Pallas kernels for 26%

profile of v1, /device:TPU:24, one launch (start us, length us, event | category | flops | bytes accessed | tf_op | source)
XLA Modules:
  0.0 72.1 jit_solution(16693520290509088459)
XLA Ops:
  0.0 0.9 %slice.45 = bf16[16,2816]{1,0:T(8,128)(2,1)S(1)} slice(bf16[256,2816]{1,0:T(8,128)(2,1)} %head_ref.1), slice={[240:256], [0:2816]} | slice | bytes 180224 | tf_op jit(solution)/shard_map/slice | solution.py:419
  0.9 3.4 %collective-permute-start = (bf16[16,2816]{1,0:T(8,128)(2,1)S(1)}, bf16[16,2816]{1,0:T(8,128)(2,1)S(1)}, u32[]{:S(2)}, u32[]{:S(2)}) collective-permute-start(bf16[16,2816]{1,0:T(8,128)(2,1)S(1)} %slice.45), channel_id=1, source_target_pairs={{0,4},{4,8},{8,12},{12,16},{16,20},{20,24},{24,28},{1,5},{5,9},{9,... | collective-permute-start | bytes 270344 | tf_op jit(solution)/shard_map/ppermute | solution.py:413
  4.3 0.7 broadcast_in_dim.43.b_ref.bkq_ref
  6.2 1.3 %fusion.11 = (s32[1]{0:T(128)}, s32[1]{0:T(128)}) fusion(s32[3]{0:T(128)} %param.17), kind=kLoop, calls=%fused_computation.29 | loop fusion | bytes 16 | tf_op jit(solution)/shard_map/slice | solution.py:36
  9.5 0.7 %pad_add_fusion.info = s32[4]{0:T(128)S(1)} fusion(s32[1]{0:T(128)} %bitcast, s32[3]{0:T(128)} %param.17), kind=kLoop, calls=%fused_computation.28 | loop fusion | flops 4 | bytes 32 | tf_op jit(solution)/shard_map/concatenate | solution.py:410
  10.3 1.4 %copy-done.1 = bf16[256,2816]{1,0:T(8,128)(2,1)S(1)} copy-done((bf16[256,2816]{1,0:T(8,128)(2,1)S(1)}, bf16[256,2816]{1,0:T(8,128)(2,1)}, u32[]{:S(2)}) %copy-start.1) | copy-done | bytes 1441816
  11.6 0.8 %copy-done.2 = f32[4,2816]{1,0:T(4,128)S(1)} copy-done((f32[4,2816]{1,0:T(4,128)S(1)}, f32[4,2816]{1,0:T(4,128)}, u32[]{:S(2)}) %copy-start.2) | copy-done | bytes 45080
  12.4 0.8 %copy-done.3 = f32[40,256]{1,0:T(8,128)S(1)} copy-done((f32[40,256]{1,0:T(8,128)S(1)}, f32[40,256]{1,0:T(8,128)}, u32[]{:S(2)}) %copy-start.3) | copy-done | bytes 40984
  13.2 6.3 %shard_map.91 = (bf16[256,2560]{1,0:T(8,128)(2,1)S(1)}, bf16[256,256]{1,0:T(8,128)(2,1)S(1)}, f32[128,2560]{1,0:T(8,128)S(1)}, f32[40,256]{1,0:T(8,128)S(1)}, f3...) custom-call(s32[4]{0:T(128)S(1)} %pad_add_fusion.info, bf16[256,2816]{1,0:T(8,128)(2,1)S(1)} %copy-done.1, ...), custom_call_target="tpu_custom_call" | custom-call | flops 167772160 | bytes 6092800 | tf_op jit(solution)/shard_map/pallas_call | solution.py:365
  19.5 1.8 %shard_map.92 = (bf16[16,2560]{1,0:T(8,128)(2,1)S(1)}, bf16[16,256]{1,0:T(8,128)(2,1)S(1)}, bf16[144,640]{1,0:T(8,128)(2,1)S(1)}, bf16[144,640]{1,0:T(8,128)(2,1...) custom-call(s32[4]{0:T(128)S(1)} %pad_add_fusion.info, ...), custom_call_target="tpu_custom_call" | custom-call | flops 10485760 | bytes 4480000 | tf_op jit(solution)/shard_map/pallas_call | solution.py:365
  21.4 0.8 %copy-done.4 = bf16[3,128,640]{2,1,0:T(8,128)(2,1)} copy-done((bf16[3,128,640]{2,1,0:T(8,128)(2,1)}, bf16[3,128,640]{2,1,0:T(8,128)(2,1)S(1)}, u32[]{:S(2)}) %copy-start.4) | copy-done | bytes 491544
  22.1 2.0 %collective-permute-start.2 = (bf16[144,640]{1,0:T(8,128)(2,1)}, bf16[144,640]{1,0:T(8,128)(2,1)S(1)}, u32[]{:S(2)}, u32[]{:S(2)}) collective-permute-start(bf16[144,640]{1,0:T(8,128)(2,1)} %get-tuple-element.39), channel_id=1, source_target_pairs={{0,8},{4,12},{8,0},{12,4},{16,24},{20,28},{24,16},{28,20},{1,9},{5... | collective-permute-start | bytes 552968 | tf_op jit(solution)/shard_map/ppermute | solution.py:413
  24.1 1.5 %collective-permute-start.3 = (bf16[144,640]{1,0:T(8,128)(2,1)S(1)}, bf16[144,640]{1,0:T(8,128)(2,1)S(1)}, u32[]{:S(2)}, u32[]{:S(2)}) collective-permute-start(bf16[144,640]{1,0:T(8,128)(2,1)S(1)} %get-tuple-element.40), channel_id=1, source_target_pairs={{0,12},{4,8},{8,4},{12,0},{16,28},{20,24},{24,20},{28,16},{1,13},{... | collective-permute-start | bytes 552968 | tf_op jit(solution)/shard_map/ppermute | solution.py:413
  26.4 1.4 %copy.10.level_ref = f32[40,20,256]{2,1,0:T(8,128)S(1)} copy(f32[40,20,256]{2,0,1:T(8,128)} %param.14) | data formatting | bytes 1638400 | tf_op args[5]
  28.0 1.9 %collective-permute-start.4 = (bf16[3,128,640]{2,1,0:T(8,128)(2,1)}, bf16[3,128,640]{2,1,0:T(8,128)(2,1)S(1)}, u32[]{:S(2)}, u32[]{:S(2)}) collective-permute-start(bf16[3,128,640]{2,1,0:T(8,128)(2,1)} %copy-done.4), channel_id=1, source_target_pairs={{0,4},{8,12},{16,20},{24,28},{1,5},{9,13},{17,21},{25,29},{2,6},{1... | collective-permute-start | bytes 1474568 | tf_op jit(solution)/shard_map/ppermute | solution.py:413
  30.0 6.9 %shard_map.93.sum_ref = f32[256,2560]{1,0:T(8,128)S(1)} custom-call(s32[4]{0:T(128)S(1)} %pad_add_fusion.info, bf16[256,2560]{1,0:T(8,128)(2,1)S(1)} %get-tuple-element.29.xs_ref, bf16[16,2560]{1,0:T(8,128)(2,1)S(1)} %get-tuple-element.33.px_ref, bf16[256,256]{1,0:T(8,128)(2,1)S(1)} %get-tuple-element.34.kq_ref, ...), custom_call_target="tpu_custom_call" | custom-call | flops 335544320 | bytes 5023744 | tf_op jit(solution)/shard_map/pallas_call | solution.py:365
  36.9 1.0 %shard_map.94 = (bf16[128,640]{1,0:T(8,128)(2,1)S(1)}, bf16[128,640]{1,0:T(8,128)(2,1)S(1)}, f32[8,128]{1,0:T(8,128)S(1)}) custom-call(s32[4]{0:T(128)S(1)} %pad_add_fusion.info, bf16[144,640]{1,0:T(8,128)(2,1)S(1)} %get-tuple-element.37.own_ref, bf16[144,640]{1,0:T(8,128)(2,1)S(1)} %collective-permute-done.1.one_ref.low_ref, ...), custom_call_target="tpu_custom_call" | custom-call | flops 327680 | bytes 1069056 | tf_op jit(solution)/shard_map/pallas_call | solution.py:365
  37.9 1.9 %collective-permute-start.5 = (bf16[128,640]{1,0:T(8,128)(2,1)S(1)}, bf16[128,640]{1,0:T(8,128)(2,1)S(1)}, u32[]{:S(2)}, u32[]{:S(2)}) collective-permute-start(bf16[128,640]{1,0:T(8,128)(2,1)S(1)} %get-tuple-element.42.pair_ref), channel_id=1, source_target_pairs={{8,12},{12,8},{24,28},{28,24},{9,13},{13,9},{25,29},{29,25},{10,14... | collective-permute-start | bytes 491528 | tf_op jit(solution)/shard_map/ppermute | solution.py:413
  39.9 1.3 %collective-permute-start.6 = (bf16[128,640]{1,0:T(8,128)(2,1)S(1)}, bf16[128,640]{1,0:T(8,128)(2,1)S(1)}, u32[]{:S(2)}, u32[]{:S(2)}) collective-permute-start(bf16[128,640]{1,0:T(8,128)(2,1)S(1)} %get-tuple-element.42.pair_ref), channel_id=1, source_target_pairs={{0,8},{4,12},{16,24},{20,28},{1,9},{5,13},{17,25},{21,29},{2,10},{... | collective-permute-start | bytes 491528 | tf_op jit(solution)/shard_map/ppermute | solution.py:413
  41.2 1.3 %collective-permute-start.7 = (bf16[128,640]{1,0:T(8,128)(2,1)S(1)}, bf16[128,640]{1,0:T(8,128)(2,1)S(1)}, u32[]{:S(2)}, u32[]{:S(2)}) collective-permute-start(bf16[128,640]{1,0:T(8,128)(2,1)S(1)} %get-tuple-element.42.pair_ref), channel_id=1, source_target_pairs={{0,12},{4,8},{16,28},{20,24},{1,13},{5,9},{17,29},{21,25},{2,14},{... | collective-permute-start | bytes 491528 | tf_op jit(solution)/shard_map/ppermute | solution.py:413
  42.5 1.3 %collective-permute-start.8 = (bf16[128,640]{1,0:T(8,128)(2,1)S(1)}, bf16[128,640]{1,0:T(8,128)(2,1)S(1)}, u32[]{:S(2)}, u32[]{:S(2)}) collective-permute-start(bf16[128,640]{1,0:T(8,128)(2,1)S(1)} %get-tuple-element.52), channel_id=1, source_target_pairs={{0,16},{4,20},{8,24},{12,28},{1,17},{5,21},{9,25},{13,29},{2,18},{... | collective-permute-start | bytes 491528 | tf_op jit(solution)/shard_map/ppermute | solution.py:413
  43.8 0.9 %fusion.5 = (f32[1,40,256]{2,1,0:T(8,128)S(1)}, f32[1,40,256]{2,1,0:T(8,128)S(1)}, f32[1,40,256]{2,1,0:T(8,128)S(1)}) fusion(f32[40,20,256]{2,0,1:T(8,128)} %param.14, f32[40,256]{1,0:T(8,128)S(1)} %get-tuple-element.36.cum_ref, f32[40]{0:T(128)S(1)} %get-tuple-element.59, f32[256]{0:T(256)S(1)} %compare_convert_fusion, f32[40]{0:T(128)S(1)} %get-tuple-element.60, ...), kind=kLoop, calls=%fused_computation.13 | loop fusion | flops 71680 | bytes 288224 | tf_op jit(solution)/shard_map/stack | solution.py:576
  44.7 1.2 %shard_map.95 = (f32[256,640]{1,0:T(8,128)S(1)}, f32[256,640]{1,0:T(8,128)S(1)}) custom-call(s32[4]{0:T(128)S(1)} %pad_add_fusion.info, f32[256,2560]{1,0:T(8,128)S(1)} %shard_map.93.sum_ref, bf16[256,256]{1,0:T(8,128)(2,1)S(1)} %get-tuple-element.34.kq_ref, bf16[16,256]{1,0:T(8,128)(2,1)S(1)} %get-tuple-element.35.pkq_ref, ...), custom_call_target="tpu_custom_call" | custom-call | flops 83886080 | bytes 5853184 | tf_op jit(solution)/shard_map/pallas_call | solution.py:365
  45.9 5.2 %collective-permute-done.8.refs_9_ = bf16[128,640]{1,0:T(8,128)(2,1)S(1)} collective-permute-done((bf16[128,640]{1,0:T(8,128)(2,1)S(1)}, bf16[128,640]{1,0:T(8,128)(2,1)S(1)}, u32[]{:S(2)}, u32[]{:S(2)}) %collective-permute-start.8) | collective-permute-done | bytes 163872 | tf_op jit(solution)/shard_map/ppermute | solution.py:413
  51.1 4.9 %collective-permute-start.9 = (bf16[128,640]{1,0:T(8,128)(2,1)S(1)}, bf16[128,640]{1,0:T(8,128)(2,1)S(1)}, u32[]{:S(2)}, u32[]{:S(2)}) collective-permute-start(bf16[128,640]{1,0:T(8,128)(2,1)S(1)} %collective-permute-done.8.refs_9_), channel_id=1, source_target_pairs={{16,20},{20,16},{24,28},{28,24},{17,21},{21,17},{25,29},{29,25},{1... | collective-permute-start | bytes 491528 | tf_op jit(solution)/shard_map/ppermute | solution.py:413
  56.0 4.7 %collective-permute-start.10 = (bf16[128,640]{1,0:T(8,128)(2,1)S(1)}, bf16[128,640]{1,0:T(8,128)(2,1)S(1)}, u32[]{:S(2)}, u32[]{:S(2)}) collective-permute-start(bf16[128,640]{1,0:T(8,128)(2,1)S(1)} %collective-permute-done.8.refs_9_), channel_id=1, source_target_pairs={{16,24},{20,28},{24,16},{28,20},{17,25},{21,29},{25,17},{29,21},{1... | collective-permute-start | bytes 491528 | tf_op jit(solution)/shard_map/ppermute | solution.py:413
  60.8 2.4 %collective-permute-start.11 = (bf16[128,640]{1,0:T(8,128)(2,1)S(1)}, bf16[128,640]{1,0:T(8,128)(2,1)S(1)}, u32[]{:S(2)}, u32[]{:S(2)}) collective-permute-start(bf16[128,640]{1,0:T(8,128)(2,1)S(1)} %collective-permute-done.8.refs_9_), channel_id=1, source_target_pairs={{16,28},{20,24},{24,20},{28,16},{17,29},{21,25},{25,21},{29,17},{1... | collective-permute-start | bytes 491528 | tf_op jit(solution)/shard_map/ppermute | solution.py:413
  63.2 1.2 %shard_map.96 = (f32[256,640]{1,0:T(8,128)S(1)}, f32[256,640]{1,0:T(8,128)S(1)}) custom-call(s32[4]{0:T(128)S(1)} %pad_add_fusion.info, f32[256,2560]{1,0:T(8,128)S(1)} %shard_map.93.sum_ref, bf16[256,256]{1,0:T(8,128)(2,1)S(1)} %get-tuple-element.34.kq_ref, bf16[16,256]{1,0:T(8,128)(2,1)S(1)} %get-tuple-element.35.pkq_ref, ...), custom_call_target="tpu_custom_call" | custom-call | flops 83886080 | bytes 5832704 | tf_op jit(solution)/shard_map/pallas_call | solution.py:365
  64.4 1.2 %shard_map.97 = (f32[256,640]{1,0:T(8,128)S(1)}, f32[256,640]{1,0:T(8,128)S(1)}) custom-call(s32[4]{0:T(128)S(1)} %pad_add_fusion.info, f32[256,2560]{1,0:T(8,128)S(1)} %shard_map.93.sum_ref, bf16[256,256]{1,0:T(8,128)(2,1)S(1)} %get-tuple-element.34.kq_ref, bf16[16,256]{1,0:T(8,128)(2,1)S(1)} %get-tuple-element.35.pkq_ref, ...), custom_call_target="tpu_custom_call" | custom-call | flops 83886080 | bytes 5832704 | tf_op jit(solution)/shard_map/pallas_call | solution.py:365
  65.7 1.2 %shard_map.98 = (f32[256,640]{1,0:T(8,128)S(1)}, f32[256,640]{1,0:T(8,128)S(1)}) custom-call(s32[4]{0:T(128)S(1)} %pad_add_fusion.info, f32[256,2560]{1,0:T(8,128)S(1)} %shard_map.93.sum_ref, bf16[256,256]{1,0:T(8,128)(2,1)S(1)} %get-tuple-element.34.kq_ref, bf16[16,256]{1,0:T(8,128)(2,1)S(1)} %get-tuple-element.35.pkq_ref, ...), custom_call_target="tpu_custom_call" | custom-call | flops 83886080 | bytes 5832704 | tf_op jit(solution)/shard_map/pallas_call | solution.py:365
  66.9 2.0 %collective-permute-done.11.refs_12_ = bf16[128,640]{1,0:T(8,128)(2,1)S(1)} collective-permute-done((bf16[128,640]{1,0:T(8,128)(2,1)S(1)}, bf16[128,640]{1,0:T(8,128)(2,1)S(1)}, u32[]{:S(2)}, u32[]{:S(2)}) %collective-permute-start.11) | collective-permute-done | bytes 163872 | tf_op jit(solution)/shard_map/ppermute | solution.py:413
  68.9 3.2 %shard_map.99 = bf16[256,2560]{1,0:T(8,128)(2,1)} custom-call(s32[4]{0:T(128)S(1)} %pad_add_fusion.info, f32[256,640]{1,0:T(8,128)S(1)} %get-tuple-element.43.refs_0_, f32[256,640]{1,0:T(8,128)S(1)} %get-tuple-element.45.refs_1_, f32[256,640]{1,0:T(8,128)S(1)} %get-tuple-element.46.refs_2_, f32[256,640]{1,0:T(8,128)S(1)} %get-tuple-element.47.refs_3_, ...), custom_call_target="tpu_custom_call" | custom-call | flops 167772160 | bytes 7284736 | tf_op jit(solution)/shard_map/pallas_call | solution.py:365
  (33 shorter events, 1.5 us)
Async XLA Ops:
  0.9 18.6 %collective-permute-start = (bf16[16,2816]{1,0:T(8,128)(2,1)S(1)}, bf16[16,2816]{1,0:T(8,128)(2,1)S(1)}, u32[]{:S(2)}, u32[]{:S(2)}) collective-permute-start(bf16[16,2816]{1,0:T(8,128)(2,1)S(1)} %slice.45), channel_id=1, source_target_pairs={{0,4},{4,8},{8,12},{12,16},{16,20},{20,24},{24,28},{1,5},{5,9},{9,... | collective-permute-start | bytes 270344 | tf_op jit(solution)/shard_map/ppermute | solution.py:413
  10.3 1.4 %copy-start.1 = (bf16[256,2816]{1,0:T(8,128)(2,1)S(1)}, bf16[256,2816]{1,0:T(8,128)(2,1)}, u32[]{:S(2)}) copy-start(bf16[256,2816]{1,0:T(8,128)(2,1)} %head_ref.1) | copy-start | bytes 4325380
  11.6 0.8 %copy-start.2 = (f32[4,2816]{1,0:T(4,128)S(1)}, f32[4,2816]{1,0:T(4,128)}, u32[]{:S(2)}) copy-start(f32[4,2816]{1,0:T(4,128)} %w_ref.3) | copy-start | bytes 135172
  12.4 0.8 %copy-start.3 = (f32[40,256]{1,0:T(8,128)S(1)}, f32[40,256]{1,0:T(8,128)}, u32[]{:S(2)}) copy-start(f32[40,256]{1,0:T(8,128)} %decay_ref.1) | copy-start | bytes 122884
  21.4 0.8 %copy-start.4 = (bf16[3,128,640]{2,1,0:T(8,128)(2,1)}, bf16[3,128,640]{2,1,0:T(8,128)(2,1)S(1)}, u32[]{:S(2)}) copy-start(bf16[3,128,640]{2,1,0:T(8,128)(2,1)S(1)} %get-tuple-element.44) | copy-start | bytes 1474564
  22.1 5.7 %copy-start.6 = (f32[40]{0:T(128)S(1)}, f32[40]{0:T(128)}, u32[]{:S(2)}) copy-start(f32[40]{0:T(128)} %param.15) | copy-start | bytes 484
  22.1 5.9 %copy-start.5 = (f32[2560]{0:T(1024)S(1)}, f32[2560]{0:T(1024)}, u32[]{:S(2)}) copy-start(f32[2560]{0:T(1024)} %param.16) | copy-start | bytes 30724
  22.1 14.8 %collective-permute-start.1 = (bf16[144,640]{1,0:T(8,128)(2,1)}, bf16[144,640]{1,0:T(8,128)(2,1)S(1)}, u32[]{:S(2)}, u32[]{:S(2)}) collective-permute-start(bf16[144,640]{1,0:T(8,128)(2,1)} %get-tuple-element.38), channel_id=1, source_target_pairs={{0,4},{4,0},{8,12},{12,8},{16,20},{20,16},{24,28},{28,24},{1,5},{5... | collective-permute-start | bytes 552968 | tf_op jit(solution)/shard_map/ppermute | solution.py:413
  22.1 14.8 %collective-permute-start.2 = (bf16[144,640]{1,0:T(8,128)(2,1)}, bf16[144,640]{1,0:T(8,128)(2,1)S(1)}, u32[]{:S(2)}, u32[]{:S(2)}) collective-permute-start(bf16[144,640]{1,0:T(8,128)(2,1)} %get-tuple-element.39), channel_id=1, source_target_pairs={{0,8},{4,12},{8,0},{12,4},{16,24},{20,28},{24,16},{28,20},{1,9},{5... | collective-permute-start | bytes 552968 | tf_op jit(solution)/shard_map/ppermute | solution.py:413
  24.1 12.8 %collective-permute-start.3 = (bf16[144,640]{1,0:T(8,128)(2,1)S(1)}, bf16[144,640]{1,0:T(8,128)(2,1)S(1)}, u32[]{:S(2)}, u32[]{:S(2)}) collective-permute-start(bf16[144,640]{1,0:T(8,128)(2,1)S(1)} %get-tuple-element.40), channel_id=1, source_target_pairs={{0,12},{4,8},{8,4},{12,0},{16,28},{20,24},{24,20},{28,16},{1,13},{... | collective-permute-start | bytes 552968 | tf_op jit(solution)/shard_map/ppermute | solution.py:413
  28.0 32.7 %collective-permute-start.4 = (bf16[3,128,640]{2,1,0:T(8,128)(2,1)}, bf16[3,128,640]{2,1,0:T(8,128)(2,1)S(1)}, u32[]{:S(2)}, u32[]{:S(2)}) collective-permute-start(bf16[3,128,640]{2,1,0:T(8,128)(2,1)} %copy-done.4), channel_id=1, source_target_pairs={{0,4},{8,12},{16,20},{24,28},{1,5},{9,13},{17,21},{25,29},{2,6},{1... | collective-permute-start | bytes 1474568 | tf_op jit(solution)/shard_map/ppermute | solution.py:413
  36.9 7.8 %copy-start = (bf16[256,2560]{1,0:T(8,128)(2,1)S(1)}, bf16[256,2560]{1,0:T(8,128)(2,1)}, u32[]{:S(2)}) copy-start(bf16[256,2560]{1,0:T(8,128)(2,1)} %gate_ref.7) | copy-start | bytes 3932164
  37.9 18.1 %collective-permute-start.5 = (bf16[128,640]{1,0:T(8,128)(2,1)S(1)}, bf16[128,640]{1,0:T(8,128)(2,1)S(1)}, u32[]{:S(2)}, u32[]{:S(2)}) collective-permute-start(bf16[128,640]{1,0:T(8,128)(2,1)S(1)} %get-tuple-element.42.pair_ref), channel_id=1, source_target_pairs={{8,12},{12,8},{24,28},{28,24},{9,13},{13,9},{25,29},{29,25},{10,14... | collective-permute-start | bytes 491528 | tf_op jit(solution)/shard_map/ppermute | solution.py:413
  39.9 24.6 %collective-permute-start.6 = (bf16[128,640]{1,0:T(8,128)(2,1)S(1)}, bf16[128,640]{1,0:T(8,128)(2,1)S(1)}, u32[]{:S(2)}, u32[]{:S(2)}) collective-permute-start(bf16[128,640]{1,0:T(8,128)(2,1)S(1)} %get-tuple-element.42.pair_ref), channel_id=1, source_target_pairs={{0,8},{4,12},{16,24},{20,28},{1,9},{5,13},{17,25},{21,29},{2,10},{... | collective-permute-start | bytes 491528 | tf_op jit(solution)/shard_map/ppermute | solution.py:413
  41.2 24.5 %collective-permute-start.7 = (bf16[128,640]{1,0:T(8,128)(2,1)S(1)}, bf16[128,640]{1,0:T(8,128)(2,1)S(1)}, u32[]{:S(2)}, u32[]{:S(2)}) collective-permute-start(bf16[128,640]{1,0:T(8,128)(2,1)S(1)} %get-tuple-element.42.pair_ref), channel_id=1, source_target_pairs={{0,12},{4,8},{16,28},{20,24},{1,13},{5,9},{17,29},{21,25},{2,14},{... | collective-permute-start | bytes 491528 | tf_op jit(solution)/shard_map/ppermute | solution.py:413
  42.5 8.7 %collective-permute-start.8 = (bf16[128,640]{1,0:T(8,128)(2,1)S(1)}, bf16[128,640]{1,0:T(8,128)(2,1)S(1)}, u32[]{:S(2)}, u32[]{:S(2)}) collective-permute-start(bf16[128,640]{1,0:T(8,128)(2,1)S(1)} %get-tuple-element.52), channel_id=1, source_target_pairs={{0,16},{4,20},{8,24},{12,28},{1,17},{5,21},{9,25},{13,29},{2,18},{... | collective-permute-start | bytes 491528 | tf_op jit(solution)/shard_map/ppermute | solution.py:413
  51.1 15.8 %collective-permute-start.9 = (bf16[128,640]{1,0:T(8,128)(2,1)S(1)}, bf16[128,640]{1,0:T(8,128)(2,1)S(1)}, u32[]{:S(2)}, u32[]{:S(2)}) collective-permute-start(bf16[128,640]{1,0:T(8,128)(2,1)S(1)} %collective-permute-done.8.refs_9_), channel_id=1, source_target_pairs={{16,20},{20,16},{24,28},{28,24},{17,21},{21,17},{25,29},{29,25},{1... | collective-permute-start | bytes 491528 | tf_op jit(solution)/shard_map/ppermute | solution.py:413
  56.0 10.9 %collective-permute-start.10 = (bf16[128,640]{1,0:T(8,128)(2,1)S(1)}, bf16[128,640]{1,0:T(8,128)(2,1)S(1)}, u32[]{:S(2)}, u32[]{:S(2)}) collective-permute-start(bf16[128,640]{1,0:T(8,128)(2,1)S(1)} %collective-permute-done.8.refs_9_), channel_id=1, source_target_pairs={{16,24},{20,28},{24,16},{28,20},{17,25},{21,29},{25,17},{29,21},{1... | collective-permute-start | bytes 491528 | tf_op jit(solution)/shard_map/ppermute | solution.py:413
  60.8 8.1 %collective-permute-start.11 = (bf16[128,640]{1,0:T(8,128)(2,1)S(1)}, bf16[128,640]{1,0:T(8,128)(2,1)S(1)}, u32[]{:S(2)}, u32[]{:S(2)}) collective-permute-start(bf16[128,640]{1,0:T(8,128)(2,1)S(1)} %collective-permute-done.8.refs_9_), channel_id=1, source_target_pairs={{16,28},{20,24},{24,20},{28,16},{17,29},{21,25},{25,21},{29,17},{1... | collective-permute-start | bytes 491528 | tf_op jit(solution)/shard_map/ppermute | solution.py:413

commit v2 on v1

v2 whole, which is shorter than its diff:
```python
import functools

import jax
import jax.numpy as jnp
from jax import lax
from jax.experimental import pallas as pl
from jax.experimental.pallas import tpu as pltpu
from jax.sharding import PartitionSpec as P

eps_norm = 1e-05
bf16 = jnp.bfloat16
f32 = jnp.float32
HALO = 16
PLACES = 4
LANES = 128
EXACT = lax.Precision.HIGHEST


def iota(shape, dim):
    return lax.broadcasted_iota(jnp.int32, shape, dim)


def dot(a, b, contract, precision=None):
    return lax.dot_general(
        a, b, (contract, ((), ())), precision=precision, preferred_element_type=f32
    )


def silu(v):
    return v * (0.5 * jnp.tanh(0.5 * v) + 0.5)


def segment_bounds(lengths, recordings):
    bounds, total = [], 0
    for index in range(recordings - 1):
        total = total + lengths[index]
        bounds.append(total)
    return bounds


def segment_of(pos, bounds):
    found = jnp.where(pos >= 0, 0, -1)
    for bound in bounds:
        found = found + jnp.where(pos >= bound, 1, 0)
    return found


def same_segment(pos, other, bounds):
    return (segment_of(pos, bounds) == segment_of(other, bounds)).astype(f32)


def two_parts(value):
    high = value.astype(bf16).astype(f32)
    return high, value - high


def spread(rows, first_head, columns, head_dim):
    offset = iota((rows, LANES), 0) - iota((rows, LANES), 1) // head_dim
    tiles = []
    for tile in range(columns // LANES):
        tiles.append(
            jnp.where(offset == first_head + tile * (LANES // head_dim), 1.0, 0.0).astype(bf16)
        )
    return jnp.concatenate(tiles, axis=1)


def conv_taps(shifts, weight_ref, lo, hi):
    taps = len(shifts)
    total = weight_ref[taps : taps + 1, lo:hi]
    for tap, piece in enumerate(shifts):
        total = total + weight_ref[tap : tap + 1, lo:hi] * piece
    return silu(total)


def features_kernel(
    dims, group, x_hbm, w_hbm, b_hbm, decay_hbm, lengths_hbm,
    xs_ref, kq_ref, part_ref, cum_ref, cumt_ref, entry_ref, head_ref, weight_ref, first_ref,
    lengths, x_ref, decay_ref, shift_ref, scaled_ref, sems,
):
    tok, heads, head_dim, taps, recordings, width, state = dims
    block = 2 * state
    fetches = [
        pltpu.make_async_copy(source, target, sems.at[at])
        for at, (source, target) in enumerate(
            (
                (lengths_hbm, lengths),
                (decay_hbm, decay_ref),
                (x_hbm, x_ref),
                (w_hbm, weight_ref.at[:taps]),
                (b_hbm, weight_ref.at[taps : taps + 1]),
            )
        )
    ]
    for fetch in fetches:
        fetch.start()

    apart = iota((tok, tok), 0) - iota((tok, tok), 1)
    upper = jnp.where(apart <= 0, 1.0, 0.0)
    lower = jnp.where(apart >= 0, 1.0, 0.0)
    fetches[0].wait()
    bounds = segment_bounds(lengths, recordings)
    first = group[0] * tok
    pos = first + iota((tok, LANES), 0)
    for tap in range(1, taps):
        same = same_segment(pos, pos - tap, bounds)
        same = jnp.concatenate([same] * (tok // LANES), axis=1)
        shift_ref[(tap - 1) * tok : tap * tok] = jnp.where(apart == tap, same, 0.0).astype(bf16)
    fetches[1].wait()
    decay = jnp.concatenate(
        [decay_ref[...], jnp.zeros((LANES - heads, tok), f32)], axis=0
    )
    cum = dot(decay_ref[...], upper, ((1,), (0,)), EXACT)
    cum_ref[...] = cum
    cumt = dot(lower, decay, ((1,), (1,)), EXACT)
    cumt_ref[...] = cumt
    end = cumt[tok - 1 : tok, :]
    last = first + tok - 1
    ewt = jnp.exp(end - cumt) * same_segment(pos, last + 0 * pos, bounds)
    along = first + iota((heads, tok), 1)
    entry_ref[...] = jnp.exp(cum) * same_segment(along, first - 1 + 0 * along, bounds)
    ewt = jnp.concatenate(two_parts(ewt), axis=1).astype(bf16)
    for fetch in fetches[2:]:
        fetch.wait()

    head_ref[...] = x_ref[:HALO]
    keys = None
    for at in [width // block] + list(range(width // block)):
        lo = at * block
        rows = x_ref[:, lo : lo + block]
        moved = dot(shift_ref[...], rows, ((1,), (0,)))
        shifts = [rows.astype(f32)]
        for tap in range(1, taps):
            shifts.append(moved[(tap - 1) * tok : tap * tok])
        value = conv_taps(shifts, weight_ref, lo, lo + block)
        if keys is None:
            kq_ref[...] = value.astype(bf16)
            keys = jnp.transpose(value[:, :state])
            keys = jnp.where(iota((state, tok), 1) >= HALO, keys, 0.0).astype(bf16)
            continue
        xs = value.astype(bf16)
        xs_ref[:, lo : lo + block] = xs
        copies = spread(LANES, lo // head_dim, block, head_dim)
        weight = dot(ewt, jnp.concatenate([copies, copies], axis=0), ((1,), (0,)))
        first_ref[:, lo : lo + block] = weight[:HALO]
        scaled_ref[:, lo : lo + block] = (xs.astype(f32) * weight).astype(bf16)
    part_ref[...] = dot(keys, scaled_ref[...], ((1,), (0,)))


def join_kernel(
    dims, lengths, group, halo_ref, head_ref, w_ref, first_ref, cumt_ref, part_ref,
    px_ref, pkq_ref, own_ref, one_ref, two_ref, three_ref, scaled_ref,
):
    tok, taps, recordings, width, state = dims
    bounds = segment_bounds(lengths, recordings)
    first = group[0] * tok
    pos = first + iota((HALO, LANES), 0)
    same = [same_segment(pos, pos - tap, bounds) for tap in range(1, taps)]

    def features(lo):
        hi = lo + LANES
        both = jnp.concatenate(
            [halo_ref[:, lo:hi].astype(f32), head_ref[:, lo:hi].astype(f32)], axis=0
        )
        shifts = [both[HALO:]] + [
            pltpu.roll(both, tap, 0)[HALO:] * same[tap - 1] for tap in range(1, taps)
        ]
        return conv_taps(shifts, w_ref, lo, hi)

    keys = None
    for lo in range(width, width + 2 * state, LANES):
        part = features(lo).astype(bf16)
        pkq_ref[:, lo - width : lo - width + LANES] = part
        if lo == width:
            keys = part
    for lo in range(0, width, LANES):
        xs = features(lo).astype(bf16)
        px_ref[:, lo : lo + LANES] = xs
        scaled_ref[:, lo : lo + LANES] = (
            xs.astype(f32) * first_ref[:, lo : lo + LANES]
        ).astype(bf16)

    end = cumt_ref[tok - 1 : tok, :]
    alive = same_segment(first + tok - 1 + 0 * pos[:1], first - 1 + 0 * pos[:1], bounds)
    through = jnp.exp(end) * alive
    high, rest = two_parts(through)
    mid, low = two_parts(rest)
    row = iota((HALO, LANES), 0)
    tail = jnp.where(row == 0, high, jnp.where(row == 1, mid, jnp.where(row == 2, low, 0.0)))
    place = lax.rem(group[0], PLACES)
    cols = width // PLACES
    for mask, out_ref in ((3, three_ref), (1, one_ref), (2, two_ref), (0, own_ref)):
        where = pl.multiple_of(jnp.bitwise_xor(place, mask) * cols, LANES)
        value = part_ref[:, pl.ds(where, cols)] + dot(
            keys, scaled_ref[:, pl.ds(where, cols)], ((0,), (0,))
        )
        out_ref[:state, :] = value.astype(bf16)
        out_ref[state:, :LANES] = tail.astype(bf16)
        out_ref[state:, LANES:] = jnp.zeros((HALO, cols - LANES), bf16)


def combine_kernel(
    dims, lengths, group, own_ref, one_ref, two_ref, three_ref, quad_ref, scale_ref, weight_ref
):
    state, head_dim = dims
    cols = quad_ref.shape[1]
    place = lax.rem(group[0], PLACES)
    refs = (own_ref, one_ref, two_ref, three_ref)
    got = []
    for ref in refs:
        tail = ref[state:, :LANES].astype(f32)
        got.append(tail[0:1] + tail[1:2] + tail[2:3])
    through = []
    for at in range(PLACES):
        total = jnp.zeros((1, LANES), f32)
        for mask in range(PLACES):
            total = total + jnp.where(jnp.bitwise_xor(place, mask) == at, got[mask], 0.0)
        through.append(total)
    ones = jnp.ones((1, LANES), f32)
    rows = []
    for mask in range(PLACES):
        at = jnp.bitwise_xor(place, mask)
        product = ones
        for later in range(1, PLACES):
            product = product * jnp.where(later > at, through[later], ones)
        rows.append(product)
    for mask in range(PLACES):
        at = jnp.bitwise_xor(place, mask)
        rows.append(jnp.where(at == 0, through[1], jnp.where(at == 1, ones, 0.0 * ones)))
    before_quad = ones
    for earlier in range(PLACES - 1):
        before_quad = before_quad * jnp.where(earlier < place, through[earlier], ones)
    everything = through[0] * through[1] * through[2] * through[3]
    row = iota((8, LANES), 0)
    scale = jnp.where(row == 1, jnp.where(place == 3, through[2], ones), ones)
    scale = jnp.where(row == 2, before_quad, scale)
    scale_ref[...] = jnp.where(row == 3, everything, scale)
    weights = jnp.concatenate(rows, axis=0)
    high, low = two_parts(weights)
    copies = spread(LANES, place * (cols // head_dim), cols, head_dim)
    weights = dot(high.astype(bf16), copies, ((1,), (0,))) + dot(
        low.astype(bf16), copies, ((1,), (0,))
    )
    weight_ref[...] = weights
    for lo in range(0, cols, LANES):
        hi = lo + LANES
        quad = jnp.zeros((state, LANES), f32)
        for mask, ref in enumerate(refs):
            quad = quad + ref[:state, lo:hi].astype(f32) * weights[mask : mask + 1, lo:hi]
        quad_ref[:, lo:hi] = quad.astype(bf16)


def pair_kernel(
    dims, lengths, group, own_ref, one_ref, two_ref, three_ref, weight_ref, two_in, three_in,
    pair_ref, own_out, two_out, three_out,
):
    (state,) = dims
    cols = pair_ref.shape[1]
    for lo in range(0, cols, LANES):
        hi = lo + LANES
        pair = jnp.zeros((state, LANES), f32)
        for mask, ref in enumerate((own_ref, one_ref, two_ref, three_ref)):
            weight = weight_ref[PLACES + mask : PLACES + mask + 1, lo:hi]
            pair = pair + ref[:state, lo:hi].astype(f32) * weight
        pair_ref[:, lo:hi] = pair.astype(bf16)
    own_out[...] = own_ref[:state]
    two_out[...] = two_in[:state]
    three_out[...] = three_in[:state]


def with_head(patch, body):
    return jnp.concatenate([patch, body[HALO:]], axis=0)


def scores_kernel(dims, lengths, group, kq_ref, pkq_ref, queries_ref, scores_ref):
    tok, recordings, state = dims
    bounds = segment_bounds(lengths, recordings)
    first = group[0] * tok
    kq = with_head(pkq_ref[...], kq_ref[...])
    queries_ref[...] = kq[:, state:]
    s_pos = iota((tok, tok), 0)
    t_pos = iota((tok, tok), 1)
    valid = same_segment(first + s_pos, first + t_pos, bounds) * jnp.where(s_pos <= t_pos, 1.0, 0.0)
    scores_ref[...] = dot(kq[:, :state], kq[:, state:], ((1,), (1,))) * valid


def local_kernel(
    dims, mask, lengths, group, xs_ref, px_ref, scores_ref, cum_ref, cumt_ref, level_ref, skip_ref,
    out_ref, mixing_ref,
):
    tok, head_dim, low_bits = dims
    cols = out_ref.shape[1]
    count = cols // head_dim
    quarter = jnp.bitwise_xor(lax.rem(group[0], PLACES), mask)
    first_head = quarter * count
    rows = 32
    row_bits = rows.bit_length() - 1
    where = pl.multiple_of(quarter * cols, LANES)
    cumt = pltpu.roll(cumt_ref[...], LANES - first_head, 1)
    diff = jnp.bitwise_xor(iota((rows, tok), 0), lax.rem(iota((rows, tok), 1), rows))
    near = jnp.zeros((rows, tok), jnp.int32)
    for bit in range(row_bits):
        near = near + (diff >= 2**bit).astype(jnp.int32)
    token = iota((1, tok), 1) // rows
    lane = iota((1, 2 * head_dim), 1)
    pieces = []
    for head in range(count):
        if head % 2 == 0:
            lo = head * head_dim
            here = pl.ds(pl.multiple_of(where + lo, LANES), 2 * head_dim)
            xs = with_head(px_ref[:, here], xs_ref[:, here]).astype(f32)
            xst = jnp.transpose(xs).astype(bf16)
        cum = cum_ref[pl.ds(first_head + head, 1), :]
        levels = [level_ref[level, pl.ds(first_head + head, 1), :] for level in range(low_bits + 1)]
        inner = jnp.broadcast_to(levels[0], (rows, tok))
        for level in range(1, row_bits + 1):
            inner = jnp.where(near == level, levels[level], inner)
        for s in range(0, tok, rows):
            at = s // rows
            start = s // LANES * LANES
            outer = jnp.zeros((1, tok), f32)
            apart = jnp.bitwise_xor(token, at)
            for level in range(row_bits + 1, low_bits + 1):
                outer = jnp.where(apart >= 2 ** (level - row_bits - 1), levels[level], outer)
            picked = jnp.where(token == at, inner, outer)[:, start:]
            gap = cum[:, start:] - cumt[s : s + rows, head : head + 1]
            value = jnp.exp(jnp.minimum(gap, 0.0)) * picked
            mixing_ref[head % 2, s : s + rows, start:] = (
                value * scores_ref[s : s + rows, start:]
            ).astype(bf16)
            if start:
                mixing_ref[head % 2, s : s + rows, :start] = jnp.zeros((rows, start), bf16)
        pieces.append(
            dot(
                xst[head % 2 * head_dim : (head % 2 + 1) * head_dim],
                mixing_ref[head % 2],
                ((1,), (0,)),
            )
        )
        if head % 2 == 1:
            both = jnp.transpose(jnp.concatenate(pieces[-2:], axis=0))
            skip = jnp.where(
                lane < head_dim, skip_ref[first_head + head - 1], skip_ref[first_head + head]
            )
            out_ref[:, lo : lo + 2 * head_dim] = both + skip * xs


def spread_rows(coef, copies):
    high, low = two_parts(coef)
    return dot(high.astype(bf16), copies, ((0,), (0,))) + dot(
        low.astype(bf16), copies, ((0,), (0,))
    )


def far_kernel(
    dims, mask, lengths, group, sum_ref, queries_ref, level_ref, entry_ref, scale_ref, low_ref,
    pair_ref, gate_ref, out_ref, next_ref,
):
    head_dim, state = dims
    cols = sum_ref.shape[1]
    heads = entry_ref.shape[0]
    quarter = jnp.bitwise_xor(lax.rem(group[0], PLACES), mask)
    first = quarter * (cols // head_dim)
    queries = queries_ref[...]
    copies = spread(heads, first, cols, head_dim)
    scale = jnp.transpose(scale_ref[...])
    entry = entry_ref[...]
    factors = []
    for bit in range(3):
        on = jnp.where(lax.rem(group[0] // 2**bit, 2) == 1, 1.0, 0.0)
        coef = level_ref[bit] * entry * (scale[:heads, bit : bit + 1] * on)
        factors.append(spread_rows(coef, copies))
    total = sum_ref[...]
    for bit, ref in enumerate((low_ref, pair_ref)):
        total = total + dot(queries, ref[:state, :], ((1,), (0,))) * factors[bit]
    where = pl.multiple_of(quarter * cols, LANES)
    gate = silu(gate_ref[:, pl.ds(where, cols)].astype(f32))
    out_ref[...] = total * gate
    next_ref[...] = factors[2] * gate


def final_kernel(dims, lengths, group, *refs):
    count, rows = dims
    sums = refs[:PLACES]
    factors = refs[PLACES : 2 * PLACES]
    queries_ref = refs[2 * PLACES]
    states = refs[2 * PLACES + 1 : 3 * PLACES + 1]
    gain_ref, out_ref, gated_ref, scale_ref = refs[3 * PLACES + 1 :]
    place = lax.rem(group[0], PLACES)
    cols = sums[0].shape[1]
    step = pl.program_id(0)

    @pl.when(step == 0)
    def _():
        queries = queries_ref[...]
        squares = jnp.zeros((queries.shape[0], LANES), f32)
        for mask in range(PLACES):
            read = dot(queries, states[mask][...], ((1,), (0,)))
            value = sums[mask][...] + read * factors[mask][...]
            gated_ref[mask] = value
            for lo in range(0, cols, LANES):
                squares = squares + value[:, lo : lo + LANES] * value[:, lo : lo + LANES]
        mean = jnp.sum(squares, axis=1, keepdims=True) / count
        scale_ref[...] = jnp.broadcast_to(lax.rsqrt(mean + eps_norm), scale_ref.shape)

    here = pl.ds(pl.multiple_of(step * rows, rows), rows)
    scale = scale_ref[here, :]
    for mask in range(PLACES):
        where = pl.multiple_of(jnp.bitwise_xor(place, mask) * cols, LANES)
        for lo in range(0, cols, LANES):
            columns = pl.ds(pl.multiple_of(where + lo, LANES), LANES)
            out_ref[:, columns] = (
                gated_ref[mask, here, lo : lo + LANES] * scale * gain_ref[:, columns]
            ).astype(bf16)


VMEM = pl.BlockSpec(memory_space=pltpu.VMEM)
HBM = pl.BlockSpec(memory_space=pltpu.HBM)
SMEM = pl.BlockSpec(memory_space=pltpu.SMEM)


def call(
    kernel, scalars, operands, outs, scratch=(), flops=0, specs=None, out_specs=None, grid=(), mb=40, after=()
):
    moved = sum(a.size * a.dtype.itemsize for a in operands)
    moved += sum(o.size * o.dtype.itemsize for o in outs)
    specs = list(specs or [VMEM] * len(operands))
    first, last = len(scalars) + len(operands), len(scalars) + len(operands) + len(after)

    def body(*refs):
        kernel(*refs[:first], *refs[last:])

    return pl.pallas_call(
        body,
        grid=grid,
        in_specs=[SMEM] * len(scalars) + specs + [pl.BlockSpec(memory_space=pl.ANY)] * len(after),
        out_specs=out_specs or [VMEM] * len(outs),
        scratch_shapes=list(scratch),
        out_shape=outs,
        compiler_params=pltpu.CompilerParams(vmem_limit_bytes=mb * 2**20),
        cost_estimate=pl.CostEstimate(
            flops=flops, bytes_accessed=moved, transcendentals=0
        ),
    )(*scalars, *operands, *after)


def shape(dims, dtype):
    return jax.ShapeDtypeStruct(dims, dtype)


def per_device(
    mixed_input,
    conv_weight,
    conv_bias,
    gate_input,
    log_decay,
    level_weights,
    skip_gain,
    norm_gain,
    seg_lengths,
):
    tok, channels = mixed_input.shape
    width = gate_input.shape[1]
    heads = log_decay.shape[0]
    head_dim = width // heads
    state = (channels - width) // 2
    taps = conv_weight.shape[0]
    recordings = seg_lengths.shape[0]
    low_bits = tok.bit_length() - 1
    groups = lax.axis_size("group")
    high_bits = groups.bit_length() - 1
    group = lax.axis_index("group").astype(jnp.int32)
    place = group % PLACES
    cols = width // PLACES
    block = 2 * state
    levels = jnp.transpose(level_weights, (1, 0, 2))

    def send(value, pairs):
        return lax.ppermute(value, "group", pairs)

    def quad_send(value, mask, wanted=lambda target: True):
        pairs = [(g, g ^ mask) for g in range(groups)]
        return send(value, pairs)

    halo = send(mixed_input[tok - HALO :], [(g, g + 1) for g in range(groups - 1)])

    def in_hbm(value):
        return pltpu.with_memory_space_constraint(value, pltpu.HBM)

    xs, kq, part, cum, cumt, entry, head, weights, first, lengths = call(
        functools.partial(
            features_kernel, (tok, heads, head_dim, taps, recordings, width, state)
        ),
        (group[None],),
        (
            in_hbm(mixed_input),
            in_hbm(conv_weight),
            in_hbm(conv_bias[None, :]),
            in_hbm(log_decay),
            in_hbm(seg_lengths),
        ),
        [
            shape((tok, width), bf16),
            shape((tok, block), bf16),
            shape((state, width), f32),
            shape((heads, tok), f32),
            shape((tok, LANES), f32),
            shape((heads, tok), f32),
            shape((HALO, channels), bf16),
            shape((8, channels), f32),
            shape((HALO, width), f32),
            shape((recordings,), jnp.int32),
        ],
        [
            pltpu.VMEM((tok, channels), bf16),
            pltpu.VMEM((heads, tok), f32),
            pltpu.VMEM(((taps - 1) * tok, tok), bf16),
            pltpu.VMEM((tok, width), bf16),
            pltpu.SemaphoreType.DMA((5,)),
        ],
        flops=2 * tok * width * state,
        specs=[HBM] * 5,
        out_specs=[VMEM] * 9 + [SMEM],
    )
    scalars = (lengths, group[None])

    payload = shape((state + HALO, cols), bf16)
    px, pkq, own, one, two, three = call(
        functools.partial(join_kernel, (tok, taps, recordings, width, state)),
        scalars,
        (halo, head, weights, first, cumt, part),
        [shape((HALO, width), bf16), shape((HALO, block), bf16)] + [payload] * PLACES,
        [pltpu.VMEM((HALO, width), bf16)],
        flops=2 * HALO * width * state,
    )

    queries, scores = call(
        functools.partial(scores_kernel, (tok, recordings, state)),
        scalars,
        (kq, pkq),
        [shape((tok, state), bf16), shape((tok, tok), f32)],
        flops=2 * tok * tok * state,
    )

    def local(mask, after=()):
        return call(
            functools.partial(local_kernel, (tok, head_dim, low_bits), mask),
            scalars,
            (xs, px, scores, cum, cumt, levels[: low_bits + 1], skip_gain),
            [shape((tok, cols), f32)],
            [pltpu.VMEM((2, tok, tok), bf16)],
            specs=[VMEM] * 6 + [SMEM],
            flops=2 * cols * tok * tok,
            after=after,
        )[0]

    got_three = quad_send(three, 3)
    got_one = quad_send(one, 1)
    got_two = quad_send(two, 2)
    sums = [local(0), local(1)]
    received = (own, got_one, got_two, got_three)
    quad, scale, spread_weights = call(
        functools.partial(combine_kernel, (state, head_dim)),
        scalars,
        received,
        [shape((state, cols), bf16), shape((8, LANES), f32), shape((8, cols), f32)],
        flops=4 * state * cols,
        after=sums,
    )
    sums.append(local(2, (quad,)))
    pair, own_state, two_state, three_state = call(
        functools.partial(pair_kernel, (state,)),
        scalars,
        received + (spread_weights, two, three),
        [shape((state, cols), bf16)] * 4,
        flops=4 * state * cols,
        after=sums[2:],
    )
    sums.append(local(3, (pair,)))

    befores = [scale[0, :heads], scale[1, :heads], scale[2, :heads]]
    crossed = []
    running, total = quad, scale[3, :heads]
    for bit in range(2, high_bits):
        mask = 2**bit
        last = bit + 1 == high_bits
        far = quad_send(running, mask, lambda target: not last or target & mask)
        crossed.append(far)
        if not last:
            on_top = group // mask % 2 == 1
            far_total = quad_send(total, mask)

            def columns(value):
                mine = lax.dynamic_slice(value, (place * (cols // head_dim),), (cols // head_dim,))
                return jnp.repeat(mine, head_dim)[None, :]

            running = jnp.where(
                on_top,
                far.astype(f32) * columns(total) + running.astype(f32),
                running.astype(f32) * columns(far_total) + far.astype(f32),
            ).astype(bf16)
            befores.append(jnp.where(on_top, far_total * befores[-1], befores[-1]))
            total = total * far_total

    odd = lambda target: target & 1
    lows = [
        got_one,
        quad_send(own_state, 1, odd),
        quad_send(three_state, 1, odd),
        quad_send(two_state, 1, odd),
    ]
    pairs = [pair] + [
        quad_send(pair, mask, lambda target: target & 2) for mask in range(1, PLACES)
    ]

    def all_quarters(value, bit):
        return [value] + [
            quad_send(value, mask, lambda target: target & 2**bit)
            for mask in range(1, PLACES)
        ]

    far_levels = levels[low_bits + 1 : low_bits + 4]
    halves = [
        list(
            call(
                functools.partial(far_kernel, (head_dim, state), mask),
                scalars,
                (sums[mask], queries, far_levels, entry, scale, lows[mask], pairs[mask], gate_input),
                [shape((tok, cols), f32), shape((tok, cols), f32)],
                flops=4 * tok * cols * state,
            )
        )
        for mask in range(PLACES)
    ]
    tops = [all_quarters(value, bit + 2) for bit, value in enumerate(crossed)]
    for bit in range(3, high_bits):
        coef = levels[low_bits + 1 + bit] * entry
        coef = coef * jnp.where(group // 2**bit % 2 == 1, befores[bit], 0.0)[:, None]
        for mask in range(PLACES):
            first_head = (place ^ mask) * (cols // head_dim)
            mine = lax.dynamic_slice_in_dim(coef, first_head, cols // head_dim, axis=0)
            gate = lax.dynamic_slice_in_dim(gate_input, (place ^ mask) * cols, cols, axis=1)
            read = jnp.dot(queries, tops[bit - 2][mask], preferred_element_type=f32)
            read = read * jnp.repeat(mine, head_dim, axis=0).T
            halves[mask][0] = halves[mask][0] + read * jax.nn.silu(gate.astype(f32))

    rows = 64
    return call(
        functools.partial(final_kernel, (float(width), rows)),
        scalars,
        [h[0] for h in halves]
        + [h[1] for h in halves]
        + [queries]
        + tops[0]
        + [norm_gain[None, :]],
        [shape((tok, width), bf16)],
        [pltpu.VMEM((PLACES, tok, cols), f32), pltpu.VMEM((tok, LANES), f32)],
        out_specs=[pl.BlockSpec((rows, width), lambda i, *_: (i, 0))],
        grid=(tok // rows,),
        flops=2 * tok * width * state,
    )[0]


def solution(mesh):
    in_specs = (
        P(("batch", "group"), None),
        P(),
        P(),
        P(("batch", "group"), None),
        P(None, ("batch", "group")),
        P(None, None, ("batch", "group")),
        P(),
        P(),
        P("batch"),
    )
    out_specs = P(("batch", "group"), None)
    return jax.shard_map(
        per_device, mesh=mesh, in_specs=in_specs, out_specs=out_specs, check_vma=False
    )
```

time: 72.8 us -> 63.3 us (0.87)
  the two profiles are of different devices: /device:TPU:24 before, /device:TPU:0 now
where the time goes in v2:
time: 63.3 us; the launch traced here: 63.1 us
  Pallas kernels  26.2 us (41%)
  starting transfers between devices  23.5 us (37%)
  waiting for transfers between devices  10.9 us (17%)
  local copies, waits for them, and re-layouts  2.28 us (4%)
    pallas_call x14, Pallas kernels, call(): pl.pallas_call(body, grid=grid, in_specs=[SMEM] * len(scalars) + specs +...  26.2 us
    ppermute x14, starting transfers between devices, send(): return lax.ppermute(value, 'group', pairs)  23.5 us
    ppermute x14, waiting for transfers between devices, send(): return lax.ppermute(value, 'group', pairs)  10.9 us
    broadcast_in_dim x1, local copies, waits for them, and re-layouts, per_device(): conv_bias[None, :]  1.32 us
  transfers between devices with their start and end apart: 14, of which 5 were waited for; matrix products, arithmetic and copies ran while one was open for 2% of the time, Pallas kernels for 34%

profile of v2, /device:TPU:0, one launch (start us, length us, event | category | flops | bytes accessed | tf_op | source)
XLA Modules:
  0.0 63.1 jit_solution(6223314241650790086)
XLA Ops:
  0.0 0.9 %slice.12 = bf16[16,2816]{1,0:T(8,128)(2,1)S(1)} slice(bf16[256,2816]{1,0:T(8,128)(2,1)} %refs_1_.1), slice={[240:256], [0:2816]} | slice | bytes 180224 | tf_op jit(solution)/shard_map/slice | solution.py:484
  0.9 4.8 %collective-permute-start = (bf16[16,2816]{1,0:T(8,128)(2,1)S(1)}, bf16[16,2816]{1,0:T(8,128)(2,1)S(1)}, u32[]{:S(2)}, u32[]{:S(2)}) collective-permute-start(bf16[16,2816]{1,0:T(8,128)(2,1)S(1)} %slice.12), channel_id=1, source_target_pairs={{0,4},{4,8},{8,12},{12,16},{16,20},{20,24},{24,28},{1,5},{5,9},{9,... | collective-permute-start | bytes 270344 | tf_op jit(solution)/shard_map/ppermute | solution.py:478
  5.7 1.3 %broadcast_in_dim.11.refs_3_ = f32[1,2816]{1,0:T(1,128)} reshape(f32[2816]{0:T(1024)} %param.11) | data formatting | bytes 22528 | tf_op jit(solution)/shard_map/broadcast_in_dim | solution.py:497
  7.1 3.8 %shard_map.91 = (bf16[256,2560]{1,0:T(8,128)(2,1)S(1)}, bf16[256,256]{1,0:T(8,128)(2,1)S(1)}, f32[128,2560]{1,0:T(8,128)S(1)}, f32[40,256]{1,0:T(8,128)S(1)}, f3...) custom-call(s32[1]{0:T(128)} %bitcast.refs_0_.refs_1_, ...), custom_call_target="tpu_custom_call" | custom-call | flops 167772160 | bytes 4848664 | tf_op jit(solution)/shard_map/pallas_call | solution.py:432
  10.9 1.1 %shard_map.92 = (bf16[16,2560]{1,0:T(8,128)(2,1)S(1)}, bf16[16,256]{1,0:T(8,128)(2,1)S(1)}, bf16[144,640]{1,0:T(8,128)(2,1)S(1)}, bf16[144,640]{1,0:T(8,128)(2,1...) custom-call(s32[3]{0:T(128)S(1)} %get-tuple-element.38.refs_0_, s32[1]{0:T(128)} %bitcast.refs_0_.refs_1_, ...), custom_call_target="tpu_custom_call" | custom-call | flops 10485760 | bytes 2703360 | tf_op jit(solution)/shard_map/pallas_call | solution.py:432
  12.0 1.6 %collective-permute-start.1 = (bf16[144,640]{1,0:T(8,128)(2,1)S(1)}, bf16[144,640]{1,0:T(8,128)(2,1)S(1)}, u32[]{:S(2)}, u32[]{:S(2)}) collective-permute-start(bf16[144,640]{1,0:T(8,128)(2,1)S(1)} %get-tuple-element.53), channel_id=1, source_target_pairs={{0,4},{4,0},{8,12},{12,8},{16,20},{20,16},{24,28},{28,24},{1,5},{5... | collective-permute-start | bytes 552968 | tf_op jit(solution)/shard_map/ppermute | solution.py:478
  13.6 1.6 %collective-permute-start.2 = (bf16[144,640]{1,0:T(8,128)(2,1)S(1)}, bf16[144,640]{1,0:T(8,128)(2,1)S(1)}, u32[]{:S(2)}, u32[]{:S(2)}) collective-permute-start(bf16[144,640]{1,0:T(8,128)(2,1)S(1)} %get-tuple-element.54.refs_7_), channel_id=1, source_target_pairs={{0,8},{4,12},{8,0},{12,4},{16,24},{20,28},{24,16},{28,20},{1,9},{5... | collective-permute-start | bytes 552968 | tf_op jit(solution)/shard_map/ppermute | solution.py:478
  15.6 0.7 %shard_map.93 = (bf16[256,128]{1,0:T(8,128)(2,1)S(1)}, f32[256,256]{1,0:T(8,128)S(1)}) custom-call(s32[3]{0:T(128)S(1)} %get-tuple-element.38.refs_0_, s32[1]{0:T(128)} %bitcast.refs_0_.refs_1_, bf16[256,256]{1,0:T(8,128)(2,1)S(1)} %get-tuple-element.46.refs_2_, bf16[16,256]{1,0:T(8,128)(2,1)S(1)} %get-tuple-element.47.refs_3_), custom_call_target="tpu_custom_call" | custom-call | flops 16777216 | bytes 466944 | tf_op jit(solution)/shard_map/pallas_call | solution.py:432
  16.3 2.3 %shard_map.95.refs_7_.refs_2_ = f32[256,640]{1,0:T(8,128)S(1)} custom-call(s32[3]{0:T(128)S(1)} %get-tuple-element.38.refs_0_, s32[1]{0:T(128)} %bitcast.refs_0_.refs_1_, bf16[256,2560]{1,0:T(8,128)(2,1)S(1)} %get-tuple-element.39.refs_2_, bf16[16,2560]{1,0:T(8,128)(2,1)S(1)} %get-tuple-element.45.refs_3_, f32[256,256]{1,0:T(8,128)S(1)} %get-tuple-element.48.refs_4_, ...), custom_call_target="tpu_custom_call" | custom-call | flops 83886080 | bytes 2850976 | tf_op jit(solution)/shard_map/pallas_call | solution.py:432
  18.6 2.3 %shard_map.94.refs_6_.refs_2_ = f32[256,640]{1,0:T(8,128)S(1)} custom-call(s32[3]{0:T(128)S(1)} %get-tuple-element.38.refs_0_, s32[1]{0:T(128)} %bitcast.refs_0_.refs_1_, bf16[256,2560]{1,0:T(8,128)(2,1)S(1)} %get-tuple-element.39.refs_2_, bf16[16,2560]{1,0:T(8,128)(2,1)S(1)} %get-tuple-element.45.refs_3_, f32[256,256]{1,0:T(8,128)S(1)} %get-tuple-element.48.refs_4_, ...), custom_call_target="tpu_custom_call" | custom-call | flops 83886080 | bytes 2850976 | tf_op jit(solution)/shard_map/pallas_call | solution.py:432
  21.2 2.1 %collective-permute-done.3.refs_5_ = bf16[144,640]{1,0:T(8,128)(2,1)S(1)} collective-permute-done((bf16[144,640]{1,0:T(8,128)(2,1)S(1)}, bf16[144,640]{1,0:T(8,128)(2,1)S(1)}, u32[]{:S(2)}, u32[]{:S(2)}) %collective-permute-start.3) | collective-permute-done | bytes 184352 | tf_op jit(solution)/shard_map/ppermute | solution.py:478
  23.3 0.9 %shard_map.96 = (bf16[128,640]{1,0:T(8,128)(2,1)S(1)}, f32[8,128]{1,0:T(8,128)S(1)}, f32[8,640]{1,0:T(8,128)S(1)}) custom-call(s32[3]{0:T(128)S(1)} %get-tuple-element.38.refs_0_, s32[1]{0:T(128)} %bitcast.refs_0_.refs_1_, bf16[144,640]{1,0:T(8,128)(2,1)S(1)} %get-tuple-element.52.refs_2_, bf16[144,640]{1,0:T(8,128)(2,1)S(1)} %collective-permute-done.1.refs_3_.refs_7_, ...), custom_call_target="tpu_custom_call" | custom-call | flops 327680 | bytes 925696 | tf_op jit(solution)/shard_map/pallas_call | solution.py:432
  24.2 2.6 %collective-permute-start.10 = (bf16[128,640]{1,0:T(8,128)(2,1)S(1)}, bf16[128,640]{1,0:T(8,128)(2,1)S(1)}, u32[]{:S(2)}, u32[]{:S(2)}) collective-permute-start(bf16[128,640]{1,0:T(8,128)(2,1)S(1)} %get-tuple-element.58.refs_9_), channel_id=1, source_target_pairs={{0,16},{4,20},{8,24},{12,28},{16,0},{20,4},{24,8},{28,12},{1,17},{... | collective-permute-start | bytes 491528 | tf_op jit(solution)/shard_map/ppermute | solution.py:478
  26.8 2.3 %shard_map.97.refs_9_.refs_2_ = f32[256,640]{1,0:T(8,128)S(1)} custom-call(s32[3]{0:T(128)S(1)} %get-tuple-element.38.refs_0_, s32[1]{0:T(128)} %bitcast.refs_0_.refs_1_, bf16[256,2560]{1,0:T(8,128)(2,1)S(1)} %get-tuple-element.39.refs_2_, bf16[16,2560]{1,0:T(8,128)(2,1)S(1)} %get-tuple-element.45.refs_3_, f32[256,256]{1,0:T(8,128)S(1)} %get-tuple-element.48.refs_4_, ...), custom_call_target="tpu_custom_call" | custom-call | flops 83886080 | bytes 2850976 | tf_op jit(solution)/shard_map/pallas_call | solution.py:432
  29.1 0.7 %shard_map.98 = (bf16[128,640]{1,0:T(8,128)(2,1)S(1)}, bf16[128,640]{1,0:T(8,128)(2,1)S(1)}, bf16[128,640]{1,0:T(8,128)(2,1)S(1)}, bf16[128,640]{1,0:T(8,128)(2,1)S(1)}) custom-call(s32[3]{0:T(128)S(1)} %get-tuple-element.38.refs_0_, s32[1]{0:T(128)} %bitcast.refs_0_.refs_1_, bf16[144,640]{1,0:T(8,128)(2,1)S(1)} %get-tuple-element.52.refs_2_, ...), custom_call_target="tpu_custom_call" | custom-call | flops 327680 | bytes 1781760 | tf_op jit(solution)/shard_map/pallas_call | solution.py:432
  29.8 1.6 %collective-permute-start.4 = (bf16[128,640]{1,0:T(8,128)(2,1)S(1)}, bf16[128,640]{1,0:T(8,128)(2,1)S(1)}, u32[]{:S(2)}, u32[]{:S(2)}) collective-permute-start(bf16[128,640]{1,0:T(8,128)(2,1)S(1)} %get-tuple-element.61), channel_id=1, source_target_pairs={{0,4},{4,0},{8,12},{12,8},{16,20},{20,16},{24,28},{28,24},{1,5},{5... | collective-permute-start | bytes 491528 | tf_op jit(solution)/shard_map/ppermute | solution.py:478
  31.4 0.5 collective-permute-start.6
  31.9 1.6 %collective-permute-start.7 = (bf16[128,640]{1,0:T(8,128)(2,1)S(1)}, bf16[128,640]{1,0:T(8,128)(2,1)S(1)}, u32[]{:S(2)}, u32[]{:S(2)}) collective-permute-start(bf16[128,640]{1,0:T(8,128)(2,1)S(1)} %get-tuple-element.59.refs_8_.refs_9_), channel_id=1, source_target_pairs={{0,8},{4,12},{8,0},{12,4},{16,24},{20,28},{24,16},{28,20},{1,9},{5... | collective-permute-start | bytes 491528 | tf_op jit(solution)/shard_map/ppermute | solution.py:478
  33.9 1.7 %collective-permute-start.8 = (bf16[128,640]{1,0:T(8,128)(2,1)S(1)}, bf16[128,640]{1,0:T(8,128)(2,1)S(1)}, u32[]{:S(2)}, u32[]{:S(2)}) collective-permute-start(bf16[128,640]{1,0:T(8,128)(2,1)S(1)} %get-tuple-element.65), channel_id=1, source_target_pairs={{0,4},{4,0},{8,12},{12,8},{16,20},{20,16},{24,28},{28,24},{1,5},{5... | collective-permute-start | bytes 491528 | tf_op jit(solution)/shard_map/ppermute | solution.py:478
  35.5 1.8 %collective-permute-done.4.refs_7_ = bf16[128,640]{1,0:T(8,128)(2,1)S(1)} collective-permute-done((bf16[128,640]{1,0:T(8,128)(2,1)S(1)}, bf16[128,640]{1,0:T(8,128)(2,1)S(1)}, u32[]{:S(2)}, u32[]{:S(2)}) %collective-permute-start.4) | collective-permute-done | bytes 163872 | tf_op jit(solution)/shard_map/ppermute | solution.py:478
  37.3 2.3 %collective-permute-start.9 = (bf16[128,640]{1,0:T(8,128)(2,1)S(1)}, bf16[128,640]{1,0:T(8,128)(2,1)S(1)}, u32[]{:S(2)}, u32[]{:S(2)}) collective-permute-start(bf16[128,640]{1,0:T(8,128)(2,1)S(1)} %get-tuple-element.59.refs_8_.refs_9_), channel_id=1, source_target_pairs={{0,12},{4,8},{8,4},{12,0},{16,28},{20,24},{24,20},{28,16},{1,13},{... | collective-permute-start | bytes 491528 | tf_op jit(solution)/shard_map/ppermute | solution.py:478
  39.6 6.3 %collective-permute-done.6.refs_7_ = bf16[128,640]{1,0:T(8,128)(2,1)S(1)} collective-permute-done((bf16[128,640]{1,0:T(8,128)(2,1)S(1)}, bf16[128,640]{1,0:T(8,128)(2,1)S(1)}, u32[]{:S(2)}, u32[]{:S(2)}) %collective-permute-start.6) | collective-permute-done | bytes 163872 | tf_op jit(solution)/shard_map/ppermute | solution.py:478
  45.8 1.4 %collective-permute-start.13 = (bf16[128,640]{1,0:T(8,128)(2,1)S(1)}, bf16[128,640]{1,0:T(8,128)(2,1)S(1)}, u32[]{:S(2)}, u32[]{:S(2)}) collective-permute-start(bf16[128,640]{1,0:T(8,128)(2,1)S(1)} %collective-permute-done.10.refs_11_), channel_id=1, source_target_pairs={{0,12},{4,8},{8,4},{12,0},{16,28},{20,24},{24,20},{28,16},{1,13},{... | collective-permute-start | bytes 491528 | tf_op jit(solution)/shard_map/ppermute | solution.py:478
  47.2 1.6 %collective-permute-start.12 = (bf16[128,640]{1,0:T(8,128)(2,1)S(1)}, bf16[128,640]{1,0:T(8,128)(2,1)S(1)}, u32[]{:S(2)}, u32[]{:S(2)}) collective-permute-start(bf16[128,640]{1,0:T(8,128)(2,1)S(1)} %collective-permute-done.10.refs_11_), channel_id=1, source_target_pairs={{0,8},{4,12},{8,0},{12,4},{16,24},{20,28},{24,16},{28,20},{1,9},{5... | collective-permute-start | bytes 491528 | tf_op jit(solution)/shard_map/ppermute | solution.py:478
  48.8 0.5 collective-permute-done.5.refs_8_
  49.3 1.5 %collective-permute-start.11 = (bf16[128,640]{1,0:T(8,128)(2,1)S(1)}, bf16[128,640]{1,0:T(8,128)(2,1)S(1)}, u32[]{:S(2)}, u32[]{:S(2)}) collective-permute-start(bf16[128,640]{1,0:T(8,128)(2,1)S(1)} %collective-permute-done.10.refs_11_), channel_id=1, source_target_pairs={{0,4},{4,0},{8,12},{12,8},{16,20},{20,16},{24,28},{28,24},{1,5},{5... | collective-permute-start | bytes 491528 | tf_op jit(solution)/shard_map/ppermute | solution.py:478
  50.9 2.3 %shard_map.102.refs_2_ = f32[256,640]{1,0:T(8,128)S(1)} custom-call(s32[3]{0:T(128)S(1)} %get-tuple-element.38.refs_0_, s32[1]{0:T(128)} %bitcast.refs_0_.refs_1_, bf16[256,2560]{1,0:T(8,128)(2,1)S(1)} %get-tuple-element.39.refs_2_, bf16[16,2560]{1,0:T(8,128)(2,1)S(1)} %get-tuple-element.45.refs_3_, f32[256,256]{1,0:T(8,128)S(1)} %get-tuple-element.48.refs_4_, ...), custom_call_target="tpu_custom_call" | custom-call | flops 83886080 | bytes 2850976 | tf_op jit(solution)/shard_map/pallas_call | solution.py:432
  53.3 1.6 %shard_map.99 = (f32[256,640]{1,0:T(8,128)S(1)}, f32[256,640]{1,0:T(8,128)S(1)}) custom-call(s32[3]{0:T(128)S(1)} %get-tuple-element.38.refs_0_, s32[1]{0:T(128)} %bitcast.refs_0_.refs_1_, f32[256,640]{1,0:T(8,128)S(1)} %shard_map.94.refs_6_.refs_2_, bf16[256,128]{1,0:T(8,128)(2,1)S(1)} %get-tuple-element.50.refs_3_.refs_10_, ...), custom_call_target="tpu_custom_call" | custom-call | flops 83886080 | bytes 3858432 | tf_op jit(solution)/shard_map/pallas_call | solution.py:432
  54.9 1.8 %shard_map.100 = (f32[256,640]{1,0:T(8,128)S(1)}, f32[256,640]{1,0:T(8,128)S(1)}) custom-call(s32[3]{0:T(128)S(1)} %get-tuple-element.38.refs_0_, s32[1]{0:T(128)} %bitcast.refs_0_.refs_1_, f32[256,640]{1,0:T(8,128)S(1)} %shard_map.95.refs_7_.refs_2_, bf16[256,128]{1,0:T(8,128)(2,1)S(1)} %get-tuple-element.50.refs_3_.refs_10_, ...), custom_call_target="tpu_custom_call" | custom-call | flops 83886080 | bytes 3837952 | tf_op jit(solution)/shard_map/pallas_call | solution.py:432
  56.7 1.6 %shard_map.101 = (f32[256,640]{1,0:T(8,128)S(1)}, f32[256,640]{1,0:T(8,128)S(1)}) custom-call(s32[3]{0:T(128)S(1)} %get-tuple-element.38.refs_0_, s32[1]{0:T(128)} %bitcast.refs_0_.refs_1_, f32[256,640]{1,0:T(8,128)S(1)} %shard_map.97.refs_9_.refs_2_, bf16[256,128]{1,0:T(8,128)(2,1)S(1)} %get-tuple-element.50.refs_3_.refs_10_, ...), custom_call_target="tpu_custom_call" | custom-call | flops 83886080 | bytes 3837952 | tf_op jit(solution)/shard_map/pallas_call | solution.py:432
  58.4 1.6 %shard_map.103 = (f32[256,640]{1,0:T(8,128)S(1)}, f32[256,640]{1,0:T(8,128)S(1)}) custom-call(s32[3]{0:T(128)S(1)} %get-tuple-element.38.refs_0_, s32[1]{0:T(128)} %bitcast.refs_0_.refs_1_, f32[256,640]{1,0:T(8,128)S(1)} %shard_map.102.refs_2_, bf16[256,128]{1,0:T(8,128)(2,1)S(1)} %get-tuple-element.50.refs_3_.refs_10_, f32[3,40,256]{2,1,0:T(8,128)S(1)} %slice.16.refs_4_, ...), custom_call_target="tpu_custom_call" | custom-call | flops 83886080 | bytes 3837952 | tf_op jit(solution)/shard_map/pallas_call | solution.py:432
  60.0 3.1 %shard_map.104 = bf16[256,2560]{1,0:T(8,128)(2,1)} custom-call(s32[3]{0:T(128)S(1)} %get-tuple-element.38.refs_0_, s32[1]{0:T(128)} %bitcast.refs_0_.refs_1_, f32[256,640]{1,0:T(8,128)S(1)} %get-tuple-element.60.refs_2_, f32[256,640]{1,0:T(8,128)S(1)} %get-tuple-element.62.refs_3_, f32[256,640]{1,0:T(8,128)S(1)} %get-tuple-element.64.refs_4_, ...), custom_call_target="tpu_custom_call" | custom-call | flops 167772160 | bytes 7284736 | tf_op jit(solution)/shard_map/pallas_call | solution.py:432
  (23 shorter events, 1.0 us)
Async XLA Ops:
  0.9 10.0 %collective-permute-start = (bf16[16,2816]{1,0:T(8,128)(2,1)S(1)}, bf16[16,2816]{1,0:T(8,128)(2,1)S(1)}, u32[]{:S(2)}, u32[]{:S(2)}) collective-permute-start(bf16[16,2816]{1,0:T(8,128)(2,1)S(1)} %slice.12), channel_id=1, source_target_pairs={{0,4},{4,8},{8,12},{12,16},{16,20},{20,24},{24,28},{1,5},{5,9},{9,... | collective-permute-start | bytes 270344 | tf_op jit(solution)/shard_map/ppermute | solution.py:478
  10.9 4.6 %copy-start.2 = (f32[40,20,256]{2,0,1:T(8,128)S(1)}, f32[40,20,256]{2,0,1:T(8,128)}, u32[]{:S(2)}) copy-start(f32[40,20,256]{2,0,1:T(8,128)} %param.14) | copy-start | bytes 2457604
  10.9 5.4 %copy-start.1 = (f32[40]{0:T(128)S(1)}, f32[40]{0:T(128)}, u32[]{:S(2)}) copy-start(f32[40]{0:T(128)} %refs_8_.7) | copy-start | bytes 484
  12.0 9.0 %collective-permute-start.1 = (bf16[144,640]{1,0:T(8,128)(2,1)S(1)}, bf16[144,640]{1,0:T(8,128)(2,1)S(1)}, u32[]{:S(2)}, u32[]{:S(2)}) collective-permute-start(bf16[144,640]{1,0:T(8,128)(2,1)S(1)} %get-tuple-element.53), channel_id=1, source_target_pairs={{0,4},{4,0},{8,12},{12,8},{16,20},{20,16},{24,28},{28,24},{1,5},{5... | collective-permute-start | bytes 552968 | tf_op jit(solution)/shard_map/ppermute | solution.py:478
  13.6 7.6 %collective-permute-start.2 = (bf16[144,640]{1,0:T(8,128)(2,1)S(1)}, bf16[144,640]{1,0:T(8,128)(2,1)S(1)}, u32[]{:S(2)}, u32[]{:S(2)}) collective-permute-start(bf16[144,640]{1,0:T(8,128)(2,1)S(1)} %get-tuple-element.54.refs_7_), channel_id=1, source_target_pairs={{0,8},{4,12},{8,0},{12,4},{16,24},{20,28},{24,16},{28,20},{1,9},{5... | collective-permute-start | bytes 552968 | tf_op jit(solution)/shard_map/ppermute | solution.py:478
  15.2 8.1 %collective-permute-start.3 = (bf16[144,640]{1,0:T(8,128)(2,1)S(1)}, bf16[144,640]{1,0:T(8,128)(2,1)S(1)}, u32[]{:S(2)}, u32[]{:S(2)}) collective-permute-start(bf16[144,640]{1,0:T(8,128)(2,1)S(1)} %get-tuple-element.55.refs_8_), channel_id=1, source_target_pairs={{0,12},{4,8},{8,4},{12,0},{16,28},{20,24},{24,20},{28,16},{1,13},{... | collective-permute-start | bytes 552968 | tf_op jit(solution)/shard_map/ppermute | solution.py:478
  24.2 9.7 %collective-permute-start.10 = (bf16[128,640]{1,0:T(8,128)(2,1)S(1)}, bf16[128,640]{1,0:T(8,128)(2,1)S(1)}, u32[]{:S(2)}, u32[]{:S(2)}) collective-permute-start(bf16[128,640]{1,0:T(8,128)(2,1)S(1)} %get-tuple-element.58.refs_9_), channel_id=1, source_target_pairs={{0,16},{4,20},{8,24},{12,28},{16,0},{20,4},{24,8},{28,12},{1,17},{... | collective-permute-start | bytes 491528 | tf_op jit(solution)/shard_map/ppermute | solution.py:478
  29.1 21.8 %copy-start.3 = (f32[2560]{0:T(1024)S(1)}, f32[2560]{0:T(1024)}, u32[]{:S(2)}) copy-start(f32[2560]{0:T(1024)} %param.16) | copy-start | bytes 30724
  29.8 7.5 %collective-permute-start.4 = (bf16[128,640]{1,0:T(8,128)(2,1)S(1)}, bf16[128,640]{1,0:T(8,128)(2,1)S(1)}, u32[]{:S(2)}, u32[]{:S(2)}) collective-permute-start(bf16[128,640]{1,0:T(8,128)(2,1)S(1)} %get-tuple-element.61), channel_id=1, source_target_pairs={{0,4},{4,0},{8,12},{12,8},{16,20},{20,16},{24,28},{28,24},{1,5},{5... | collective-permute-start | bytes 491528 | tf_op jit(solution)/shard_map/ppermute | solution.py:478
  31.4 14.4 %collective-permute-start.6 = (bf16[128,640]{1,0:T(8,128)(2,1)S(1)}, bf16[128,640]{1,0:T(8,128)(2,1)S(1)}, u32[]{:S(2)}, u32[]{:S(2)}) collective-permute-start(bf16[128,640]{1,0:T(8,128)(2,1)S(1)} %get-tuple-element.63), channel_id=1, source_target_pairs={{0,4},{4,0},{8,12},{12,8},{16,20},{20,16},{24,28},{28,24},{1,5},{5... | collective-permute-start | bytes 491528 | tf_op jit(solution)/shard_map/ppermute | solution.py:478
  31.9 15.3 %collective-permute-start.7 = (bf16[128,640]{1,0:T(8,128)(2,1)S(1)}, bf16[128,640]{1,0:T(8,128)(2,1)S(1)}, u32[]{:S(2)}, u32[]{:S(2)}) collective-permute-start(bf16[128,640]{1,0:T(8,128)(2,1)S(1)} %get-tuple-element.59.refs_8_.refs_9_), channel_id=1, source_target_pairs={{0,8},{4,12},{8,0},{12,4},{16,24},{20,28},{24,16},{28,20},{1,9},{5... | collective-permute-start | bytes 491528 | tf_op jit(solution)/shard_map/ppermute | solution.py:478
  33.5 15.8 %collective-permute-start.5 = (bf16[128,640]{1,0:T(8,128)(2,1)S(1)}, bf16[128,640]{1,0:T(8,128)(2,1)S(1)}, u32[]{:S(2)}, u32[]{:S(2)}) collective-permute-start(bf16[128,640]{1,0:T(8,128)(2,1)S(1)} %get-tuple-element.59.refs_8_.refs_9_), channel_id=1, source_target_pairs={{0,4},{4,0},{8,12},{12,8},{16,20},{20,16},{24,28},{28,24},{1,5},{5... | collective-permute-start | bytes 491528 | tf_op jit(solution)/shard_map/ppermute | solution.py:478
  33.9 24.5 %collective-permute-start.8 = (bf16[128,640]{1,0:T(8,128)(2,1)S(1)}, bf16[128,640]{1,0:T(8,128)(2,1)S(1)}, u32[]{:S(2)}, u32[]{:S(2)}) collective-permute-start(bf16[128,640]{1,0:T(8,128)(2,1)S(1)} %get-tuple-element.65), channel_id=1, source_target_pairs={{0,4},{4,0},{8,12},{12,8},{16,20},{20,16},{24,28},{28,24},{1,5},{5... | collective-permute-start | bytes 491528 | tf_op jit(solution)/shard_map/ppermute | solution.py:478
  37.3 21.0 %collective-permute-start.9 = (bf16[128,640]{1,0:T(8,128)(2,1)S(1)}, bf16[128,640]{1,0:T(8,128)(2,1)S(1)}, u32[]{:S(2)}, u32[]{:S(2)}) collective-permute-start(bf16[128,640]{1,0:T(8,128)(2,1)S(1)} %get-tuple-element.59.refs_8_.refs_9_), channel_id=1, source_target_pairs={{0,12},{4,8},{8,4},{12,0},{16,28},{20,24},{24,20},{28,16},{1,13},{... | collective-permute-start | bytes 491528 | tf_op jit(solution)/shard_map/ppermute | solution.py:478
  45.8 14.2 %collective-permute-start.13 = (bf16[128,640]{1,0:T(8,128)(2,1)S(1)}, bf16[128,640]{1,0:T(8,128)(2,1)S(1)}, u32[]{:S(2)}, u32[]{:S(2)}) collective-permute-start(bf16[128,640]{1,0:T(8,128)(2,1)S(1)} %collective-permute-done.10.refs_11_), channel_id=1, source_target_pairs={{0,12},{4,8},{8,4},{12,0},{16,28},{20,24},{24,20},{28,16},{1,13},{... | collective-permute-start | bytes 491528 | tf_op jit(solution)/shard_map/ppermute | solution.py:478
  47.2 12.8 %collective-permute-start.12 = (bf16[128,640]{1,0:T(8,128)(2,1)S(1)}, bf16[128,640]{1,0:T(8,128)(2,1)S(1)}, u32[]{:S(2)}, u32[]{:S(2)}) collective-permute-start(bf16[128,640]{1,0:T(8,128)(2,1)S(1)} %collective-permute-done.10.refs_11_), channel_id=1, source_target_pairs={{0,8},{4,12},{8,0},{12,4},{16,24},{20,28},{24,16},{28,20},{1,9},{5... | collective-permute-start | bytes 491528 | tf_op jit(solution)/shard_map/ppermute | solution.py:478
  49.3 10.7 %collective-permute-start.11 = (bf16[128,640]{1,0:T(8,128)(2,1)S(1)}, bf16[128,640]{1,0:T(8,128)(2,1)S(1)}, u32[]{:S(2)}, u32[]{:S(2)}) collective-permute-start(bf16[128,640]{1,0:T(8,128)(2,1)S(1)} %collective-permute-done.10.refs_11_), channel_id=1, source_target_pairs={{0,4},{4,0},{8,12},{12,8},{16,20},{20,16},{24,28},{28,24},{1,5},{5... | collective-permute-start | bytes 491528 | tf_op jit(solution)/shard_map/ppermute | solution.py:478
  50.9 2.3 %copy-start = (bf16[256,2560]{1,0:T(8,128)(2,1)S(1)}, bf16[256,2560]{1,0:T(8,128)(2,1)}, u32[]{:S(2)}) copy-start(bf16[256,2560]{1,0:T(8,128)(2,1)} %refs_9_.7) | copy-start | bytes 3932164

commit v3 on v2

--- a/solution.py
+++ b/solution.py
@@ -87,7 +87,7 @@
                 (decay_hbm, decay_ref),
                 (x_hbm, x_ref),
                 (w_hbm, weight_ref.at[:taps]),
-                (b_hbm, weight_ref.at[taps : taps + 1]),
+                (b_hbm, weight_ref.at[taps]),
             )
         )
     ]
@@ -250,29 +250,36 @@
 
 
 def pair_kernel(
-    dims, lengths, group, own_ref, one_ref, two_ref, three_ref, weight_ref, two_in, three_in,
-    pair_ref, own_out, two_out, three_out,
+    dims, lengths, group, own_ref, one_ref, two_ref, three_ref, weight_ref, two_in,
+    pair_ref, beside_ref, across_ref,
 ):
     (state,) = dims
     cols = pair_ref.shape[1]
+    beside_ref[:state] = own_ref[:state]
+    beside_ref[state : 2 * state] = two_in[:state]
+    across_ref[state:] = three_ref[:state]
     for lo in range(0, cols, LANES):
         hi = lo + LANES
         pair = jnp.zeros((state, LANES), f32)
         for mask, ref in enumerate((own_ref, one_ref, two_ref, three_ref)):
             weight = weight_ref[PLACES + mask : PLACES + mask + 1, lo:hi]
             pair = pair + ref[:state, lo:hi].astype(f32) * weight
-        pair_ref[:, lo:hi] = pair.astype(bf16)
-    own_out[...] = own_ref[:state]
-    two_out[...] = two_in[:state]
-    three_out[...] = three_in[:state]
+        pair = pair.astype(bf16)
+        pair_ref[:, lo:hi] = pair
+        across_ref[:state, lo:hi] = pair
+        beside_ref[2 * state :, lo:hi] = pair
 
 
 def with_head(patch, body):
     return jnp.concatenate([patch, body[HALO:]], axis=0)
 
 
-def scores_kernel(dims, lengths, group, kq_ref, pkq_ref, queries_ref, scores_ref):
-    tok, recordings, state = dims
+def shared_kernel(
+    dims, lengths, group, kq_ref, pkq_ref, cumt_ref, level_ref, entry_ref,
+    queries_ref, scores_ref, parts_ref, coef_ref,
+):
+    tok, recordings, state, far_from = dims
+    heads = entry_ref.shape[0]
     bounds = segment_bounds(lengths, recordings)
     first = group[0] * tok
     kq = with_head(pkq_ref[...], kq_ref[...])
@@ -281,11 +288,18 @@
     t_pos = iota((tok, tok), 1)
     valid = same_segment(first + s_pos, first + t_pos, bounds) * jnp.where(s_pos <= t_pos, 1.0, 0.0)
     scores_ref[...] = dot(kq[:, :state], kq[:, state:], ((1,), (1,))) * valid
+    high, rest = two_parts(cumt_ref[...])
+    mid, low = two_parts(rest)
+    parts_ref[...] = jnp.concatenate([high, mid, low], axis=1).astype(bf16)
+    for bit in range(coef_ref.shape[0]):
+        coef = level_ref[far_from + bit] * entry_ref[...]
+        coef = jnp.concatenate([coef, jnp.zeros((LANES - heads, tok), f32)], axis=0)
+        coef_ref[bit] = jnp.transpose(coef)
 
 
 def local_kernel(
-    dims, mask, lengths, group, xs_ref, px_ref, scores_ref, cum_ref, cumt_ref, level_ref, skip_ref,
-    out_ref, mixing_ref,
+    dims, mask, lengths, group, xs_ref, px_ref, scores_ref, cum_ref, parts_ref, level_ref, skip_ref,
+    out_ref, mixing_ref, copied_ref,
 ):
     tok, head_dim, low_bits = dims
     cols = out_ref.shape[1]
@@ -295,20 +309,23 @@
     rows = 32
     row_bits = rows.bit_length() - 1
     where = pl.multiple_of(quarter * cols, LANES)
-    cumt = pltpu.roll(cumt_ref[...], LANES - first_head, 1)
+    copies = spread(LANES, first_head, count * LANES, LANES)
+    copied_ref[...] = dot(parts_ref[...], jnp.concatenate([copies] * 3, axis=0), ((1,), (0,)))
     diff = jnp.bitwise_xor(iota((rows, tok), 0), lax.rem(iota((rows, tok), 1), rows))
     near = jnp.zeros((rows, tok), jnp.int32)
     for bit in range(row_bits):
         near = near + (diff >= 2**bit).astype(jnp.int32)
     token = iota((1, tok), 1) // rows
     lane = iota((1, 2 * head_dim), 1)
+    unit = jnp.where(iota((tok, tok), 0) == iota((tok, tok), 1), 1.0, 0.0).astype(bf16)
+    mixing_ref[...] = jnp.zeros(mixing_ref.shape, bf16)
     pieces = []
     for head in range(count):
         if head % 2 == 0:
             lo = head * head_dim
             here = pl.ds(pl.multiple_of(where + lo, LANES), 2 * head_dim)
-            xs = with_head(px_ref[:, here], xs_ref[:, here]).astype(f32)
-            xst = jnp.transpose(xs).astype(bf16)
+            xs = with_head(px_ref[:, here], xs_ref[:, here])
+            xst = jnp.transpose(xs)
         cum = cum_ref[pl.ds(first_head + head, 1), :]
         levels = [level_ref[level, pl.ds(first_head + head, 1), :] for level in range(low_bits + 1)]
         inner = jnp.broadcast_to(levels[0], (rows, tok))
@@ -316,19 +333,21 @@
             inner = jnp.where(near == level, levels[level], inner)
         for s in range(0, tok, rows):
             at = s // rows
-            start = s // LANES * LANES
             outer = jnp.zeros((1, tok), f32)
             apart = jnp.bitwise_xor(token, at)
             for level in range(row_bits + 1, low_bits + 1):
                 outer = jnp.where(apart >= 2 ** (level - row_bits - 1), levels[level], outer)
-            picked = jnp.where(token == at, inner, outer)[:, start:]
-            gap = cum[:, start:] - cumt[s : s + rows, head : head + 1]
-            value = jnp.exp(jnp.minimum(gap, 0.0)) * picked
-            mixing_ref[head % 2, s : s + rows, start:] = (
-                value * scores_ref[s : s + rows, start:]
-            ).astype(bf16)
-            if start:
-                mixing_ref[head % 2, s : s + rows, :start] = jnp.zeros((rows, start), bf16)
+            before = copied_ref[s : s + rows, head * LANES : (head + 1) * LANES]
+            for t in range(s // LANES * LANES, tok, LANES):
+                here_t = slice(t, t + LANES)
+                picked = outer[:, here_t]
+                gap = cum[:, here_t] - before
+                if t <= s:
+                    picked = jnp.where(token[:, here_t] == at, inner[:, here_t], picked)
+                    gap = jnp.minimum(gap, 0.0)
+                mixing_ref[head % 2, s : s + rows, here_t] = (
+                    jnp.exp(gap) * picked * scores_ref[s : s + rows, here_t]
+                ).astype(bf16)
         pieces.append(
             dot(
                 xst[head % 2 * head_dim : (head % 2 + 1) * head_dim],
@@ -337,45 +356,40 @@
             )
         )
         if head % 2 == 1:
-            both = jnp.transpose(jnp.concatenate(pieces[-2:], axis=0))
+            both = jnp.concatenate(pieces[-2:], axis=0)
             skip = jnp.where(
                 lane < head_dim, skip_ref[first_head + head - 1], skip_ref[first_head + head]
             )
-            out_ref[:, lo : lo + 2 * head_dim] = both + skip * xs
-
-
-def spread_rows(coef, copies):
-    high, low = two_parts(coef)
-    return dot(high.astype(bf16), copies, ((0,), (0,))) + dot(
-        low.astype(bf16), copies, ((0,), (0,))
-    )
+            out_ref[:, lo : lo + 2 * head_dim] = jnp.transpose(both) + skip * xs.astype(f32)
 
 
 def far_kernel(
-    dims, mask, lengths, group, sum_ref, queries_ref, level_ref, entry_ref, scale_ref, low_ref,
+    dims, mask, lengths, group, sum_ref, queries_ref, coef_ref, scale_ref, low_ref,
     pair_ref, gate_ref, out_ref, next_ref,
 ):
-    head_dim, state = dims
-    cols = sum_ref.shape[1]
-    heads = entry_ref.shape[0]
+    head_dim, state, low_from, pair_from = dims
+    tok, cols = sum_ref.shape
     quarter = jnp.bitwise_xor(lax.rem(group[0], PLACES), mask)
     first = quarter * (cols // head_dim)
     queries = queries_ref[...]
-    copies = spread(heads, first, cols, head_dim)
-    scale = jnp.transpose(scale_ref[...])
-    entry = entry_ref[...]
-    factors = []
-    for bit in range(3):
+    coefs = []
+    for bit in range(coef_ref.shape[0]):
         on = jnp.where(lax.rem(group[0] // 2**bit, 2) == 1, 1.0, 0.0)
-        coef = level_ref[bit] * entry * (scale[:heads, bit : bit + 1] * on)
-        factors.append(spread_rows(coef, copies))
+        coef = two_parts(coef_ref[bit] * (scale_ref[bit : bit + 1, :] * on))
+        coefs.append(jnp.concatenate(coef, axis=1).astype(bf16))
+    copies = spread(LANES, first, cols, head_dim)
+    factors = dot(
+        jnp.concatenate(coefs, axis=0), jnp.concatenate([copies, copies], axis=0), ((1,), (0,))
+    )
     total = sum_ref[...]
-    for bit, ref in enumerate((low_ref, pair_ref)):
-        total = total + dot(queries, ref[:state, :], ((1,), (0,))) * factors[bit]
+    for bit, state_in in enumerate(
+        (low_ref[low_from : low_from + state], pair_ref[pair_from : pair_from + state])
+    ):
+        total = total + dot(queries, state_in, ((1,), (0,))) * factors[bit * tok : (bit + 1) * tok]
     where = pl.multiple_of(quarter * cols, LANES)
     gate = silu(gate_ref[:, pl.ds(where, cols)].astype(f32))
     out_ref[...] = total * gate
-    next_ref[...] = factors[2] * gate
+    next_ref[...] = factors[2 * tok :] * gate
 
 
 def final_kernel(dims, lengths, group, *refs):
@@ -477,8 +491,8 @@
     def send(value, pairs):
         return lax.ppermute(value, "group", pairs)
 
-    def quad_send(value, mask, wanted=lambda target: True):
-        pairs = [(g, g ^ mask) for g in range(groups)]
+    def quad_send(value, mask, wanted=lambda source, target: True):
+        pairs = [(g, g ^ mask) for g in range(groups) if wanted(g, g ^ mask)]
         return send(value, pairs)
 
     halo = send(mixed_input[tok - HALO :], [(g, g + 1) for g in range(groups - 1)])
@@ -494,7 +508,7 @@
         (
             in_hbm(mixed_input),
             in_hbm(conv_weight),
-            in_hbm(conv_bias[None, :]),
+            in_hbm(conv_bias),
             in_hbm(log_decay),
             in_hbm(seg_lengths),
         ),
@@ -533,11 +547,16 @@
         flops=2 * HALO * width * state,
     )
 
-    queries, scores = call(
-        functools.partial(scores_kernel, (tok, recordings, state)),
+    queries, scores, parts, coefs = call(
+        functools.partial(shared_kernel, (tok, recordings, state, low_bits + 1)),
         scalars,
-        (kq, pkq),
-        [shape((tok, state), bf16), shape((tok, tok), f32)],
+        (kq, pkq, cumt, levels, entry),
+        [
+            shape((tok, state), bf16),
+            shape((tok, tok), f32),
+            shape((tok, 3 * LANES), bf16),
+            shape((3, tok, LANES), f32),
+        ],
         flops=2 * tok * tok * state,
     )
 
@@ -545,9 +564,9 @@
         return call(
             functools.partial(local_kernel, (tok, head_dim, low_bits), mask),
             scalars,
-            (xs, px, scores, cum, cumt, levels[: low_bits + 1], skip_gain),
+            (xs, px, scores, cum, parts, levels, skip_gain),
             [shape((tok, cols), f32)],
-            [pltpu.VMEM((2, tok, tok), bf16)],
+            [pltpu.VMEM((2, tok, tok), bf16), pltpu.VMEM((tok, cols // head_dim * LANES), f32)],
             specs=[VMEM] * 6 + [SMEM],
             flops=2 * cols * tok * tok,
             after=after,
@@ -566,16 +585,23 @@
         flops=4 * state * cols,
         after=sums,
     )
-    sums.append(local(2, (quad,)))
-    pair, own_state, two_state, three_state = call(
+    pair, beside, across = call(
         functools.partial(pair_kernel, (state,)),
         scalars,
-        received + (spread_weights, two, three),
-        [shape((state, cols), bf16)] * 4,
+        received + (spread_weights, two),
+        [
+            shape((state, cols), bf16),
+            shape((3 * state, cols), bf16),
+            shape((2 * state, cols), bf16),
+        ],
         flops=4 * state * cols,
-        after=sums[2:],
-    )
-    sums.append(local(3, (pair,)))
+        after=(quad,),
+    )
+    sums.append(local(2, (quad,)))
+    sums.append(local(3, ()))
+    got_three_of_pair = quad_send(pair, 3, lambda source, target: target & 2)
+    got_beside = quad_send(beside, 1)
+    got_across = quad_send(across, 2)
 
     befores = [scale[0, :heads], scale[1, :heads], scale[2, :heads]]
     crossed = []
@@ -583,8 +609,8 @@
     for bit in range(2, high_bits):
         mask = 2**bit
         last = bit + 1 == high_bits
-        far = quad_send(running, mask, lambda target: not last or target & mask)
-        crossed.append(far)
+        far = quad_send(running, mask, lambda source, target: True)
+        crossed.append(lax.optimization_barrier((far, sums[3], sums[2]))[0])
         if not last:
             on_top = group // mask % 2 == 1
             far_total = quad_send(total, mask)
@@ -601,30 +627,21 @@
             befores.append(jnp.where(on_top, far_total * befores[-1], befores[-1]))
             total = total * far_total
 
-    odd = lambda target: target & 1
-    lows = [
-        got_one,
-        quad_send(own_state, 1, odd),
-        quad_send(three_state, 1, odd),
-        quad_send(two_state, 1, odd),
-    ]
-    pairs = [pair] + [
-        quad_send(pair, mask, lambda target: target & 2) for mask in range(1, PLACES)
-    ]
+    lows = [(got_one, 0), (got_beside, 0), (got_across, state), (got_beside, state)]
+    pairs = [(pair, 0), (got_beside, 2 * state), (got_across, 0), (got_three_of_pair, 0)]
 
     def all_quarters(value, bit):
         return [value] + [
-            quad_send(value, mask, lambda target: target & 2**bit)
+            quad_send(value, mask)
             for mask in range(1, PLACES)
         ]
 
-    far_levels = levels[low_bits + 1 : low_bits + 4]
     halves = [
         list(
             call(
-                functools.partial(far_kernel, (head_dim, state), mask),
+                functools.partial(far_kernel, (head_dim, state, lows[mask][1], pairs[mask][1]), mask),
                 scalars,
-                (sums[mask], queries, far_levels, entry, scale, lows[mask], pairs[mask], gate_input),
+                (sums[mask], queries, coefs, scale, lows[mask][0], pairs[mask][0], gate_input),
                 [shape((tok, cols), f32), shape((tok, cols), f32)],
                 flops=4 * tok * cols * state,
             )
@@ -643,7 +660,7 @@
             read = read * jnp.repeat(mine, head_dim, axis=0).T
             halves[mask][0] = halves[mask][0] + read * jax.nn.silu(gate.astype(f32))
 
-    rows = 64
+    rows = 128
     return call(
         functools.partial(final_kernel, (float(width), rows)),
         scalars,

time: 63.3 us -> 49.8 us (0.79)
  waiting for transfers between devices: 10.9 us -> 6.34 us
  Pallas kernels: 26.2 us -> 21.8 us
  starting transfers between devices: 23.5 us -> 20.3 us
  local copies, waits for them, and re-layouts: 2.28 us -> 0.93 us
    ppermute x14 -> x11, waiting for transfers between devices: 10.9 us -> 6.34 us  [send(): return lax.ppermute(value, 'group', pairs)]
    pallas_call x14, Pallas kernels: 26.2 us -> 21.8 us  [call(): pl.pallas_call(body, grid=grid, in_specs=[SMEM] * len(scalars) + specs +...]
    ppermute x14 -> x11, starting transfers between devices: 23.5 us -> 20.3 us  [send(): return lax.ppermute(value, 'group', pairs)]
    broadcast_in_dim x1 -> x0, local copies, waits for them, and re-layouts: 1.32 us -> none  [per_device(): conv_bias[None, :]]
  transfers between devices with their start and end apart: 14 -> 11, of which waited for: 5 -> 3; matrix products, arithmetic and copies ran while one was open for 2% -> 0% of each run, Pallas kernels for 34% -> 34%
where the time goes in v3:
time: 49.8 us; the launch traced here: 49.6 us
  Pallas kernels  21.8 us (44%)
  starting transfers between devices  20.3 us (41%)
  waiting for transfers between devices  6.34 us (13%)
  local copies, waits for them, and re-layouts  0.93 us (2%)
    pallas_call x14, Pallas kernels, call(): pl.pallas_call(body, grid=grid, in_specs=[SMEM] * len(scalars) + specs +...  21.8 us
    ppermute x11, starting transfers between devices, send(): return lax.ppermute(value, 'group', pairs)  20.3 us
    ppermute x11, waiting for transfers between devices, send(): return lax.ppermute(value, 'group', pairs)  6.34 us
  transfers between devices with their start and end apart: 11, of which 3 were waited for; matrix products, arithmetic and copies ran while one was open for 0% of the time, Pallas kernels for 34%

profile of v3, /device:TPU:0, one launch (start us, length us, event | category | flops | bytes accessed | tf_op | source)
XLA Modules:
  0.0 49.6 jit_solution(17414748592629495848)
XLA Ops:
  0.0 0.9 %slice.3 = bf16[16,2816]{1,0:T(8,128)(2,1)S(1)} slice(bf16[256,2816]{1,0:T(8,128)(2,1)} %refs_1_.1), slice={[240:256], [0:2816]} | slice | bytes 180224 | tf_op jit(solution)/shard_map/slice | solution.py:498
  0.9 4.8 %collective-permute-start = (bf16[16,2816]{1,0:T(8,128)(2,1)S(1)}, bf16[16,2816]{1,0:T(8,128)(2,1)S(1)}, u32[]{:S(2)}, u32[]{:S(2)}) collective-permute-start(bf16[16,2816]{1,0:T(8,128)(2,1)S(1)} %slice.3), channel_id=1, source_target_pairs={{0,4},{4,8},{8,12},{12,16},{16,20},{20,24},{24,28},{1,5},{5,9},{9,... | collective-permute-start | bytes 270344 | tf_op jit(solution)/shard_map/ppermute | solution.py:492
  5.7 3.8 %shard_map.91 = (bf16[256,2560]{1,0:T(8,128)(2,1)S(1)}, bf16[256,256]{1,0:T(8,128)(2,1)S(1)}, f32[128,2560]{1,0:T(8,128)S(1)}, f32[40,256]{1,0:T(8,128)S(1)}, f3...) custom-call(s32[1]{0:T(128)} %bitcast.refs_0_.refs_1_, ...), custom_call_target="tpu_custom_call" | custom-call | flops 167772160 | bytes 4848664 | tf_op jit(solution)/shard_map/pallas_call | solution.py:446
  9.6 0.0 copy-start.1
  9.6 0.0 copy-start.2
  9.6 1.0 %shard_map.92 = (bf16[16,2560]{1,0:T(8,128)(2,1)S(1)}, bf16[16,256]{1,0:T(8,128)(2,1)S(1)}, bf16[144,640]{1,0:T(8,128)(2,1)S(1)}, bf16[144,640]{1,0:T(8,128)(2,1...) custom-call(s32[3]{0:T(128)S(1)} %get-tuple-element.40.refs_0_, s32[1]{0:T(128)} %bitcast.refs_0_.refs_1_, ...), custom_call_target="tpu_custom_call" | custom-call | flops 10485760 | bytes 2703360 | tf_op jit(solution)/shard_map/pallas_call | solution.py:446
  10.7 1.6 %collective-permute-start.1 = (bf16[144,640]{1,0:T(8,128)(2,1)S(1)}, bf16[144,640]{1,0:T(8,128)(2,1)S(1)}, u32[]{:S(2)}, u32[]{:S(2)}) collective-permute-start(bf16[144,640]{1,0:T(8,128)(2,1)S(1)} %get-tuple-element.57), channel_id=1, source_target_pairs={{0,4},{4,0},{8,12},{12,8},{16,20},{20,16},{24,28},{28,24},{1,5},{5... | collective-permute-start | bytes 552968 | tf_op jit(solution)/shard_map/ppermute | solution.py:492
  12.3 1.6 %collective-permute-start.2 = (bf16[144,640]{1,0:T(8,128)(2,1)S(1)}, bf16[144,640]{1,0:T(8,128)(2,1)S(1)}, u32[]{:S(2)}, u32[]{:S(2)}) collective-permute-start(bf16[144,640]{1,0:T(8,128)(2,1)S(1)} %get-tuple-element.58.refs_7_), channel_id=1, source_target_pairs={{0,8},{4,12},{8,0},{12,4},{16,24},{20,28},{24,16},{28,20},{1,9},{5... | collective-permute-start | bytes 552968 | tf_op jit(solution)/shard_map/ppermute | solution.py:492
  13.9 0.4 collective-permute-start.3
  14.2 0.8 %shard_map.93 = (bf16[256,128]{1,0:T(8,128)(2,1)S(1)}, f32[256,256]{1,0:T(8,128)S(1)}, bf16[256,384]{1,0:T(8,128)(2,1)S(1)}, f32[3,256,128]{2,1,0:T(8,128)S(1)}) custom-call(s32[3]{0:T(128)S(1)} %get-tuple-element.40.refs_0_, s32[1]{0:T(128)} %bitcast.refs_0_.refs_1_, bf16[256,256]{1,0:T(8,128)(2,1)S(1)} %get-tuple-element.48.refs_2_, ...), custom_call_target="tpu_custom_call" | custom-call | flops 16777216 | bytes 2048000 | tf_op jit(solution)/shard_map/pallas_call | solution.py:446
  15.0 1.8 %shard_map.95.refs_7_.refs_2_ = f32[256,640]{1,0:T(8,128)S(1)} custom-call(s32[3]{0:T(128)S(1)} %get-tuple-element.40.refs_0_, s32[1]{0:T(128)} %bitcast.refs_0_.refs_1_, bf16[256,2560]{1,0:T(8,128)(2,1)S(1)} %get-tuple-element.41.refs_2_, bf16[16,2560]{1,0:T(8,128)(2,1)S(1)} %get-tuple-element.47.refs_3_, f32[256,256]{1,0:T(8,128)S(1)} %get-tuple-element.51.refs_4_, ...), custom_call_target="tpu_custom_call" | custom-call | flops 83886080 | bytes 3367072 | tf_op jit(solution)/shard_map/pallas_call | solution.py:446
  16.8 1.8 %shard_map.94.refs_6_.refs_2_ = f32[256,640]{1,0:T(8,128)S(1)} custom-call(s32[3]{0:T(128)S(1)} %get-tuple-element.40.refs_0_, s32[1]{0:T(128)} %bitcast.refs_0_.refs_1_, bf16[256,2560]{1,0:T(8,128)(2,1)S(1)} %get-tuple-element.41.refs_2_, bf16[16,2560]{1,0:T(8,128)(2,1)S(1)} %get-tuple-element.47.refs_3_, f32[256,256]{1,0:T(8,128)S(1)} %get-tuple-element.51.refs_4_, ...), custom_call_target="tpu_custom_call" | custom-call | flops 83886080 | bytes 3367072 | tf_op jit(solution)/shard_map/pallas_call | solution.py:446
  18.6 1.3 %collective-permute-done.2.refs_4_ = bf16[144,640]{1,0:T(8,128)(2,1)S(1)} collective-permute-done((bf16[144,640]{1,0:T(8,128)(2,1)S(1)}, bf16[144,640]{1,0:T(8,128)(2,1)S(1)}, u32[]{:S(2)}, u32[]{:S(2)}) %collective-permute-start.2) | collective-permute-done | bytes 184352 | tf_op jit(solution)/shard_map/ppermute | solution.py:492
  19.9 2.1 %collective-permute-done.3.refs_5_ = bf16[144,640]{1,0:T(8,128)(2,1)S(1)} collective-permute-done((bf16[144,640]{1,0:T(8,128)(2,1)S(1)}, bf16[144,640]{1,0:T(8,128)(2,1)S(1)}, u32[]{:S(2)}, u32[]{:S(2)}) %collective-permute-start.3) | collective-permute-done | bytes 184352 | tf_op jit(solution)/shard_map/ppermute | solution.py:492
  22.0 0.9 %shard_map.96 = (bf16[128,640]{1,0:T(8,128)(2,1)S(1)}, f32[8,128]{1,0:T(8,128)S(1)}, f32[8,640]{1,0:T(8,128)S(1)}) custom-call(s32[3]{0:T(128)S(1)} %get-tuple-element.40.refs_0_, s32[1]{0:T(128)} %bitcast.refs_0_.refs_1_, bf16[144,640]{1,0:T(8,128)(2,1)S(1)} %get-tuple-element.56.refs_2_, bf16[144,640]{1,0:T(8,128)(2,1)S(1)} %collective-permute-done.1.refs_3_.refs_6_, ...), custom_call_target="tpu_custom_call" | custom-call | flops 327680 | bytes 925696 | tf_op jit(solution)/shard_map/pallas_call | solution.py:446
  22.8 0.7 %shard_map.97 = (bf16[128,640]{1,0:T(8,128)(2,1)S(1)}, bf16[384,640]{1,0:T(8,128)(2,1)S(1)}, bf16[256,640]{1,0:T(8,128)(2,1)S(1)}) custom-call(s32[3]{0:T(128)S(1)} %get-tuple-element.40.refs_0_, s32[1]{0:T(128)} %bitcast.refs_0_.refs_1_, bf16[144,640]{1,0:T(8,128)(2,1)S(1)} %get-tuple-element.56.refs_2_, ...), custom_call_target="tpu_custom_call" | custom-call | flops 327680 | bytes 1925120 | tf_op jit(solution)/shard_map/pallas_call | solution.py:446
  23.6 1.6 %collective-permute-start.4 = (bf16[384,640]{1,0:T(8,128)(2,1)S(1)}, bf16[384,640]{1,0:T(8,128)(2,1)S(1)}, u32[]{:S(2)}, u32[]{:S(2)}) collective-permute-start(bf16[384,640]{1,0:T(8,128)(2,1)S(1)} %get-tuple-element.65), channel_id=1, source_target_pairs={{0,4},{4,0},{8,12},{12,8},{16,20},{20,16},{24,28},{28,24},{1,5},{5... | collective-permute-start | bytes 1474568 | tf_op jit(solution)/shard_map/ppermute | solution.py:492
  25.2 1.6 %collective-permute-start.5 = (bf16[256,640]{1,0:T(8,128)(2,1)S(1)}, bf16[256,640]{1,0:T(8,128)(2,1)S(1)}, u32[]{:S(2)}, u32[]{:S(2)}) collective-permute-start(bf16[256,640]{1,0:T(8,128)(2,1)S(1)} %get-tuple-element.67), channel_id=1, source_target_pairs={{0,8},{4,12},{8,0},{12,4},{16,24},{20,28},{24,16},{28,20},{1,9},{5... | collective-permute-start | bytes 983048 | tf_op jit(solution)/shard_map/ppermute | solution.py:492
  26.8 1.4 %collective-permute-start.7 = (bf16[128,640]{1,0:T(8,128)(2,1)S(1)}, bf16[128,640]{1,0:T(8,128)(2,1)S(1)}, u32[]{:S(2)}, u32[]{:S(2)}) collective-permute-start(bf16[128,640]{1,0:T(8,128)(2,1)S(1)} %get-tuple-element.62.refs_8_.refs_9_), channel_id=1, source_target_pairs={{0,16},{4,20},{8,24},{12,28},{16,0},{20,4},{24,8},{28,12},{1,17},{... | collective-permute-start | bytes 491528 | tf_op jit(solution)/shard_map/ppermute | solution.py:492
  28.2 1.8 %shard_map.102.refs_2_ = f32[256,640]{1,0:T(8,128)S(1)} custom-call(s32[3]{0:T(128)S(1)} %get-tuple-element.40.refs_0_, s32[1]{0:T(128)} %bitcast.refs_0_.refs_1_, bf16[256,2560]{1,0:T(8,128)(2,1)S(1)} %get-tuple-element.41.refs_2_, bf16[16,2560]{1,0:T(8,128)(2,1)S(1)} %get-tuple-element.47.refs_3_, f32[256,256]{1,0:T(8,128)S(1)} %get-tuple-element.51.refs_4_, ...), custom_call_target="tpu_custom_call" | custom-call | flops 83886080 | bytes 3367072 | tf_op jit(solution)/shard_map/pallas_call | solution.py:446
  29.9 0.0 copy-start
  30.0 3.8 %collective-permute-start.6 = (bf16[128,640]{1,0:T(8,128)(2,1)S(1)}, bf16[128,640]{1,0:T(8,128)(2,1)S(1)}, u32[]{:S(2)}, u32[]{:S(2)}) collective-permute-start(bf16[128,640]{1,0:T(8,128)(2,1)S(1)} %get-tuple-element.63.refs_7_), channel_id=1, source_target_pairs={{0,12},{4,8},{16,28},{20,24},{1,13},{5,9},{17,29},{21,25},{2,14},{... | collective-permute-start | bytes 491528 | tf_op jit(solution)/shard_map/ppermute | solution.py:492
  33.7 1.8 %shard_map.100.refs_2_ = f32[256,640]{1,0:T(8,128)S(1)} custom-call(s32[3]{0:T(128)S(1)} %get-tuple-element.40.refs_0_, s32[1]{0:T(128)} %bitcast.refs_0_.refs_1_, bf16[256,2560]{1,0:T(8,128)(2,1)S(1)} %get-tuple-element.41.refs_2_, bf16[16,2560]{1,0:T(8,128)(2,1)S(1)} %get-tuple-element.47.refs_3_, f32[256,256]{1,0:T(8,128)S(1)} %get-tuple-element.51.refs_4_, ...), custom_call_target="tpu_custom_call" | custom-call | flops 83886080 | bytes 3367072 | tf_op jit(solution)/shard_map/pallas_call | solution.py:446
  35.5 2.9 %collective-permute-done.7.refs_11_ = bf16[128,640]{1,0:T(8,128)(2,1)S(1)} collective-permute-done((bf16[128,640]{1,0:T(8,128)(2,1)S(1)}, bf16[128,640]{1,0:T(8,128)(2,1)S(1)}, u32[]{:S(2)}, u32[]{:S(2)}) %collective-permute-start.7) | collective-permute-done | bytes 163872 | tf_op jit(solution)/shard_map/ppermute | solution.py:492
  38.4 0.4 collective-permute-start.10
  38.9 2.3 %collective-permute-start.8 = (bf16[128,640]{1,0:T(8,128)(2,1)S(1)}, bf16[128,640]{1,0:T(8,128)(2,1)S(1)}, u32[]{:S(2)}, u32[]{:S(2)}) collective-permute-start(bf16[128,640]{1,0:T(8,128)(2,1)S(1)} %collective-permute-done.7.refs_11_), channel_id=1, source_target_pairs={{0,4},{4,0},{8,12},{12,8},{16,20},{20,16},{24,28},{28,24},{1,5},{5... | collective-permute-start | bytes 491528 | tf_op jit(solution)/shard_map/ppermute | solution.py:492
  41.2 0.8 %collective-permute-start.9 = (bf16[128,640]{1,0:T(8,128)(2,1)S(1)}, bf16[128,640]{1,0:T(8,128)(2,1)S(1)}, u32[]{:S(2)}, u32[]{:S(2)}) collective-permute-start(bf16[128,640]{1,0:T(8,128)(2,1)S(1)} %collective-permute-done.7.refs_11_), channel_id=1, source_target_pairs={{0,8},{4,12},{8,0},{12,4},{16,24},{20,28},{24,16},{28,20},{1,9},{5... | collective-permute-start | bytes 491528 | tf_op jit(solution)/shard_map/ppermute | solution.py:492
  41.9 1.3 %shard_map.98 = (f32[256,640]{1,0:T(8,128)S(1)}, f32[256,640]{1,0:T(8,128)S(1)}) custom-call(s32[3]{0:T(128)S(1)} %get-tuple-element.40.refs_0_, s32[1]{0:T(128)} %bitcast.refs_0_.refs_1_, f32[256,640]{1,0:T(8,128)S(1)} %shard_map.94.refs_6_.refs_2_, bf16[256,128]{1,0:T(8,128)(2,1)S(1)} %get-tuple-element.54.refs_3_.refs_10_, ...), custom_call_target="tpu_custom_call" | custom-call | flops 83886080 | bytes 4087808 | tf_op jit(solution)/shard_map/pallas_call | solution.py:446
  43.2 1.2 %shard_map.101 = (f32[256,640]{1,0:T(8,128)S(1)}, f32[256,640]{1,0:T(8,128)S(1)}) custom-call(s32[3]{0:T(128)S(1)} %get-tuple-element.40.refs_0_, s32[1]{0:T(128)} %bitcast.refs_0_.refs_1_, f32[256,640]{1,0:T(8,128)S(1)} %shard_map.100.refs_2_, bf16[256,128]{1,0:T(8,128)(2,1)S(1)} %get-tuple-element.54.refs_3_.refs_10_, ...), custom_call_target="tpu_custom_call" | custom-call | flops 83886080 | bytes 4395008 | tf_op jit(solution)/shard_map/pallas_call | solution.py:446
  44.5 1.3 %shard_map.99 = (f32[256,640]{1,0:T(8,128)S(1)}, f32[256,640]{1,0:T(8,128)S(1)}) custom-call(s32[3]{0:T(128)S(1)} %get-tuple-element.40.refs_0_, s32[1]{0:T(128)} %bitcast.refs_0_.refs_1_, f32[256,640]{1,0:T(8,128)S(1)} %shard_map.95.refs_7_.refs_2_, bf16[256,128]{1,0:T(8,128)(2,1)S(1)} %get-tuple-element.54.refs_3_.refs_10_, ...), custom_call_target="tpu_custom_call" | custom-call | flops 83886080 | bytes 4722688 | tf_op jit(solution)/shard_map/pallas_call | solution.py:446
  45.8 1.3 %shard_map.103 = (f32[256,640]{1,0:T(8,128)S(1)}, f32[256,640]{1,0:T(8,128)S(1)}) custom-call(s32[3]{0:T(128)S(1)} %get-tuple-element.40.refs_0_, s32[1]{0:T(128)} %bitcast.refs_0_.refs_1_, f32[256,640]{1,0:T(8,128)S(1)} %shard_map.102.refs_2_, bf16[256,128]{1,0:T(8,128)(2,1)S(1)} %get-tuple-element.54.refs_3_.refs_10_, ...), custom_call_target="tpu_custom_call" | custom-call | flops 83886080 | bytes 4395008 | tf_op jit(solution)/shard_map/pallas_call | solution.py:446
  47.1 2.5 %shard_map.104 = bf16[256,2560]{1,0:T(8,128)(2,1)} custom-call(s32[3]{0:T(128)S(1)} %get-tuple-element.40.refs_0_, s32[1]{0:T(128)} %bitcast.refs_0_.refs_1_, f32[256,640]{1,0:T(8,128)S(1)} %get-tuple-element.64.refs_2_, f32[256,640]{1,0:T(8,128)S(1)} %get-tuple-element.66.refs_3_, f32[256,640]{1,0:T(8,128)S(1)} %get-tuple-element.68.refs_4_, ...), custom_call_target="tpu_custom_call" | custom-call | flops 167772160 | bytes 7284736 | tf_op jit(solution)/shard_map/pallas_call | solution.py:446
  (14 shorter events, 0.0 us)
Async XLA Ops:
  0.9 8.7 %collective-permute-start = (bf16[16,2816]{1,0:T(8,128)(2,1)S(1)}, bf16[16,2816]{1,0:T(8,128)(2,1)S(1)}, u32[]{:S(2)}, u32[]{:S(2)}) collective-permute-start(bf16[16,2816]{1,0:T(8,128)(2,1)S(1)} %slice.3), channel_id=1, source_target_pairs={{0,4},{4,8},{8,12},{12,16},{16,20},{20,24},{24,28},{1,5},{5,9},{9,... | collective-permute-start | bytes 270344 | tf_op jit(solution)/shard_map/ppermute | solution.py:492
  9.6 4.6 %copy-start.1 = (f32[40,20,256]{2,0,1:T(8,128)S(1)}, f32[40,20,256]{2,0,1:T(8,128)}, u32[]{:S(2)}) copy-start(f32[40,20,256]{2,0,1:T(8,128)} %param.14) | copy-start | bytes 2457604
  9.6 5.4 %copy-start.2 = (f32[40]{0:T(128)S(1)}, f32[40]{0:T(128)}, u32[]{:S(2)}) copy-start(f32[40]{0:T(128)} %refs_8_.14) | copy-start | bytes 484
  10.7 7.9 %collective-permute-start.1 = (bf16[144,640]{1,0:T(8,128)(2,1)S(1)}, bf16[144,640]{1,0:T(8,128)(2,1)S(1)}, u32[]{:S(2)}, u32[]{:S(2)}) collective-permute-start(bf16[144,640]{1,0:T(8,128)(2,1)S(1)} %get-tuple-element.57), channel_id=1, source_target_pairs={{0,4},{4,0},{8,12},{12,8},{16,20},{20,16},{24,28},{28,24},{1,5},{5... | collective-permute-start | bytes 552968 | tf_op jit(solution)/shard_map/ppermute | solution.py:492
  12.3 7.6 %collective-permute-start.2 = (bf16[144,640]{1,0:T(8,128)(2,1)S(1)}, bf16[144,640]{1,0:T(8,128)(2,1)S(1)}, u32[]{:S(2)}, u32[]{:S(2)}) collective-permute-start(bf16[144,640]{1,0:T(8,128)(2,1)S(1)} %get-tuple-element.58.refs_7_), channel_id=1, source_target_pairs={{0,8},{4,12},{8,0},{12,4},{16,24},{20,28},{24,16},{28,20},{1,9},{5... | collective-permute-start | bytes 552968 | tf_op jit(solution)/shard_map/ppermute | solution.py:492
  13.9 8.1 %collective-permute-start.3 = (bf16[144,640]{1,0:T(8,128)(2,1)S(1)}, bf16[144,640]{1,0:T(8,128)(2,1)S(1)}, u32[]{:S(2)}, u32[]{:S(2)}) collective-permute-start(bf16[144,640]{1,0:T(8,128)(2,1)S(1)} %get-tuple-element.59), channel_id=1, source_target_pairs={{0,12},{4,8},{8,4},{12,0},{16,28},{20,24},{24,20},{28,16},{1,13},{... | collective-permute-start | bytes 552968 | tf_op jit(solution)/shard_map/ppermute | solution.py:492
  23.6 20.9 %collective-permute-start.4 = (bf16[384,640]{1,0:T(8,128)(2,1)S(1)}, bf16[384,640]{1,0:T(8,128)(2,1)S(1)}, u32[]{:S(2)}, u32[]{:S(2)}) collective-permute-start(bf16[384,640]{1,0:T(8,128)(2,1)S(1)} %get-tuple-element.65), channel_id=1, source_target_pairs={{0,4},{4,0},{8,12},{12,8},{16,20},{20,16},{24,28},{28,24},{1,5},{5... | collective-permute-start | bytes 1474568 | tf_op jit(solution)/shard_map/ppermute | solution.py:492
  25.2 16.0 %collective-permute-start.5 = (bf16[256,640]{1,0:T(8,128)(2,1)S(1)}, bf16[256,640]{1,0:T(8,128)(2,1)S(1)}, u32[]{:S(2)}, u32[]{:S(2)}) collective-permute-start(bf16[256,640]{1,0:T(8,128)(2,1)S(1)} %get-tuple-element.67), channel_id=1, source_target_pairs={{0,8},{4,12},{8,0},{12,4},{16,24},{20,28},{24,16},{28,20},{1,9},{5... | collective-permute-start | bytes 983048 | tf_op jit(solution)/shard_map/ppermute | solution.py:492
  26.8 11.7 %collective-permute-start.7 = (bf16[128,640]{1,0:T(8,128)(2,1)S(1)}, bf16[128,640]{1,0:T(8,128)(2,1)S(1)}, u32[]{:S(2)}, u32[]{:S(2)}) collective-permute-start(bf16[128,640]{1,0:T(8,128)(2,1)S(1)} %get-tuple-element.62.refs_8_.refs_9_), channel_id=1, source_target_pairs={{0,16},{4,20},{8,24},{12,28},{16,0},{20,4},{24,8},{28,12},{1,17},{... | collective-permute-start | bytes 491528 | tf_op jit(solution)/shard_map/ppermute | solution.py:492
  29.9 12.0 %copy-start.3 = (f32[2560]{0:T(1024)S(1)}, f32[2560]{0:T(1024)}, u32[]{:S(2)}) copy-start(f32[2560]{0:T(1024)} %param.16) | copy-start | bytes 30724
  29.9 12.0 %copy-start = (bf16[256,2560]{1,0:T(8,128)(2,1)S(1)}, bf16[256,2560]{1,0:T(8,128)(2,1)}, u32[]{:S(2)}) copy-start(bf16[256,2560]{1,0:T(8,128)(2,1)} %refs_8_.15) | copy-start | bytes 3932164
  30.0 15.8 %collective-permute-start.6 = (bf16[128,640]{1,0:T(8,128)(2,1)S(1)}, bf16[128,640]{1,0:T(8,128)(2,1)S(1)}, u32[]{:S(2)}, u32[]{:S(2)}) collective-permute-start(bf16[128,640]{1,0:T(8,128)(2,1)S(1)} %get-tuple-element.63.refs_7_), channel_id=1, source_target_pairs={{0,12},{4,8},{16,28},{20,24},{1,13},{5,9},{17,29},{21,25},{2,14},{... | collective-permute-start | bytes 491528 | tf_op jit(solution)/shard_map/ppermute | solution.py:492
  38.4 8.6 %collective-permute-start.10 = (bf16[128,640]{1,0:T(8,128)(2,1)S(1)}, bf16[128,640]{1,0:T(8,128)(2,1)S(1)}, u32[]{:S(2)}, u32[]{:S(2)}) collective-permute-start(bf16[128,640]{1,0:T(8,128)(2,1)S(1)} %collective-permute-done.7.refs_11_), channel_id=1, source_target_pairs={{0,12},{4,8},{8,4},{12,0},{16,28},{20,24},{24,20},{28,16},{1,13},{... | collective-permute-start | bytes 491528 | tf_op jit(solution)/shard_map/ppermute | solution.py:492
  38.9 8.2 %collective-permute-start.8 = (bf16[128,640]{1,0:T(8,128)(2,1)S(1)}, bf16[128,640]{1,0:T(8,128)(2,1)S(1)}, u32[]{:S(2)}, u32[]{:S(2)}) collective-permute-start(bf16[128,640]{1,0:T(8,128)(2,1)S(1)} %collective-permute-done.7.refs_11_), channel_id=1, source_target_pairs={{0,4},{4,0},{8,12},{12,8},{16,20},{20,16},{24,28},{28,24},{1,5},{5... | collective-permute-start | bytes 491528 | tf_op jit(solution)/shard_map/ppermute | solution.py:492
  41.2 5.9 %collective-permute-start.9 = (bf16[128,640]{1,0:T(8,128)(2,1)S(1)}, bf16[128,640]{1,0:T(8,128)(2,1)S(1)}, u32[]{:S(2)}, u32[]{:S(2)}) collective-permute-start(bf16[128,640]{1,0:T(8,128)(2,1)S(1)} %collective-permute-done.7.refs_11_), channel_id=1, source_target_pairs={{0,8},{4,12},{8,0},{12,4},{16,24},{20,28},{24,16},{28,20},{1,9},{5... | collective-permute-start | bytes 491528 | tf_op jit(solution)/shard_map/ppermute | solution.py:492

commit v4 on v3

--- a/solution.py
+++ b/solution.py
@@ -13,7 +13,6 @@
 HALO = 16
 PLACES = 4
 LANES = 128
-EXACT = lax.Precision.HIGHEST
 
 
 def iota(shape, dim):
@@ -95,8 +94,8 @@
         fetch.start()
 
     apart = iota((tok, tok), 0) - iota((tok, tok), 1)
-    upper = jnp.where(apart <= 0, 1.0, 0.0)
-    lower = jnp.where(apart >= 0, 1.0, 0.0)
+    upper = jnp.where(apart <= 0, 1.0, 0.0).astype(bf16)
+    lower = jnp.where(apart >= 0, 1.0, 0.0).astype(bf16)
     fetches[0].wait()
     bounds = segment_bounds(lengths, recordings)
     first = group[0] * tok
@@ -106,12 +105,15 @@
         same = jnp.concatenate([same] * (tok // LANES), axis=1)
         shift_ref[(tap - 1) * tok : tap * tok] = jnp.where(apart == tap, same, 0.0).astype(bf16)
     fetches[1].wait()
-    decay = jnp.concatenate(
-        [decay_ref[...], jnp.zeros((LANES - heads, tok), f32)], axis=0
-    )
-    cum = dot(decay_ref[...], upper, ((1,), (0,)), EXACT)
+    pad = jnp.zeros((LANES - heads, tok), f32)
+    high, rest = two_parts(jnp.concatenate([decay_ref[...], pad], axis=0))
+    mid, low = two_parts(rest)
+    parts = jnp.concatenate([high, mid, low], axis=0).astype(bf16)
+    cum = dot(parts, upper, ((1,), (0,)))
+    cum = cum[:heads] + cum[LANES : LANES + heads] + cum[2 * LANES : 2 * LANES + heads]
     cum_ref[...] = cum
-    cumt = dot(lower, decay, ((1,), (1,)), EXACT)
+    cumt = dot(lower, parts, ((1,), (1,)))
+    cumt = cumt[:, :LANES] + cumt[:, LANES : 2 * LANES] + cumt[:, 2 * LANES :]
     cumt_ref[...] = cumt
     end = cumt[tok - 1 : tok, :]
     last = first + tok - 1
@@ -365,7 +367,7 @@
 
 def far_kernel(
     dims, mask, lengths, group, sum_ref, queries_ref, coef_ref, scale_ref, low_ref,
-    pair_ref, gate_ref, out_ref, next_ref,
+    pair_ref, gate_ref, *refs,
 ):
     head_dim, state, low_from, pair_from = dims
     tok, cols = sum_ref.shape
@@ -382,49 +384,64 @@
         jnp.concatenate(coefs, axis=0), jnp.concatenate([copies, copies], axis=0), ((1,), (0,))
     )
     total = sum_ref[...]
-    for bit, state_in in enumerate(
-        (low_ref[low_from : low_from + state], pair_ref[pair_from : pair_from + state])
-    ):
+    states = [low_ref[low_from : low_from + state], pair_ref[pair_from : pair_from + state]]
+    if len(refs) > 2:
+        states.append(refs[0][...])
+    for bit, state_in in enumerate(states):
         total = total + dot(queries, state_in, ((1,), (0,))) * factors[bit * tok : (bit + 1) * tok]
     where = pl.multiple_of(quarter * cols, LANES)
     gate = silu(gate_ref[:, pl.ds(where, cols)].astype(f32))
+    if len(refs) == 2:
+        out_ref, next_ref = refs
+        out_ref[...] = total * gate
+        next_ref[...] = factors[2 * tok :] * gate
+        return
+    _, own_sum_ref, own_factor_ref, own_top_ref, out_ref, own_ref = refs
     out_ref[...] = total * gate
-    next_ref[...] = factors[2 * tok :] * gate
-
-
-def final_kernel(dims, lengths, group, *refs):
-    count, rows = dims
-    sums = refs[:PLACES]
-    factors = refs[PLACES : 2 * PLACES]
-    queries_ref = refs[2 * PLACES]
-    states = refs[2 * PLACES + 1 : 3 * PLACES + 1]
-    gain_ref, out_ref, gated_ref, scale_ref = refs[3 * PLACES + 1 :]
+    read = dot(queries, own_top_ref[...], ((1,), (0,)))
+    own_ref[...] = own_sum_ref[...] + read * own_factor_ref[...]
+
+
+def final_kernel(
+    dims, lengths, group, queries_ref, own_ref, done_ref, one_sum, one_factor, one_top, two_sum,
+    two_factor, two_top, gain_ref, out_hbm, gated_ref, out_ref, sems,
+):
+    count, masks, chunks = dims
     place = lax.rem(group[0], PLACES)
-    cols = sums[0].shape[1]
-    step = pl.program_id(0)
-
-    @pl.when(step == 0)
-    def _():
-        queries = queries_ref[...]
-        squares = jnp.zeros((queries.shape[0], LANES), f32)
-        for mask in range(PLACES):
-            read = dot(queries, states[mask][...], ((1,), (0,)))
-            value = sums[mask][...] + read * factors[mask][...]
-            gated_ref[mask] = value
-            for lo in range(0, cols, LANES):
-                squares = squares + value[:, lo : lo + LANES] * value[:, lo : lo + LANES]
-        mean = jnp.sum(squares, axis=1, keepdims=True) / count
-        scale_ref[...] = jnp.broadcast_to(lax.rsqrt(mean + eps_norm), scale_ref.shape)
-
-    here = pl.ds(pl.multiple_of(step * rows, rows), rows)
-    scale = scale_ref[here, :]
-    for mask in range(PLACES):
-        where = pl.multiple_of(jnp.bitwise_xor(place, mask) * cols, LANES)
+    tok, cols = own_ref.shape
+    queries = queries_ref[...]
+    squares = jnp.zeros((tok, LANES), f32)
+    for at, (total, factor, top) in enumerate(
+        (
+            (own_ref, None, None),
+            (done_ref, None, None),
+            (one_sum, one_factor, one_top),
+            (two_sum, two_factor, two_top),
+        )
+    ):
+        value = total[...]
+        if top is not None:
+            value = value + dot(queries, top[...], ((1,), (0,))) * factor[...]
+            gated_ref[at - 2] = value
         for lo in range(0, cols, LANES):
-            columns = pl.ds(pl.multiple_of(where + lo, LANES), LANES)
-            out_ref[:, columns] = (
-                gated_ref[mask, here, lo : lo + LANES] * scale * gain_ref[:, columns]
+            squares = squares + value[:, lo : lo + LANES] * value[:, lo : lo + LANES]
+    mean = jnp.sum(squares, axis=1, keepdims=True) / count
+    scale = lax.rsqrt(mean + eps_norm)
+    rows = tok // chunks
+    copies = []
+    for chunk in range(chunks):
+        here = slice(chunk * rows, (chunk + 1) * rows)
+        for at, mask in enumerate(masks):
+            where = pl.multiple_of(jnp.bitwise_xor(place, mask) * cols, LANES)
+            value = (own_ref[here], done_ref[here])[at] if at < 2 else gated_ref[at - 2, here]
+            out_ref[here, pl.ds(where, cols)] = (
+                value * scale[here] * gain_ref[:, pl.ds(where, cols)]
             ).astype(bf16)
+        copy = pltpu.make_async_copy(out_ref.at[here], out_hbm.at[here], sems.at[chunk])
+        copy.start()
+        copies.append(copy)
+    for copy in copies:
+        copy.wait()
 
 
 VMEM = pl.BlockSpec(memory_space=pltpu.VMEM)
@@ -603,6 +620,23 @@
     got_beside = quad_send(beside, 1)
     got_across = quad_send(across, 2)
 
+    lows = [(got_one, 0), (got_beside, 0), (got_across, state), (got_beside, state)]
+    pairs = [(pair, 0), (got_beside, 2 * state), (got_across, 0), (got_three_of_pair, 0)]
+
+    def far_part(mask, more=(), after=()):
+        return list(
+            call(
+                functools.partial(far_kernel, (head_dim, state, lows[mask][1], pairs[mask][1]), mask),
+                scalars,
+                (sums[mask], queries, coefs, scale, lows[mask][0], pairs[mask][0], gate_input) + more,
+                [shape((tok, cols), f32), shape((tok, cols), f32)],
+                flops=int(2 * 1.1e9),
+                after=after,
+            )
+        )
+
+    halves = {0: far_part(0)}
+
     befores = [scale[0, :heads], scale[1, :heads], scale[2, :heads]]
     crossed = []
     running, total = quad, scale[3, :heads]
@@ -610,7 +644,7 @@
         mask = 2**bit
         last = bit + 1 == high_bits
         far = quad_send(running, mask, lambda source, target: True)
-        crossed.append(lax.optimization_barrier((far, sums[3], sums[2]))[0])
+        crossed.append(lax.optimization_barrier((far, sums[3], sums[2], halves[0][0]))[0])
         if not last:
             on_top = group // mask % 2 == 1
             far_total = quad_send(total, mask)
@@ -627,28 +661,16 @@
             befores.append(jnp.where(on_top, far_total * befores[-1], befores[-1]))
             total = total * far_total
 
-    lows = [(got_one, 0), (got_beside, 0), (got_across, state), (got_beside, state)]
-    pairs = [(pair, 0), (got_beside, 2 * state), (got_across, 0), (got_three_of_pair, 0)]
-
     def all_quarters(value, bit):
         return [value] + [
             quad_send(value, mask)
             for mask in range(1, PLACES)
         ]
 
-    halves = [
-        list(
-            call(
-                functools.partial(far_kernel, (head_dim, state, lows[mask][1], pairs[mask][1]), mask),
-                scalars,
-                (sums[mask], queries, coefs, scale, lows[mask][0], pairs[mask][0], gate_input),
-                [shape((tok, cols), f32), shape((tok, cols), f32)],
-                flops=4 * tok * cols * state,
-            )
-        )
-        for mask in range(PLACES)
-    ]
     tops = [all_quarters(value, bit + 2) for bit, value in enumerate(crossed)]
+    halves[2] = far_part(2)
+    halves[1] = far_part(1, after=halves[2][:1])
+    extra = {mask: [] for mask in range(PLACES)}
     for bit in range(3, high_bits):
         coef = levels[low_bits + 1 + bit] * entry
         coef = coef * jnp.where(group // 2**bit % 2 == 1, befores[bit], 0.0)[:, None]
@@ -658,21 +680,35 @@
             gate = lax.dynamic_slice_in_dim(gate_input, (place ^ mask) * cols, cols, axis=1)
             read = jnp.dot(queries, tops[bit - 2][mask], preferred_element_type=f32)
             read = read * jnp.repeat(mine, head_dim, axis=0).T
-            halves[mask][0] = halves[mask][0] + read * jax.nn.silu(gate.astype(f32))
-
-    rows = 128
+            extra[mask].append(read * jax.nn.silu(gate.astype(f32)))
+    for mask in halves:
+        halves[mask][0] = sum(extra[mask], halves[mask][0])
+    done, own_done = far_part(3, (tops[0][3], halves[0][0], halves[0][1], tops[0][0]), halves[1][:1])
+    done = sum(extra[3], done)
+
+    chunks = 4
     return call(
-        functools.partial(final_kernel, (float(width), rows)),
+        functools.partial(final_kernel, (float(width), (0, 3, 1, 2), chunks)),
         scalars,
-        [h[0] for h in halves]
-        + [h[1] for h in halves]
-        + [queries]
-        + tops[0]
-        + [norm_gain[None, :]],
+        (
+            queries,
+            own_done,
+            done,
+            halves[1][0],
+            halves[1][1],
+            tops[0][1],
+            halves[2][0],
+            halves[2][1],
+            tops[0][2],
+            norm_gain[None, :],
+        ),
         [shape((tok, width), bf16)],
-        [pltpu.VMEM((PLACES, tok, cols), f32), pltpu.VMEM((tok, LANES), f32)],
-        out_specs=[pl.BlockSpec((rows, width), lambda i, *_: (i, 0))],
-        grid=(tok // rows,),
+        [
+            pltpu.VMEM((2, tok, cols), f32),
+            pltpu.VMEM((tok, width), bf16),
+            pltpu.SemaphoreType.DMA((chunks,)),
+        ],
+        out_specs=[HBM],
         flops=2 * tok * width * state,
     )[0]
 

time: 49.8 us -> 47.6 us (0.956)
  waiting for transfers between devices: 6.34 us -> 4.08 us
    ppermute x11, waiting for transfers between devices: 6.34 us -> 4.08 us  [send(): return lax.ppermute(value, 'group', pairs)]
  transfers between devices with their start and end apart: 11 -> 11, of which waited for: 3 -> 5; matrix products, arithmetic and copies ran while one was open for 0% -> 0% of each run, Pallas kernels for 34% -> 36%
where the time goes in v4:
time: 47.6 us; the launch traced here: 47.4 us
  Pallas kernels  21.7 us (46%)
  starting transfers between devices  20.3 us (43%)
  waiting for transfers between devices  4.08 us (9%)
  local copies, waits for them, and re-layouts  0.92 us (2%)
    pallas_call x14, Pallas kernels, call(): pl.pallas_call(body, grid=grid, in_specs=[SMEM] * len(scalars) + specs +...  21.7 us
    ppermute x11, starting transfers between devices, send(): return lax.ppermute(value, 'group', pairs)  20.3 us
    ppermute x11, waiting for transfers between devices, send(): return lax.ppermute(value, 'group', pairs)  4.08 us
  transfers between devices with their start and end apart: 11, of which 5 were waited for; matrix products, arithmetic and copies ran while one was open for 0% of the time, Pallas kernels for 36%

profile of v4, /device:TPU:0, one launch (start us, length us, event | category | flops | bytes accessed | tf_op | source)
XLA Modules:
  0.0 47.4 jit_solution(14017404847094715752)
XLA Ops:
  0.0 0.9 %slice.3 = bf16[16,2816]{1,0:T(8,128)(2,1)S(1)} slice(bf16[256,2816]{1,0:T(8,128)(2,1)} %refs_1_.1), slice={[240:256], [0:2816]} | slice | bytes 180224 | tf_op jit(solution)/shard_map/slice | solution.py:515
  0.9 4.8 %collective-permute-start = (bf16[16,2816]{1,0:T(8,128)(2,1)S(1)}, bf16[16,2816]{1,0:T(8,128)(2,1)S(1)}, u32[]{:S(2)}, u32[]{:S(2)}) collective-permute-start(bf16[16,2816]{1,0:T(8,128)(2,1)S(1)} %slice.3), channel_id=1, source_target_pairs={{0,4},{4,8},{8,12},{12,16},{16,20},{20,24},{24,28},{1,5},{5,9},{9,... | collective-permute-start | bytes 270344 | tf_op jit(solution)/shard_map/ppermute | solution.py:509
  5.7 3.8 %shard_map.91 = (bf16[256,2560]{1,0:T(8,128)(2,1)S(1)}, bf16[256,256]{1,0:T(8,128)(2,1)S(1)}, f32[128,2560]{1,0:T(8,128)S(1)}, f32[40,256]{1,0:T(8,128)S(1)}, f3...) custom-call(s32[1]{0:T(128)} %bitcast.refs_0_.refs_1_, ...), custom_call_target="tpu_custom_call" | custom-call | flops 167772160 | bytes 4848664 | tf_op jit(solution)/shard_map/pallas_call | solution.py:463
  9.5 0.0 copy-start
  9.5 0.0 copy-start.1
  9.5 1.1 %shard_map.92 = (bf16[16,2560]{1,0:T(8,128)(2,1)S(1)}, bf16[16,256]{1,0:T(8,128)(2,1)S(1)}, bf16[144,640]{1,0:T(8,128)(2,1)S(1)}, bf16[144,640]{1,0:T(8,128)(2,1...) custom-call(s32[3]{0:T(128)S(1)} %get-tuple-element.40.refs_0_, s32[1]{0:T(128)} %bitcast.refs_0_.refs_1_, ...), custom_call_target="tpu_custom_call" | custom-call | flops 10485760 | bytes 2703360 | tf_op jit(solution)/shard_map/pallas_call | solution.py:463
  10.6 1.6 %collective-permute-start.1 = (bf16[144,640]{1,0:T(8,128)(2,1)S(1)}, bf16[144,640]{1,0:T(8,128)(2,1)S(1)}, u32[]{:S(2)}, u32[]{:S(2)}) collective-permute-start(bf16[144,640]{1,0:T(8,128)(2,1)S(1)} %get-tuple-element.57), channel_id=1, source_target_pairs={{0,4},{4,0},{8,12},{12,8},{16,20},{20,16},{24,28},{28,24},{1,5},{5... | collective-permute-start | bytes 552968 | tf_op jit(solution)/shard_map/ppermute | solution.py:509
  12.2 1.6 %collective-permute-start.2 = (bf16[144,640]{1,0:T(8,128)(2,1)S(1)}, bf16[144,640]{1,0:T(8,128)(2,1)S(1)}, u32[]{:S(2)}, u32[]{:S(2)}) collective-permute-start(bf16[144,640]{1,0:T(8,128)(2,1)S(1)} %get-tuple-element.58.refs_7_), channel_id=1, source_target_pairs={{0,8},{4,12},{8,0},{12,4},{16,24},{20,28},{24,16},{28,20},{1,9},{5... | collective-permute-start | bytes 552968 | tf_op jit(solution)/shard_map/ppermute | solution.py:509
  13.8 0.4 collective-permute-start.3
  14.2 0.8 %shard_map.93 = (bf16[256,128]{1,0:T(8,128)(2,1)S(1)}, f32[256,256]{1,0:T(8,128)S(1)}, bf16[256,384]{1,0:T(8,128)(2,1)S(1)}, f32[3,256,128]{2,1,0:T(8,128)S(1)}) custom-call(s32[3]{0:T(128)S(1)} %get-tuple-element.40.refs_0_, s32[1]{0:T(128)} %bitcast.refs_0_.refs_1_, bf16[256,256]{1,0:T(8,128)(2,1)S(1)} %get-tuple-element.41.refs_2_, ...), custom_call_target="tpu_custom_call" | custom-call | flops 16777216 | bytes 2048000 | tf_op jit(solution)/shard_map/pallas_call | solution.py:463
  14.9 1.8 %shard_map.95.refs_6_.refs_2_ = f32[256,640]{1,0:T(8,128)S(1)} custom-call(s32[3]{0:T(128)S(1)} %get-tuple-element.40.refs_0_, s32[1]{0:T(128)} %bitcast.refs_0_.refs_1_, bf16[256,2560]{1,0:T(8,128)(2,1)S(1)} %get-tuple-element.50.refs_2_, bf16[16,2560]{1,0:T(8,128)(2,1)S(1)} %get-tuple-element.51.refs_3_, f32[256,256]{1,0:T(8,128)S(1)} %get-tuple-element.52.refs_4_, ...), custom_call_target="tpu_custom_call" | custom-call | flops 83886080 | bytes 3367072 | tf_op jit(solution)/shard_map/pallas_call | solution.py:463
  16.7 1.8 %shard_map.96.refs_7_.refs_2_ = f32[256,640]{1,0:T(8,128)S(1)} custom-call(s32[3]{0:T(128)S(1)} %get-tuple-element.40.refs_0_, s32[1]{0:T(128)} %bitcast.refs_0_.refs_1_, bf16[256,2560]{1,0:T(8,128)(2,1)S(1)} %get-tuple-element.50.refs_2_, bf16[16,2560]{1,0:T(8,128)(2,1)S(1)} %get-tuple-element.51.refs_3_, f32[256,256]{1,0:T(8,128)S(1)} %get-tuple-element.52.refs_4_, ...), custom_call_target="tpu_custom_call" | custom-call | flops 83886080 | bytes 3367072 | tf_op jit(solution)/shard_map/pallas_call | solution.py:463
  18.5 1.3 %collective-permute-done.2.refs_4_ = bf16[144,640]{1,0:T(8,128)(2,1)S(1)} collective-permute-done((bf16[144,640]{1,0:T(8,128)(2,1)S(1)}, bf16[144,640]{1,0:T(8,128)(2,1)S(1)}, u32[]{:S(2)}, u32[]{:S(2)}) %collective-permute-start.2) | collective-permute-done | bytes 184352 | tf_op jit(solution)/shard_map/ppermute | solution.py:509
  19.8 2.1 %collective-permute-done.3.refs_5_ = bf16[144,640]{1,0:T(8,128)(2,1)S(1)} collective-permute-done((bf16[144,640]{1,0:T(8,128)(2,1)S(1)}, bf16[144,640]{1,0:T(8,128)(2,1)S(1)}, u32[]{:S(2)}, u32[]{:S(2)}) %collective-permute-start.3) | collective-permute-done | bytes 184352 | tf_op jit(solution)/shard_map/ppermute | solution.py:509
  21.9 0.9 %shard_map.97 = (bf16[128,640]{1,0:T(8,128)(2,1)S(1)}, f32[8,128]{1,0:T(8,128)S(1)}, f32[8,640]{1,0:T(8,128)S(1)}) custom-call(s32[3]{0:T(128)S(1)} %get-tuple-element.40.refs_0_, s32[1]{0:T(128)} %bitcast.refs_0_.refs_1_, bf16[144,640]{1,0:T(8,128)(2,1)S(1)} %get-tuple-element.56.refs_2_, bf16[144,640]{1,0:T(8,128)(2,1)S(1)} %collective-permute-done.1.refs_3_.refs_6_, ...), custom_call_target="tpu_custom_call" | custom-call | flops 327680 | bytes 925696 | tf_op jit(solution)/shard_map/pallas_call | solution.py:463
  22.8 0.7 %shard_map.98 = (bf16[128,640]{1,0:T(8,128)(2,1)S(1)}, bf16[384,640]{1,0:T(8,128)(2,1)S(1)}, bf16[256,640]{1,0:T(8,128)(2,1)S(1)}) custom-call(s32[3]{0:T(128)S(1)} %get-tuple-element.40.refs_0_, s32[1]{0:T(128)} %bitcast.refs_0_.refs_1_, bf16[144,640]{1,0:T(8,128)(2,1)S(1)} %get-tuple-element.56.refs_2_, ...), custom_call_target="tpu_custom_call" | custom-call | flops 327680 | bytes 1925120 | tf_op jit(solution)/shard_map/pallas_call | solution.py:463
  23.5 1.6 %collective-permute-start.8 = (bf16[256,640]{1,0:T(8,128)(2,1)S(1)}, bf16[256,640]{1,0:T(8,128)(2,1)S(1)}, u32[]{:S(2)}, u32[]{:S(2)}) collective-permute-start(bf16[256,640]{1,0:T(8,128)(2,1)S(1)} %get-tuple-element.68), channel_id=1, source_target_pairs={{0,8},{4,12},{8,0},{12,4},{16,24},{20,28},{24,16},{28,20},{1,9},{5... | collective-permute-start | bytes 983048 | tf_op jit(solution)/shard_map/ppermute | solution.py:509
  25.1 1.6 %collective-permute-start.4 = (bf16[384,640]{1,0:T(8,128)(2,1)S(1)}, bf16[384,640]{1,0:T(8,128)(2,1)S(1)}, u32[]{:S(2)}, u32[]{:S(2)}) collective-permute-start(bf16[384,640]{1,0:T(8,128)(2,1)S(1)} %get-tuple-element.63), channel_id=1, source_target_pairs={{0,4},{4,0},{8,12},{12,8},{16,20},{20,16},{24,28},{28,24},{1,5},{5... | collective-permute-start | bytes 1474568 | tf_op jit(solution)/shard_map/ppermute | solution.py:509
  26.7 1.8 %shard_map.94.refs_2_ = f32[256,640]{1,0:T(8,128)S(1)} custom-call(s32[3]{0:T(128)S(1)} %get-tuple-element.40.refs_0_, s32[1]{0:T(128)} %bitcast.refs_0_.refs_1_, bf16[256,2560]{1,0:T(8,128)(2,1)S(1)} %get-tuple-element.50.refs_2_, bf16[16,2560]{1,0:T(8,128)(2,1)S(1)} %get-tuple-element.51.refs_3_, f32[256,256]{1,0:T(8,128)S(1)} %get-tuple-element.52.refs_4_, ...), custom_call_target="tpu_custom_call" | custom-call | flops 83886080 | bytes 3367072 | tf_op jit(solution)/shard_map/pallas_call | solution.py:463
  28.5 1.5 %collective-permute-start.6 = (bf16[128,640]{1,0:T(8,128)(2,1)S(1)}, bf16[128,640]{1,0:T(8,128)(2,1)S(1)}, u32[]{:S(2)}, u32[]{:S(2)}) collective-permute-start(bf16[128,640]{1,0:T(8,128)(2,1)S(1)} %get-tuple-element.62.refs_8_.refs_9_), channel_id=1, source_target_pairs={{0,16},{4,20},{8,24},{12,28},{16,0},{20,4},{24,8},{28,12},{1,17},{... | collective-permute-start | bytes 491528 | tf_op jit(solution)/shard_map/ppermute | solution.py:509
  29.9 3.8 %collective-permute-start.5 = (bf16[128,640]{1,0:T(8,128)(2,1)S(1)}, bf16[128,640]{1,0:T(8,128)(2,1)S(1)}, u32[]{:S(2)}, u32[]{:S(2)}) collective-permute-start(bf16[128,640]{1,0:T(8,128)(2,1)S(1)} %get-tuple-element.64.refs_7_), channel_id=1, source_target_pairs={{0,12},{4,8},{16,28},{20,24},{1,13},{5,9},{17,29},{21,25},{2,14},{... | collective-permute-start | bytes 491528 | tf_op jit(solution)/shard_map/ppermute | solution.py:509
  33.7 1.7 %shard_map.99.refs_2_ = f32[256,640]{1,0:T(8,128)S(1)} custom-call(s32[3]{0:T(128)S(1)} %get-tuple-element.40.refs_0_, s32[1]{0:T(128)} %bitcast.refs_0_.refs_1_, bf16[256,2560]{1,0:T(8,128)(2,1)S(1)} %get-tuple-element.50.refs_2_, bf16[16,2560]{1,0:T(8,128)(2,1)S(1)} %get-tuple-element.51.refs_3_, f32[256,256]{1,0:T(8,128)S(1)} %get-tuple-element.52.refs_4_, ...), custom_call_target="tpu_custom_call" | custom-call | flops 83886080 | bytes 3367072 | tf_op jit(solution)/shard_map/pallas_call | solution.py:463
  35.5 1.3 %shard_map.100 = (f32[256,640]{1,0:T(8,128)S(1)}, f32[256,640]{1,0:T(8,128)S(1)}) custom-call(s32[3]{0:T(128)S(1)} %get-tuple-element.40.refs_0_, s32[1]{0:T(128)} %bitcast.refs_0_.refs_1_, f32[256,640]{1,0:T(8,128)S(1)} %shard_map.95.refs_6_.refs_2_, bf16[256,128]{1,0:T(8,128)(2,1)S(1)} %get-tuple-element.49.refs_3_.refs_2_, ...), custom_call_target="tpu_custom_call" | custom-call | flops 2200000000 | bytes 4087808 | tf_op jit(solution)/shard_map/pallas_call | solution.py:463
  36.7 0.3 collective-permute-done.6.refs_12_
  37.1 2.0 %collective-permute-start.7 = (bf16[128,640]{1,0:T(8,128)(2,1)S(1)}, bf16[128,640]{1,0:T(8,128)(2,1)S(1)}, u32[]{:S(2)}, u32[]{:S(2)}) collective-permute-start(bf16[128,640]{1,0:T(8,128)(2,1)S(1)} %collective-permute-done.6.refs_12_), channel_id=1, source_target_pairs={{0,12},{4,8},{8,4},{12,0},{16,28},{20,24},{24,20},{28,16},{1,13},{... | collective-permute-start | bytes 491528 | tf_op jit(solution)/shard_map/ppermute | solution.py:509
  39.1 1.5 %collective-permute-start.10 = (bf16[128,640]{1,0:T(8,128)(2,1)S(1)}, bf16[128,640]{1,0:T(8,128)(2,1)S(1)}, u32[]{:S(2)}, u32[]{:S(2)}) collective-permute-start(bf16[128,640]{1,0:T(8,128)(2,1)S(1)} %collective-permute-done.6.refs_12_), channel_id=1, source_target_pairs={{0,8},{4,12},{8,0},{12,4},{16,24},{20,28},{24,16},{28,20},{1,9},{5... | collective-permute-start | bytes 491528 | tf_op jit(solution)/shard_map/ppermute | solution.py:509
  40.6 1.3 %shard_map.101 = (f32[256,640]{1,0:T(8,128)S(1)}, f32[256,640]{1,0:T(8,128)S(1)}) custom-call(s32[3]{0:T(128)S(1)} %get-tuple-element.40.refs_0_, s32[1]{0:T(128)} %bitcast.refs_0_.refs_1_, f32[256,640]{1,0:T(8,128)S(1)} %shard_map.99.refs_2_, bf16[256,128]{1,0:T(8,128)(2,1)S(1)} %get-tuple-element.49.refs_3_.refs_2_, ...), custom_call_target="tpu_custom_call" | custom-call | flops 2200000000 | bytes 4395008 | tf_op jit(solution)/shard_map/pallas_call | solution.py:463
  41.8 1.3 %shard_map.102 = (f32[256,640]{1,0:T(8,128)S(1)}, f32[256,640]{1,0:T(8,128)S(1)}) custom-call(s32[3]{0:T(128)S(1)} %get-tuple-element.40.refs_0_, s32[1]{0:T(128)} %bitcast.refs_0_.refs_1_, f32[256,640]{1,0:T(8,128)S(1)} %shard_map.96.refs_7_.refs_2_, bf16[256,128]{1,0:T(8,128)(2,1)S(1)} %get-tuple-element.49.refs_3_.refs_2_, ...), custom_call_target="tpu_custom_call" | custom-call | flops 2200000000 | bytes 4722688 | tf_op jit(solution)/shard_map/pallas_call | solution.py:463
  43.1 0.2 collective-permute-done.7.refs_9_
  43.4 1.6 %shard_map.103 = (f32[256,640]{1,0:T(8,128)S(1)}, f32[256,640]{1,0:T(8,128)S(1)}) custom-call(s32[3]{0:T(128)S(1)} %get-tuple-element.40.refs_0_, s32[1]{0:T(128)} %bitcast.refs_0_.refs_1_, f32[256,640]{1,0:T(8,128)S(1)} %shard_map.94.refs_2_, bf16[256,128]{1,0:T(8,128)(2,1)S(1)} %get-tuple-element.49.refs_3_.refs_2_, ...), custom_call_target="tpu_custom_call" | custom-call | flops 2200000000 | bytes 6033408 | tf_op jit(solution)/shard_map/pallas_call | solution.py:463
  44.9 0.1 collective-permute-done.9.refs_7_
  45.1 2.2 %shard_map.104 = bf16[256,2560]{1,0:T(8,128)(2,1)} custom-call(s32[3]{0:T(128)S(1)} %get-tuple-element.40.refs_0_, s32[1]{0:T(128)} %bitcast.refs_0_.refs_1_, bf16[256,128]{1,0:T(8,128)(2,1)S(1)} %get-tuple-element.49.refs_3_.refs_2_, f32[256,640]{1,0:T(8,128)S(1)} %get-tuple-element.71.refs_3_, f32[256,640]{1,0:T(8,128)S(1)} %get-tuple-element.72.refs_4_, ...), custom_call_target="tpu_custom_call" | custom-call | flops 167772160 | bytes 5646336 | tf_op jit(solution)/shard_map/pallas_call | solution.py:463
  (14 shorter events, 0.0 us)
Async XLA Ops:
  0.9 8.6 %collective-permute-start = (bf16[16,2816]{1,0:T(8,128)(2,1)S(1)}, bf16[16,2816]{1,0:T(8,128)(2,1)S(1)}, u32[]{:S(2)}, u32[]{:S(2)}) collective-permute-start(bf16[16,2816]{1,0:T(8,128)(2,1)S(1)} %slice.3), channel_id=1, source_target_pairs={{0,4},{4,8},{8,12},{12,16},{16,20},{20,24},{24,28},{1,5},{5,9},{9,... | collective-permute-start | bytes 270344 | tf_op jit(solution)/shard_map/ppermute | solution.py:509
  9.5 4.7 %copy-start = (f32[40,20,256]{2,0,1:T(8,128)S(1)}, f32[40,20,256]{2,0,1:T(8,128)}, u32[]{:S(2)}) copy-start(f32[40,20,256]{2,0,1:T(8,128)} %param.14) | copy-start | bytes 2457604
  9.5 5.4 %copy-start.1 = (f32[40]{0:T(128)S(1)}, f32[40]{0:T(128)}, u32[]{:S(2)}) copy-start(f32[40]{0:T(128)} %refs_8_.11) | copy-start | bytes 484
  10.6 7.9 %collective-permute-start.1 = (bf16[144,640]{1,0:T(8,128)(2,1)S(1)}, bf16[144,640]{1,0:T(8,128)(2,1)S(1)}, u32[]{:S(2)}, u32[]{:S(2)}) collective-permute-start(bf16[144,640]{1,0:T(8,128)(2,1)S(1)} %get-tuple-element.57), channel_id=1, source_target_pairs={{0,4},{4,0},{8,12},{12,8},{16,20},{20,16},{24,28},{28,24},{1,5},{5... | collective-permute-start | bytes 552968 | tf_op jit(solution)/shard_map/ppermute | solution.py:509
  12.2 7.6 %collective-permute-start.2 = (bf16[144,640]{1,0:T(8,128)(2,1)S(1)}, bf16[144,640]{1,0:T(8,128)(2,1)S(1)}, u32[]{:S(2)}, u32[]{:S(2)}) collective-permute-start(bf16[144,640]{1,0:T(8,128)(2,1)S(1)} %get-tuple-element.58.refs_7_), channel_id=1, source_target_pairs={{0,8},{4,12},{8,0},{12,4},{16,24},{20,28},{24,16},{28,20},{1,9},{5... | collective-permute-start | bytes 552968 | tf_op jit(solution)/shard_map/ppermute | solution.py:509
  13.8 8.1 %collective-permute-start.3 = (bf16[144,640]{1,0:T(8,128)(2,1)S(1)}, bf16[144,640]{1,0:T(8,128)(2,1)S(1)}, u32[]{:S(2)}, u32[]{:S(2)}) collective-permute-start(bf16[144,640]{1,0:T(8,128)(2,1)S(1)} %get-tuple-element.59), channel_id=1, source_target_pairs={{0,12},{4,8},{8,4},{12,0},{16,28},{20,24},{24,20},{28,16},{1,13},{... | collective-permute-start | bytes 552968 | tf_op jit(solution)/shard_map/ppermute | solution.py:509
  21.9 4.8 %copy-start.3 = (f32[2560]{0:T(1024)S(1)}, f32[2560]{0:T(1024)}, u32[]{:S(2)}) copy-start(f32[2560]{0:T(1024)} %param.16) | copy-start | bytes 30724
  23.5 15.6 %collective-permute-start.8 = (bf16[256,640]{1,0:T(8,128)(2,1)S(1)}, bf16[256,640]{1,0:T(8,128)(2,1)S(1)}, u32[]{:S(2)}, u32[]{:S(2)}) collective-permute-start(bf16[256,640]{1,0:T(8,128)(2,1)S(1)} %get-tuple-element.68), channel_id=1, source_target_pairs={{0,8},{4,12},{8,0},{12,4},{16,24},{20,28},{24,16},{28,20},{1,9},{5... | collective-permute-start | bytes 983048 | tf_op jit(solution)/shard_map/ppermute | solution.py:509
  25.1 16.7 %collective-permute-start.4 = (bf16[384,640]{1,0:T(8,128)(2,1)S(1)}, bf16[384,640]{1,0:T(8,128)(2,1)S(1)}, u32[]{:S(2)}, u32[]{:S(2)}) collective-permute-start(bf16[384,640]{1,0:T(8,128)(2,1)S(1)} %get-tuple-element.63), channel_id=1, source_target_pairs={{0,4},{4,0},{8,12},{12,8},{16,20},{20,16},{24,28},{28,24},{1,5},{5... | collective-permute-start | bytes 1474568 | tf_op jit(solution)/shard_map/ppermute | solution.py:509
  28.5 8.6 %collective-permute-start.6 = (bf16[128,640]{1,0:T(8,128)(2,1)S(1)}, bf16[128,640]{1,0:T(8,128)(2,1)S(1)}, u32[]{:S(2)}, u32[]{:S(2)}) collective-permute-start(bf16[128,640]{1,0:T(8,128)(2,1)S(1)} %get-tuple-element.62.refs_8_.refs_9_), channel_id=1, source_target_pairs={{0,16},{4,20},{8,24},{12,28},{16,0},{20,4},{24,8},{28,12},{1,17},{... | collective-permute-start | bytes 491528 | tf_op jit(solution)/shard_map/ppermute | solution.py:509
  29.9 5.5 %copy-start.2 = (bf16[256,2560]{1,0:T(8,128)(2,1)S(1)}, bf16[256,2560]{1,0:T(8,128)(2,1)}, u32[]{:S(2)}) copy-start(bf16[256,2560]{1,0:T(8,128)(2,1)} %refs_8_.15) | copy-start | bytes 3932164
  29.9 13.2 %collective-permute-start.5 = (bf16[128,640]{1,0:T(8,128)(2,1)S(1)}, bf16[128,640]{1,0:T(8,128)(2,1)S(1)}, u32[]{:S(2)}, u32[]{:S(2)}) collective-permute-start(bf16[128,640]{1,0:T(8,128)(2,1)S(1)} %get-tuple-element.64.refs_7_), channel_id=1, source_target_pairs={{0,12},{4,8},{16,28},{20,24},{1,13},{5,9},{17,29},{21,25},{2,14},{... | collective-permute-start | bytes 491528 | tf_op jit(solution)/shard_map/ppermute | solution.py:509
  37.1 6.3 %collective-permute-start.7 = (bf16[128,640]{1,0:T(8,128)(2,1)S(1)}, bf16[128,640]{1,0:T(8,128)(2,1)S(1)}, u32[]{:S(2)}, u32[]{:S(2)}) collective-permute-start(bf16[128,640]{1,0:T(8,128)(2,1)S(1)} %collective-permute-done.6.refs_12_), channel_id=1, source_target_pairs={{0,12},{4,8},{8,4},{12,0},{16,28},{20,24},{24,20},{28,16},{1,13},{... | collective-permute-start | bytes 491528 | tf_op jit(solution)/shard_map/ppermute | solution.py:509
  39.1 6.0 %collective-permute-start.9 = (bf16[128,640]{1,0:T(8,128)(2,1)S(1)}, bf16[128,640]{1,0:T(8,128)(2,1)S(1)}, u32[]{:S(2)}, u32[]{:S(2)}) collective-permute-start(bf16[128,640]{1,0:T(8,128)(2,1)S(1)} %collective-permute-done.6.refs_12_), channel_id=1, source_target_pairs={{0,4},{4,0},{8,12},{12,8},{16,20},{20,16},{24,28},{28,24},{1,5},{5... | collective-permute-start | bytes 491528 | tf_op jit(solution)/shard_map/ppermute | solution.py:509
  39.1 6.0 %collective-permute-start.10 = (bf16[128,640]{1,0:T(8,128)(2,1)S(1)}, bf16[128,640]{1,0:T(8,128)(2,1)S(1)}, u32[]{:S(2)}, u32[]{:S(2)}) collective-permute-start(bf16[128,640]{1,0:T(8,128)(2,1)S(1)} %collective-permute-done.6.refs_12_), channel_id=1, source_target_pairs={{0,8},{4,12},{8,0},{12,4},{16,24},{20,28},{24,16},{28,20},{1,9},{5... | collective-permute-start | bytes 491528 | tf_op jit(solution)/shard_map/ppermute | solution.py:509

commit v5 on v4

--- a/solution.py
+++ b/solution.py
@@ -512,7 +512,7 @@
         pairs = [(g, g ^ mask) for g in range(groups) if wanted(g, g ^ mask)]
         return send(value, pairs)
 
-    halo = send(mixed_input[tok - HALO :], [(g, g + 1) for g in range(groups - 1)])
+    halo = send(mixed_input[tok - HALO :], [(g, (g + 1) % groups) for g in range(groups)])
 
     def in_hbm(value):
         return pltpu.with_memory_space_constraint(value, pltpu.HBM)

time: 47.6 us -> 45.9 us (0.964)
  starting transfers between devices: 20.3 us -> 16.8 us
  waiting for transfers between devices: 4.08 us -> 5.71 us
    ppermute x11, starting transfers between devices: 20.3 us -> 16.8 us  [send(): return lax.ppermute(value, 'group', pairs)]
    ppermute x11, waiting for transfers between devices: 4.08 us -> 5.71 us  [send(): return lax.ppermute(value, 'group', pairs)]
  transfers between devices with their start and end apart: 11 -> 11, of which waited for: 5 -> 5; matrix products, arithmetic and copies ran while one was open for 0% -> 0% of each run, Pallas kernels for 36% -> 37%
where the time goes in v5:
time: 45.9 us; the launch traced here: 45.5 us
  Pallas kernels  21.7 us (47%)
  starting transfers between devices  16.8 us (37%)
  waiting for transfers between devices  5.71 us (12%)
  local copies, waits for them, and re-layouts  0.92 us (2%)
    pallas_call x14, Pallas kernels, call(): pl.pallas_call(body, grid=grid, in_specs=[SMEM] * len(scalars) + specs +...  21.7 us
    ppermute x11, starting transfers between devices, send(): return lax.ppermute(value, 'group', pairs)  16.8 us
    ppermute x11, waiting for transfers between devices, send(): return lax.ppermute(value, 'group', pairs)  5.71 us
  transfers between devices with their start and end apart: 11, of which 5 were waited for; matrix products, arithmetic and copies ran while one was open for 0% of the time, Pallas kernels for 37%

profile of v5, /device:TPU:0, one launch (start us, length us, event | category | flops | bytes accessed | tf_op | source)
XLA Modules:
  0.0 45.5 jit_solution(16147316123730448095)
XLA Ops:
  0.0 0.9 %slice.3 = bf16[16,2816]{1,0:T(8,128)(2,1)S(1)} slice(bf16[256,2816]{1,0:T(8,128)(2,1)} %refs_1_.1), slice={[240:256], [0:2816]} | slice | bytes 180224 | tf_op jit(solution)/shard_map/slice | solution.py:515
  0.9 2.9 %collective-permute-start = (bf16[16,2816]{1,0:T(8,128)(2,1)S(1)}, bf16[16,2816]{1,0:T(8,128)(2,1)S(1)}, u32[]{:S(2)}, u32[]{:S(2)}) collective-permute-start(bf16[16,2816]{1,0:T(8,128)(2,1)S(1)} %slice.3), channel_id=1, source_target_pairs={{0,4},{4,8},{8,12},{12,16},{16,20},{20,24},{24,28},{28,0},{1,5},{5... | collective-permute-start | bytes 270344 | tf_op jit(solution)/shard_map/ppermute | solution.py:509
  3.8 3.7 %shard_map.91 = (bf16[256,2560]{1,0:T(8,128)(2,1)S(1)}, bf16[256,256]{1,0:T(8,128)(2,1)S(1)}, f32[128,2560]{1,0:T(8,128)S(1)}, f32[40,256]{1,0:T(8,128)S(1)}, f3...) custom-call(s32[1]{0:T(128)} %bitcast.refs_0_.refs_1_, ...), custom_call_target="tpu_custom_call" | custom-call | flops 167772160 | bytes 4848664 | tf_op jit(solution)/shard_map/pallas_call | solution.py:463
  7.6 0.0 copy-start
  7.6 1.9 %collective-permute-done.refs_2_ = bf16[16,2816]{1,0:T(8,128)(2,1)S(1)} collective-permute-done((bf16[16,2816]{1,0:T(8,128)(2,1)S(1)}, bf16[16,2816]{1,0:T(8,128)(2,1)S(1)}, u32[]{:S(2)}, u32[]{:S(2)}) %collective-permute-start) | collective-permute-done | bytes 90144 | tf_op jit(solution)/shard_map/ppermute | solution.py:509
  9.5 1.0 %shard_map.92 = (bf16[16,2560]{1,0:T(8,128)(2,1)S(1)}, bf16[16,256]{1,0:T(8,128)(2,1)S(1)}, bf16[144,640]{1,0:T(8,128)(2,1)S(1)}, bf16[144,640]{1,0:T(8,128)(2,1...) custom-call(s32[3]{0:T(128)S(1)} %get-tuple-element.40.refs_0_, s32[1]{0:T(128)} %bitcast.refs_0_.refs_1_, ...), custom_call_target="tpu_custom_call" | custom-call | flops 10485760 | bytes 2703360 | tf_op jit(solution)/shard_map/pallas_call | solution.py:463
  10.5 0.1 collective-permute-start.1
  10.6 1.2 %collective-permute-start.2 = (bf16[144,640]{1,0:T(8,128)(2,1)S(1)}, bf16[144,640]{1,0:T(8,128)(2,1)S(1)}, u32[]{:S(2)}, u32[]{:S(2)}) collective-permute-start(bf16[144,640]{1,0:T(8,128)(2,1)S(1)} %get-tuple-element.58.refs_7_), channel_id=1, source_target_pairs={{0,8},{4,12},{8,0},{12,4},{16,24},{20,28},{24,16},{28,20},{1,9},{5... | collective-permute-start | bytes 552968 | tf_op jit(solution)/shard_map/ppermute | solution.py:509
  11.9 2.2 %collective-permute-start.3 = (bf16[144,640]{1,0:T(8,128)(2,1)S(1)}, bf16[144,640]{1,0:T(8,128)(2,1)S(1)}, u32[]{:S(2)}, u32[]{:S(2)}) collective-permute-start(bf16[144,640]{1,0:T(8,128)(2,1)S(1)} %get-tuple-element.59), channel_id=1, source_target_pairs={{0,12},{4,8},{8,4},{12,0},{16,28},{20,24},{24,20},{28,16},{1,13},{... | collective-permute-start | bytes 552968 | tf_op jit(solution)/shard_map/ppermute | solution.py:509
  14.1 0.8 %shard_map.93 = (bf16[256,128]{1,0:T(8,128)(2,1)S(1)}, f32[256,256]{1,0:T(8,128)S(1)}, bf16[256,384]{1,0:T(8,128)(2,1)S(1)}, f32[3,256,128]{2,1,0:T(8,128)S(1)}) custom-call(s32[3]{0:T(128)S(1)} %get-tuple-element.40.refs_0_, s32[1]{0:T(128)} %bitcast.refs_0_.refs_1_, bf16[256,256]{1,0:T(8,128)(2,1)S(1)} %get-tuple-element.41.refs_2_, ...), custom_call_target="tpu_custom_call" | custom-call | flops 16777216 | bytes 2048000 | tf_op jit(solution)/shard_map/pallas_call | solution.py:463
  14.9 1.8 %shard_map.95.refs_6_.refs_2_ = f32[256,640]{1,0:T(8,128)S(1)} custom-call(s32[3]{0:T(128)S(1)} %get-tuple-element.40.refs_0_, s32[1]{0:T(128)} %bitcast.refs_0_.refs_1_, bf16[256,2560]{1,0:T(8,128)(2,1)S(1)} %get-tuple-element.50.refs_2_, bf16[16,2560]{1,0:T(8,128)(2,1)S(1)} %get-tuple-element.51.refs_3_, f32[256,256]{1,0:T(8,128)S(1)} %get-tuple-element.52.refs_4_, ...), custom_call_target="tpu_custom_call" | custom-call | flops 83886080 | bytes 3367072 | tf_op jit(solution)/shard_map/pallas_call | solution.py:463
  16.7 1.8 %shard_map.96.refs_7_.refs_2_ = f32[256,640]{1,0:T(8,128)S(1)} custom-call(s32[3]{0:T(128)S(1)} %get-tuple-element.40.refs_0_, s32[1]{0:T(128)} %bitcast.refs_0_.refs_1_, bf16[256,2560]{1,0:T(8,128)(2,1)S(1)} %get-tuple-element.50.refs_2_, bf16[16,2560]{1,0:T(8,128)(2,1)S(1)} %get-tuple-element.51.refs_3_, f32[256,256]{1,0:T(8,128)S(1)} %get-tuple-element.52.refs_4_, ...), custom_call_target="tpu_custom_call" | custom-call | flops 83886080 | bytes 3367072 | tf_op jit(solution)/shard_map/pallas_call | solution.py:463
  18.4 3.1 %collective-permute-done.3.refs_5_ = bf16[144,640]{1,0:T(8,128)(2,1)S(1)} collective-permute-done((bf16[144,640]{1,0:T(8,128)(2,1)S(1)}, bf16[144,640]{1,0:T(8,128)(2,1)S(1)}, u32[]{:S(2)}, u32[]{:S(2)}) %collective-permute-start.3) | collective-permute-done | bytes 184352 | tf_op jit(solution)/shard_map/ppermute | solution.py:509
  21.6 0.9 %shard_map.97 = (bf16[128,640]{1,0:T(8,128)(2,1)S(1)}, f32[8,128]{1,0:T(8,128)S(1)}, f32[8,640]{1,0:T(8,128)S(1)}) custom-call(s32[3]{0:T(128)S(1)} %get-tuple-element.40.refs_0_, s32[1]{0:T(128)} %bitcast.refs_0_.refs_1_, bf16[144,640]{1,0:T(8,128)(2,1)S(1)} %get-tuple-element.56.refs_2_, bf16[144,640]{1,0:T(8,128)(2,1)S(1)} %collective-permute-done.1.refs_3_.refs_6_, ...), custom_call_target="tpu_custom_call" | custom-call | flops 327680 | bytes 925696 | tf_op jit(solution)/shard_map/pallas_call | solution.py:463
  22.4 0.7 %shard_map.98 = (bf16[128,640]{1,0:T(8,128)(2,1)S(1)}, bf16[384,640]{1,0:T(8,128)(2,1)S(1)}, bf16[256,640]{1,0:T(8,128)(2,1)S(1)}) custom-call(s32[3]{0:T(128)S(1)} %get-tuple-element.40.refs_0_, s32[1]{0:T(128)} %bitcast.refs_0_.refs_1_, bf16[144,640]{1,0:T(8,128)(2,1)S(1)} %get-tuple-element.56.refs_2_, ...), custom_call_target="tpu_custom_call" | custom-call | flops 327680 | bytes 1925120 | tf_op jit(solution)/shard_map/pallas_call | solution.py:463
  23.2 0.3 collective-permute-start.8
  23.5 1.2 %collective-permute-start.4 = (bf16[384,640]{1,0:T(8,128)(2,1)S(1)}, bf16[384,640]{1,0:T(8,128)(2,1)S(1)}, u32[]{:S(2)}, u32[]{:S(2)}) collective-permute-start(bf16[384,640]{1,0:T(8,128)(2,1)S(1)} %get-tuple-element.63), channel_id=1, source_target_pairs={{0,4},{4,0},{8,12},{12,8},{16,20},{20,16},{24,28},{28,24},{1,5},{5... | collective-permute-start | bytes 1474568 | tf_op jit(solution)/shard_map/ppermute | solution.py:509
  24.8 1.8 %shard_map.94.refs_2_ = f32[256,640]{1,0:T(8,128)S(1)} custom-call(s32[3]{0:T(128)S(1)} %get-tuple-element.40.refs_0_, s32[1]{0:T(128)} %bitcast.refs_0_.refs_1_, bf16[256,2560]{1,0:T(8,128)(2,1)S(1)} %get-tuple-element.50.refs_2_, bf16[16,2560]{1,0:T(8,128)(2,1)S(1)} %get-tuple-element.51.refs_3_, f32[256,256]{1,0:T(8,128)S(1)} %get-tuple-element.52.refs_4_, ...), custom_call_target="tpu_custom_call" | custom-call | flops 83886080 | bytes 3367072 | tf_op jit(solution)/shard_map/pallas_call | solution.py:463
  26.5 1.5 %collective-permute-start.6 = (bf16[128,640]{1,0:T(8,128)(2,1)S(1)}, bf16[128,640]{1,0:T(8,128)(2,1)S(1)}, u32[]{:S(2)}, u32[]{:S(2)}) collective-permute-start(bf16[128,640]{1,0:T(8,128)(2,1)S(1)} %get-tuple-element.62.refs_8_.refs_9_), channel_id=1, source_target_pairs={{0,16},{4,20},{8,24},{12,28},{16,0},{20,4},{24,8},{28,12},{1,17},{... | collective-permute-start | bytes 491528 | tf_op jit(solution)/shard_map/ppermute | solution.py:509
  28.0 3.8 %collective-permute-start.5 = (bf16[128,640]{1,0:T(8,128)(2,1)S(1)}, bf16[128,640]{1,0:T(8,128)(2,1)S(1)}, u32[]{:S(2)}, u32[]{:S(2)}) collective-permute-start(bf16[128,640]{1,0:T(8,128)(2,1)S(1)} %get-tuple-element.64.refs_7_), channel_id=1, source_target_pairs={{0,12},{4,8},{16,28},{20,24},{1,13},{5,9},{17,29},{21,25},{2,14},{... | collective-permute-start | bytes 491528 | tf_op jit(solution)/shard_map/ppermute | solution.py:509
  31.8 1.7 %shard_map.99.refs_2_ = f32[256,640]{1,0:T(8,128)S(1)} custom-call(s32[3]{0:T(128)S(1)} %get-tuple-element.40.refs_0_, s32[1]{0:T(128)} %bitcast.refs_0_.refs_1_, bf16[256,2560]{1,0:T(8,128)(2,1)S(1)} %get-tuple-element.50.refs_2_, bf16[16,2560]{1,0:T(8,128)(2,1)S(1)} %get-tuple-element.51.refs_3_, f32[256,256]{1,0:T(8,128)S(1)} %get-tuple-element.52.refs_4_, ...), custom_call_target="tpu_custom_call" | custom-call | flops 83886080 | bytes 3367072 | tf_op jit(solution)/shard_map/pallas_call | solution.py:463
  33.5 1.3 %shard_map.100 = (f32[256,640]{1,0:T(8,128)S(1)}, f32[256,640]{1,0:T(8,128)S(1)}) custom-call(s32[3]{0:T(128)S(1)} %get-tuple-element.40.refs_0_, s32[1]{0:T(128)} %bitcast.refs_0_.refs_1_, f32[256,640]{1,0:T(8,128)S(1)} %shard_map.95.refs_6_.refs_2_, bf16[256,128]{1,0:T(8,128)(2,1)S(1)} %get-tuple-element.49.refs_3_.refs_2_, ...), custom_call_target="tpu_custom_call" | custom-call | flops 2200000000 | bytes 4087808 | tf_op jit(solution)/shard_map/pallas_call | solution.py:463
  34.8 0.3 collective-permute-done.6.refs_12_
  35.2 1.5 %collective-permute-start.7 = (bf16[128,640]{1,0:T(8,128)(2,1)S(1)}, bf16[128,640]{1,0:T(8,128)(2,1)S(1)}, u32[]{:S(2)}, u32[]{:S(2)}) collective-permute-start(bf16[128,640]{1,0:T(8,128)(2,1)S(1)} %collective-permute-done.6.refs_12_), channel_id=1, source_target_pairs={{0,12},{4,8},{8,4},{12,0},{16,28},{20,24},{24,20},{28,16},{1,13},{... | collective-permute-start | bytes 491528 | tf_op jit(solution)/shard_map/ppermute | solution.py:509
  36.7 0.5 collective-permute-start.9
  37.1 1.5 %collective-permute-start.10 = (bf16[128,640]{1,0:T(8,128)(2,1)S(1)}, bf16[128,640]{1,0:T(8,128)(2,1)S(1)}, u32[]{:S(2)}, u32[]{:S(2)}) collective-permute-start(bf16[128,640]{1,0:T(8,128)(2,1)S(1)} %collective-permute-done.6.refs_12_), channel_id=1, source_target_pairs={{0,8},{4,12},{8,0},{12,4},{16,24},{20,28},{24,16},{28,20},{1,9},{5... | collective-permute-start | bytes 491528 | tf_op jit(solution)/shard_map/ppermute | solution.py:509
  38.7 1.3 %shard_map.101 = (f32[256,640]{1,0:T(8,128)S(1)}, f32[256,640]{1,0:T(8,128)S(1)}) custom-call(s32[3]{0:T(128)S(1)} %get-tuple-element.40.refs_0_, s32[1]{0:T(128)} %bitcast.refs_0_.refs_1_, f32[256,640]{1,0:T(8,128)S(1)} %shard_map.99.refs_2_, bf16[256,128]{1,0:T(8,128)(2,1)S(1)} %get-tuple-element.49.refs_3_.refs_2_, ...), custom_call_target="tpu_custom_call" | custom-call | flops 2200000000 | bytes 4395008 | tf_op jit(solution)/shard_map/pallas_call | solution.py:463
  40.0 1.3 %shard_map.102 = (f32[256,640]{1,0:T(8,128)S(1)}, f32[256,640]{1,0:T(8,128)S(1)}) custom-call(s32[3]{0:T(128)S(1)} %get-tuple-element.40.refs_0_, s32[1]{0:T(128)} %bitcast.refs_0_.refs_1_, f32[256,640]{1,0:T(8,128)S(1)} %shard_map.96.refs_7_.refs_2_, bf16[256,128]{1,0:T(8,128)(2,1)S(1)} %get-tuple-element.49.refs_3_.refs_2_, ...), custom_call_target="tpu_custom_call" | custom-call | flops 2200000000 | bytes 4722688 | tf_op jit(solution)/shard_map/pallas_call | solution.py:463
  41.2 0.3 collective-permute-done.7.refs_9_
  41.5 1.6 %shard_map.103 = (f32[256,640]{1,0:T(8,128)S(1)}, f32[256,640]{1,0:T(8,128)S(1)}) custom-call(s32[3]{0:T(128)S(1)} %get-tuple-element.40.refs_0_, s32[1]{0:T(128)} %bitcast.refs_0_.refs_1_, f32[256,640]{1,0:T(8,128)S(1)} %shard_map.94.refs_2_, bf16[256,128]{1,0:T(8,128)(2,1)S(1)} %get-tuple-element.49.refs_3_.refs_2_, ...), custom_call_target="tpu_custom_call" | custom-call | flops 2200000000 | bytes 6033408 | tf_op jit(solution)/shard_map/pallas_call | solution.py:463
  43.1 0.1 collective-permute-done.9.refs_7_
  43.2 2.2 %shard_map.104 = bf16[256,2560]{1,0:T(8,128)(2,1)} custom-call(s32[3]{0:T(128)S(1)} %get-tuple-element.40.refs_0_, s32[1]{0:T(128)} %bitcast.refs_0_.refs_1_, bf16[256,128]{1,0:T(8,128)(2,1)S(1)} %get-tuple-element.49.refs_3_.refs_2_, f32[256,640]{1,0:T(8,128)S(1)} %get-tuple-element.71.refs_3_, f32[256,640]{1,0:T(8,128)S(1)} %get-tuple-element.72.refs_4_, ...), custom_call_target="tpu_custom_call" | custom-call | flops 167772160 | bytes 5646336 | tf_op jit(solution)/shard_map/pallas_call | solution.py:463
  (14 shorter events, 0.0 us)
Async XLA Ops:
  0.9 8.6 %collective-permute-start = (bf16[16,2816]{1,0:T(8,128)(2,1)S(1)}, bf16[16,2816]{1,0:T(8,128)(2,1)S(1)}, u32[]{:S(2)}, u32[]{:S(2)}) collective-permute-start(bf16[16,2816]{1,0:T(8,128)(2,1)S(1)} %slice.3), channel_id=1, source_target_pairs={{0,4},{4,8},{8,12},{12,16},{16,20},{20,24},{24,28},{28,0},{1,5},{5... | collective-permute-start | bytes 270344 | tf_op jit(solution)/shard_map/ppermute | solution.py:509
  7.6 6.5 %copy-start = (f32[40,20,256]{2,0,1:T(8,128)S(1)}, f32[40,20,256]{2,0,1:T(8,128)}, u32[]{:S(2)}) copy-start(f32[40,20,256]{2,0,1:T(8,128)} %param.14) | copy-start | bytes 2457604
  9.5 5.4 %copy-start.1 = (f32[40]{0:T(128)S(1)}, f32[40]{0:T(128)}, u32[]{:S(2)}) copy-start(f32[40]{0:T(128)} %refs_8_.11) | copy-start | bytes 484
  10.5 7.9 %collective-permute-start.1 = (bf16[144,640]{1,0:T(8,128)(2,1)S(1)}, bf16[144,640]{1,0:T(8,128)(2,1)S(1)}, u32[]{:S(2)}, u32[]{:S(2)}) collective-permute-start(bf16[144,640]{1,0:T(8,128)(2,1)S(1)} %get-tuple-element.57), channel_id=1, source_target_pairs={{0,4},{4,0},{8,12},{12,8},{16,20},{20,16},{24,28},{28,24},{1,5},{5... | collective-permute-start | bytes 552968 | tf_op jit(solution)/shard_map/ppermute | solution.py:509
  10.6 7.8 %collective-permute-start.2 = (bf16[144,640]{1,0:T(8,128)(2,1)S(1)}, bf16[144,640]{1,0:T(8,128)(2,1)S(1)}, u32[]{:S(2)}, u32[]{:S(2)}) collective-permute-start(bf16[144,640]{1,0:T(8,128)(2,1)S(1)} %get-tuple-element.58.refs_7_), channel_id=1, source_target_pairs={{0,8},{4,12},{8,0},{12,4},{16,24},{20,28},{24,16},{28,20},{1,9},{5... | collective-permute-start | bytes 552968 | tf_op jit(solution)/shard_map/ppermute | solution.py:509
  11.9 9.7 %collective-permute-start.3 = (bf16[144,640]{1,0:T(8,128)(2,1)S(1)}, bf16[144,640]{1,0:T(8,128)(2,1)S(1)}, u32[]{:S(2)}, u32[]{:S(2)}) collective-permute-start(bf16[144,640]{1,0:T(8,128)(2,1)S(1)} %get-tuple-element.59), channel_id=1, source_target_pairs={{0,12},{4,8},{8,4},{12,0},{16,28},{20,24},{24,20},{28,16},{1,13},{... | collective-permute-start | bytes 552968 | tf_op jit(solution)/shard_map/ppermute | solution.py:509
  21.6 3.2 %copy-start.3 = (f32[2560]{0:T(1024)S(1)}, f32[2560]{0:T(1024)}, u32[]{:S(2)}) copy-start(f32[2560]{0:T(1024)} %param.16) | copy-start | bytes 30724
  23.2 14.0 %collective-permute-start.8 = (bf16[256,640]{1,0:T(8,128)(2,1)S(1)}, bf16[256,640]{1,0:T(8,128)(2,1)S(1)}, u32[]{:S(2)}, u32[]{:S(2)}) collective-permute-start(bf16[256,640]{1,0:T(8,128)(2,1)S(1)} %get-tuple-element.68), channel_id=1, source_target_pairs={{0,8},{4,12},{8,0},{12,4},{16,24},{20,28},{24,16},{28,20},{1,9},{5... | collective-permute-start | bytes 983048 | tf_op jit(solution)/shard_map/ppermute | solution.py:509
  23.5 16.4 %collective-permute-start.4 = (bf16[384,640]{1,0:T(8,128)(2,1)S(1)}, bf16[384,640]{1,0:T(8,128)(2,1)S(1)}, u32[]{:S(2)}, u32[]{:S(2)}) collective-permute-start(bf16[384,640]{1,0:T(8,128)(2,1)S(1)} %get-tuple-element.63), channel_id=1, source_target_pairs={{0,4},{4,0},{8,12},{12,8},{16,20},{20,16},{24,28},{28,24},{1,5},{5... | collective-permute-start | bytes 1474568 | tf_op jit(solution)/shard_map/ppermute | solution.py:509
  26.5 8.6 %collective-permute-start.6 = (bf16[128,640]{1,0:T(8,128)(2,1)S(1)}, bf16[128,640]{1,0:T(8,128)(2,1)S(1)}, u32[]{:S(2)}, u32[]{:S(2)}) collective-permute-start(bf16[128,640]{1,0:T(8,128)(2,1)S(1)} %get-tuple-element.62.refs_8_.refs_9_), channel_id=1, source_target_pairs={{0,16},{4,20},{8,24},{12,28},{16,0},{20,4},{24,8},{28,12},{1,17},{... | collective-permute-start | bytes 491528 | tf_op jit(solution)/shard_map/ppermute | solution.py:509
  28.0 5.5 %copy-start.2 = (bf16[256,2560]{1,0:T(8,128)(2,1)S(1)}, bf16[256,2560]{1,0:T(8,128)(2,1)}, u32[]{:S(2)}) copy-start(bf16[256,2560]{1,0:T(8,128)(2,1)} %refs_8_.15) | copy-start | bytes 3932164
  28.0 13.2 %collective-permute-start.5 = (bf16[128,640]{1,0:T(8,128)(2,1)S(1)}, bf16[128,640]{1,0:T(8,128)(2,1)S(1)}, u32[]{:S(2)}, u32[]{:S(2)}) collective-permute-start(bf16[128,640]{1,0:T(8,128)(2,1)S(1)} %get-tuple-element.64.refs_7_), channel_id=1, source_target_pairs={{0,12},{4,8},{16,28},{20,24},{1,13},{5,9},{17,29},{21,25},{2,14},{... | collective-permute-start | bytes 491528 | tf_op jit(solution)/shard_map/ppermute | solution.py:509
  35.2 6.3 %collective-permute-start.7 = (bf16[128,640]{1,0:T(8,128)(2,1)S(1)}, bf16[128,640]{1,0:T(8,128)(2,1)S(1)}, u32[]{:S(2)}, u32[]{:S(2)}) collective-permute-start(bf16[128,640]{1,0:T(8,128)(2,1)S(1)} %collective-permute-done.6.refs_12_), channel_id=1, source_target_pairs={{0,12},{4,8},{8,4},{12,0},{16,28},{20,24},{24,20},{28,16},{1,13},{... | collective-permute-start | bytes 491528 | tf_op jit(solution)/shard_map/ppermute | solution.py:509
  36.7 6.5 %collective-permute-start.9 = (bf16[128,640]{1,0:T(8,128)(2,1)S(1)}, bf16[128,640]{1,0:T(8,128)(2,1)S(1)}, u32[]{:S(2)}, u32[]{:S(2)}) collective-permute-start(bf16[128,640]{1,0:T(8,128)(2,1)S(1)} %collective-permute-done.6.refs_12_), channel_id=1, source_target_pairs={{0,4},{4,0},{8,12},{12,8},{16,20},{20,16},{24,28},{28,24},{1,5},{5... | collective-permute-start | bytes 491528 | tf_op jit(solution)/shard_map/ppermute | solution.py:509
  37.1 6.0 %collective-permute-start.10 = (bf16[128,640]{1,0:T(8,128)(2,1)S(1)}, bf16[128,640]{1,0:T(8,128)(2,1)S(1)}, u32[]{:S(2)}, u32[]{:S(2)}) collective-permute-start(bf16[128,640]{1,0:T(8,128)(2,1)S(1)} %collective-permute-done.6.refs_12_), channel_id=1, source_target_pairs={{0,8},{4,12},{8,0},{12,4},{16,24},{20,28},{24,16},{28,20},{1,9},{5... | collective-permute-start | bytes 491528 | tf_op jit(solution)/shard_map/ppermute | solution.py:509

commit v6 on v5

--- a/solution.py
+++ b/solution.py
@@ -25,8 +25,12 @@
     )
 
 
+def silu_of_half(h):
+    return h * jnp.tanh(h) + h
+
+
 def silu(v):
-    return v * (0.5 * jnp.tanh(0.5 * v) + 0.5)
+    return silu_of_half(0.5 * v)
 
 
 def segment_bounds(lengths, recordings):
@@ -68,7 +72,7 @@
     total = weight_ref[taps : taps + 1, lo:hi]
     for tap, piece in enumerate(shifts):
         total = total + weight_ref[tap : tap + 1, lo:hi] * piece
-    return silu(total)
+    return silu_of_half(total)
 
 
 def features_kernel(
@@ -124,6 +128,7 @@
     for fetch in fetches[2:]:
         fetch.wait()
 
+    weight_ref[: taps + 1] = 0.5 * weight_ref[: taps + 1]
     head_ref[...] = x_ref[:HALO]
     keys = None
     for at in [width // block] + list(range(width // block)):
@@ -239,8 +244,10 @@
     weights = jnp.concatenate(rows, axis=0)
     high, low = two_parts(weights)
     copies = spread(LANES, place * (cols // head_dim), cols, head_dim)
-    weights = dot(high.astype(bf16), copies, ((1,), (0,))) + dot(
-        low.astype(bf16), copies, ((1,), (0,))
+    weights = dot(
+        jnp.concatenate([high, low], axis=1).astype(bf16),
+        jnp.concatenate([copies, copies], axis=0),
+        ((1,), (0,)),
     )
     weight_ref[...] = weights
     for lo in range(0, cols, LANES):

time: 45.9 us -> 45.9 us (level)
  no operation moved by 1% of the time
where the time goes in v6:
time: 45.9 us; the launch traced here: 45.4 us
  Pallas kernels  21.5 us (47%)
  starting transfers between devices  16.7 us (36%)
  waiting for transfers between devices  5.95 us (13%)
  local copies, waits for them, and re-layouts  0.92 us (2%)
    pallas_call x14, Pallas kernels, call(): pl.pallas_call(body, grid=grid, in_specs=[SMEM] * len(scalars) + specs +...  21.5 us
    ppermute x11, starting transfers between devices, send(): return lax.ppermute(value, 'group', pairs)  16.7 us
    ppermute x11, waiting for transfers between devices, send(): return lax.ppermute(value, 'group', pairs)  5.95 us
  transfers between devices with their start and end apart: 11, of which 5 were waited for; matrix products, arithmetic and copies ran while one was open for 0% of the time, Pallas kernels for 37%

profile of v6, /device:TPU:0, one launch (start us, length us, event | category | flops | bytes accessed | tf_op | source)
XLA Modules:
  0.0 45.4 jit_solution(14226254569508833102)
XLA Ops:
  0.0 0.9 %slice.3 = bf16[16,2816]{1,0:T(8,128)(2,1)S(1)} slice(bf16[256,2816]{1,0:T(8,128)(2,1)} %refs_1_.1), slice={[240:256], [0:2816]} | slice | bytes 180224 | tf_op jit(solution)/shard_map/slice | solution.py:522
  0.9 2.9 %collective-permute-start = (bf16[16,2816]{1,0:T(8,128)(2,1)S(1)}, bf16[16,2816]{1,0:T(8,128)(2,1)S(1)}, u32[]{:S(2)}, u32[]{:S(2)}) collective-permute-start(bf16[16,2816]{1,0:T(8,128)(2,1)S(1)} %slice.3), channel_id=1, source_target_pairs={{0,4},{4,8},{8,12},{12,16},{16,20},{20,24},{24,28},{28,0},{1,5},{5... | collective-permute-start | bytes 270344 | tf_op jit(solution)/shard_map/ppermute | solution.py:516
  3.8 3.6 %shard_map.91 = (bf16[256,2560]{1,0:T(8,128)(2,1)S(1)}, bf16[256,256]{1,0:T(8,128)(2,1)S(1)}, f32[128,2560]{1,0:T(8,128)S(1)}, f32[40,256]{1,0:T(8,128)S(1)}, f3...) custom-call(s32[1]{0:T(128)} %bitcast.refs_0_.refs_1_, ...), custom_call_target="tpu_custom_call" | custom-call | flops 167772160 | bytes 4848664 | tf_op jit(solution)/shard_map/pallas_call | solution.py:470
  7.5 0.0 copy-start
  7.5 2.0 %collective-permute-done.refs_2_ = bf16[16,2816]{1,0:T(8,128)(2,1)S(1)} collective-permute-done((bf16[16,2816]{1,0:T(8,128)(2,1)S(1)}, bf16[16,2816]{1,0:T(8,128)(2,1)S(1)}, u32[]{:S(2)}, u32[]{:S(2)}) %collective-permute-start) | collective-permute-done | bytes 90144 | tf_op jit(solution)/shard_map/ppermute | solution.py:516
  9.5 1.0 %shard_map.92 = (bf16[16,2560]{1,0:T(8,128)(2,1)S(1)}, bf16[16,256]{1,0:T(8,128)(2,1)S(1)}, bf16[144,640]{1,0:T(8,128)(2,1)S(1)}, bf16[144,640]{1,0:T(8,128)(2,1...) custom-call(s32[3]{0:T(128)S(1)} %get-tuple-element.40.refs_0_, s32[1]{0:T(128)} %bitcast.refs_0_.refs_1_, ...), custom_call_target="tpu_custom_call" | custom-call | flops 10485760 | bytes 2703360 | tf_op jit(solution)/shard_map/pallas_call | solution.py:470
  10.5 0.1 collective-permute-start.1
  10.6 1.1 %collective-permute-start.2 = (bf16[144,640]{1,0:T(8,128)(2,1)S(1)}, bf16[144,640]{1,0:T(8,128)(2,1)S(1)}, u32[]{:S(2)}, u32[]{:S(2)}) collective-permute-start(bf16[144,640]{1,0:T(8,128)(2,1)S(1)} %get-tuple-element.58.refs_7_), channel_id=1, source_target_pairs={{0,8},{4,12},{8,0},{12,4},{16,24},{20,28},{24,16},{28,20},{1,9},{5... | collective-permute-start | bytes 552968 | tf_op jit(solution)/shard_map/ppermute | solution.py:516
  11.7 2.4 %collective-permute-start.3 = (bf16[144,640]{1,0:T(8,128)(2,1)S(1)}, bf16[144,640]{1,0:T(8,128)(2,1)S(1)}, u32[]{:S(2)}, u32[]{:S(2)}) collective-permute-start(bf16[144,640]{1,0:T(8,128)(2,1)S(1)} %get-tuple-element.59), channel_id=1, source_target_pairs={{0,12},{4,8},{8,4},{12,0},{16,28},{20,24},{24,20},{28,16},{1,13},{... | collective-permute-start | bytes 552968 | tf_op jit(solution)/shard_map/ppermute | solution.py:516
  14.1 0.8 %shard_map.93 = (bf16[256,128]{1,0:T(8,128)(2,1)S(1)}, f32[256,256]{1,0:T(8,128)S(1)}, bf16[256,384]{1,0:T(8,128)(2,1)S(1)}, f32[3,256,128]{2,1,0:T(8,128)S(1)}) custom-call(s32[3]{0:T(128)S(1)} %get-tuple-element.40.refs_0_, s32[1]{0:T(128)} %bitcast.refs_0_.refs_1_, bf16[256,256]{1,0:T(8,128)(2,1)S(1)} %get-tuple-element.41.refs_2_, ...), custom_call_target="tpu_custom_call" | custom-call | flops 16777216 | bytes 2048000 | tf_op jit(solution)/shard_map/pallas_call | solution.py:470
  14.9 1.8 %shard_map.95.refs_6_.refs_2_ = f32[256,640]{1,0:T(8,128)S(1)} custom-call(s32[3]{0:T(128)S(1)} %get-tuple-element.40.refs_0_, s32[1]{0:T(128)} %bitcast.refs_0_.refs_1_, bf16[256,2560]{1,0:T(8,128)(2,1)S(1)} %get-tuple-element.50.refs_2_, bf16[16,2560]{1,0:T(8,128)(2,1)S(1)} %get-tuple-element.51.refs_3_, f32[256,256]{1,0:T(8,128)S(1)} %get-tuple-element.52.refs_4_, ...), custom_call_target="tpu_custom_call" | custom-call | flops 83886080 | bytes 3367072 | tf_op jit(solution)/shard_map/pallas_call | solution.py:470
  16.6 1.8 %shard_map.96.refs_7_.refs_2_ = f32[256,640]{1,0:T(8,128)S(1)} custom-call(s32[3]{0:T(128)S(1)} %get-tuple-element.40.refs_0_, s32[1]{0:T(128)} %bitcast.refs_0_.refs_1_, bf16[256,2560]{1,0:T(8,128)(2,1)S(1)} %get-tuple-element.50.refs_2_, bf16[16,2560]{1,0:T(8,128)(2,1)S(1)} %get-tuple-element.51.refs_3_, f32[256,256]{1,0:T(8,128)S(1)} %get-tuple-element.52.refs_4_, ...), custom_call_target="tpu_custom_call" | custom-call | flops 83886080 | bytes 3367072 | tf_op jit(solution)/shard_map/pallas_call | solution.py:470
  18.4 3.1 %collective-permute-done.3.refs_5_ = bf16[144,640]{1,0:T(8,128)(2,1)S(1)} collective-permute-done((bf16[144,640]{1,0:T(8,128)(2,1)S(1)}, bf16[144,640]{1,0:T(8,128)(2,1)S(1)}, u32[]{:S(2)}, u32[]{:S(2)}) %collective-permute-start.3) | collective-permute-done | bytes 184352 | tf_op jit(solution)/shard_map/ppermute | solution.py:516
  21.6 0.8 %shard_map.97 = (bf16[128,640]{1,0:T(8,128)(2,1)S(1)}, f32[8,128]{1,0:T(8,128)S(1)}, f32[8,640]{1,0:T(8,128)S(1)}) custom-call(s32[3]{0:T(128)S(1)} %get-tuple-element.40.refs_0_, s32[1]{0:T(128)} %bitcast.refs_0_.refs_1_, bf16[144,640]{1,0:T(8,128)(2,1)S(1)} %get-tuple-element.56.refs_2_, bf16[144,640]{1,0:T(8,128)(2,1)S(1)} %collective-permute-done.1.refs_3_.refs_6_, ...), custom_call_target="tpu_custom_call" | custom-call | flops 327680 | bytes 925696 | tf_op jit(solution)/shard_map/pallas_call | solution.py:470
  22.4 0.7 %shard_map.98 = (bf16[128,640]{1,0:T(8,128)(2,1)S(1)}, bf16[384,640]{1,0:T(8,128)(2,1)S(1)}, bf16[256,640]{1,0:T(8,128)(2,1)S(1)}) custom-call(s32[3]{0:T(128)S(1)} %get-tuple-element.40.refs_0_, s32[1]{0:T(128)} %bitcast.refs_0_.refs_1_, bf16[144,640]{1,0:T(8,128)(2,1)S(1)} %get-tuple-element.56.refs_2_, ...), custom_call_target="tpu_custom_call" | custom-call | flops 327680 | bytes 1925120 | tf_op jit(solution)/shard_map/pallas_call | solution.py:470
  23.1 0.3 collective-permute-start.8
  23.5 1.1 %collective-permute-start.4 = (bf16[384,640]{1,0:T(8,128)(2,1)S(1)}, bf16[384,640]{1,0:T(8,128)(2,1)S(1)}, u32[]{:S(2)}, u32[]{:S(2)}) collective-permute-start(bf16[384,640]{1,0:T(8,128)(2,1)S(1)} %get-tuple-element.63), channel_id=1, source_target_pairs={{0,4},{4,0},{8,12},{12,8},{16,20},{20,16},{24,28},{28,24},{1,5},{5... | collective-permute-start | bytes 1474568 | tf_op jit(solution)/shard_map/ppermute | solution.py:516
  24.6 1.8 %shard_map.94.refs_2_ = f32[256,640]{1,0:T(8,128)S(1)} custom-call(s32[3]{0:T(128)S(1)} %get-tuple-element.40.refs_0_, s32[1]{0:T(128)} %bitcast.refs_0_.refs_1_, bf16[256,2560]{1,0:T(8,128)(2,1)S(1)} %get-tuple-element.50.refs_2_, bf16[16,2560]{1,0:T(8,128)(2,1)S(1)} %get-tuple-element.51.refs_3_, f32[256,256]{1,0:T(8,128)S(1)} %get-tuple-element.52.refs_4_, ...), custom_call_target="tpu_custom_call" | custom-call | flops 83886080 | bytes 3367072 | tf_op jit(solution)/shard_map/pallas_call | solution.py:470
  26.4 1.5 %collective-permute-start.6 = (bf16[128,640]{1,0:T(8,128)(2,1)S(1)}, bf16[128,640]{1,0:T(8,128)(2,1)S(1)}, u32[]{:S(2)}, u32[]{:S(2)}) collective-permute-start(bf16[128,640]{1,0:T(8,128)(2,1)S(1)} %get-tuple-element.62.refs_8_.refs_9_), channel_id=1, source_target_pairs={{0,16},{4,20},{8,24},{12,28},{16,0},{20,4},{24,8},{28,12},{1,17},{... | collective-permute-start | bytes 491528 | tf_op jit(solution)/shard_map/ppermute | solution.py:516
  27.9 3.8 %collective-permute-start.5 = (bf16[128,640]{1,0:T(8,128)(2,1)S(1)}, bf16[128,640]{1,0:T(8,128)(2,1)S(1)}, u32[]{:S(2)}, u32[]{:S(2)}) collective-permute-start(bf16[128,640]{1,0:T(8,128)(2,1)S(1)} %get-tuple-element.64.refs_7_), channel_id=1, source_target_pairs={{0,12},{4,8},{16,28},{20,24},{1,13},{5,9},{17,29},{21,25},{2,14},{... | collective-permute-start | bytes 491528 | tf_op jit(solution)/shard_map/ppermute | solution.py:516
  31.6 1.8 %shard_map.99.refs_2_ = f32[256,640]{1,0:T(8,128)S(1)} custom-call(s32[3]{0:T(128)S(1)} %get-tuple-element.40.refs_0_, s32[1]{0:T(128)} %bitcast.refs_0_.refs_1_, bf16[256,2560]{1,0:T(8,128)(2,1)S(1)} %get-tuple-element.50.refs_2_, bf16[16,2560]{1,0:T(8,128)(2,1)S(1)} %get-tuple-element.51.refs_3_, f32[256,256]{1,0:T(8,128)S(1)} %get-tuple-element.52.refs_4_, ...), custom_call_target="tpu_custom_call" | custom-call | flops 83886080 | bytes 3367072 | tf_op jit(solution)/shard_map/pallas_call | solution.py:470
  33.4 1.3 %shard_map.100 = (f32[256,640]{1,0:T(8,128)S(1)}, f32[256,640]{1,0:T(8,128)S(1)}) custom-call(s32[3]{0:T(128)S(1)} %get-tuple-element.40.refs_0_, s32[1]{0:T(128)} %bitcast.refs_0_.refs_1_, f32[256,640]{1,0:T(8,128)S(1)} %shard_map.95.refs_6_.refs_2_, bf16[256,128]{1,0:T(8,128)(2,1)S(1)} %get-tuple-element.49.refs_3_.refs_2_, ...), custom_call_target="tpu_custom_call" | custom-call | flops 2200000000 | bytes 4087808 | tf_op jit(solution)/shard_map/pallas_call | solution.py:470
  34.7 0.1 collective-permute-done.6.refs_12_
  34.8 1.7 %collective-permute-start.7 = (bf16[128,640]{1,0:T(8,128)(2,1)S(1)}, bf16[128,640]{1,0:T(8,128)(2,1)S(1)}, u32[]{:S(2)}, u32[]{:S(2)}) collective-permute-start(bf16[128,640]{1,0:T(8,128)(2,1)S(1)} %collective-permute-done.6.refs_12_), channel_id=1, source_target_pairs={{0,12},{4,8},{8,4},{12,0},{16,28},{20,24},{24,20},{28,16},{1,13},{... | collective-permute-start | bytes 491528 | tf_op jit(solution)/shard_map/ppermute | solution.py:516
  36.5 0.0 collective-permute-start.9
  36.5 1.7 %collective-permute-start.10 = (bf16[128,640]{1,0:T(8,128)(2,1)S(1)}, bf16[128,640]{1,0:T(8,128)(2,1)S(1)}, u32[]{:S(2)}, u32[]{:S(2)}) collective-permute-start(bf16[128,640]{1,0:T(8,128)(2,1)S(1)} %collective-permute-done.6.refs_12_), channel_id=1, source_target_pairs={{0,8},{4,12},{8,0},{12,4},{16,24},{20,28},{24,16},{28,20},{1,9},{5... | collective-permute-start | bytes 491528 | tf_op jit(solution)/shard_map/ppermute | solution.py:516
  38.3 1.3 %shard_map.101 = (f32[256,640]{1,0:T(8,128)S(1)}, f32[256,640]{1,0:T(8,128)S(1)}) custom-call(s32[3]{0:T(128)S(1)} %get-tuple-element.40.refs_0_, s32[1]{0:T(128)} %bitcast.refs_0_.refs_1_, f32[256,640]{1,0:T(8,128)S(1)} %shard_map.99.refs_2_, bf16[256,128]{1,0:T(8,128)(2,1)S(1)} %get-tuple-element.49.refs_3_.refs_2_, ...), custom_call_target="tpu_custom_call" | custom-call | flops 2200000000 | bytes 4395008 | tf_op jit(solution)/shard_map/pallas_call | solution.py:470
  39.6 1.3 %shard_map.102 = (f32[256,640]{1,0:T(8,128)S(1)}, f32[256,640]{1,0:T(8,128)S(1)}) custom-call(s32[3]{0:T(128)S(1)} %get-tuple-element.40.refs_0_, s32[1]{0:T(128)} %bitcast.refs_0_.refs_1_, f32[256,640]{1,0:T(8,128)S(1)} %shard_map.96.refs_7_.refs_2_, bf16[256,128]{1,0:T(8,128)(2,1)S(1)} %get-tuple-element.49.refs_3_.refs_2_, ...), custom_call_target="tpu_custom_call" | custom-call | flops 2200000000 | bytes 4722688 | tf_op jit(solution)/shard_map/pallas_call | solution.py:470
  40.8 0.5 %collective-permute-done.7.refs_9_ = bf16[128,640]{1,0:T(8,128)(2,1)S(1)} collective-permute-done((bf16[128,640]{1,0:T(8,128)(2,1)S(1)}, bf16[128,640]{1,0:T(8,128)(2,1)S(1)}, u32[]{:S(2)}, u32[]{:S(2)}) %collective-permute-start.7) | collective-permute-done | bytes 163872 | tf_op jit(solution)/shard_map/ppermute | solution.py:516
  41.3 1.6 %shard_map.103 = (f32[256,640]{1,0:T(8,128)S(1)}, f32[256,640]{1,0:T(8,128)S(1)}) custom-call(s32[3]{0:T(128)S(1)} %get-tuple-element.40.refs_0_, s32[1]{0:T(128)} %bitcast.refs_0_.refs_1_, f32[256,640]{1,0:T(8,128)S(1)} %shard_map.94.refs_2_, bf16[256,128]{1,0:T(8,128)(2,1)S(1)} %get-tuple-element.49.refs_3_.refs_2_, ...), custom_call_target="tpu_custom_call" | custom-call | flops 2200000000 | bytes 6033408 | tf_op jit(solution)/shard_map/pallas_call | solution.py:470
  42.9 0.2 collective-permute-done.10.refs_10_
  43.1 2.2 %shard_map.104 = bf16[256,2560]{1,0:T(8,128)(2,1)} custom-call(s32[3]{0:T(128)S(1)} %get-tuple-element.40.refs_0_, s32[1]{0:T(128)} %bitcast.refs_0_.refs_1_, bf16[256,128]{1,0:T(8,128)(2,1)S(1)} %get-tuple-element.49.refs_3_.refs_2_, f32[256,640]{1,0:T(8,128)S(1)} %get-tuple-element.71.refs_3_, f32[256,640]{1,0:T(8,128)S(1)} %get-tuple-element.72.refs_4_, ...), custom_call_target="tpu_custom_call" | custom-call | flops 167772160 | bytes 5646336 | tf_op jit(solution)/shard_map/pallas_call | solution.py:470
  (14 shorter events, 0.0 us)
Async XLA Ops:
  0.9 8.6 %collective-permute-start = (bf16[16,2816]{1,0:T(8,128)(2,1)S(1)}, bf16[16,2816]{1,0:T(8,128)(2,1)S(1)}, u32[]{:S(2)}, u32[]{:S(2)}) collective-permute-start(bf16[16,2816]{1,0:T(8,128)(2,1)S(1)} %slice.3), channel_id=1, source_target_pairs={{0,4},{4,8},{8,12},{12,16},{16,20},{20,24},{24,28},{28,0},{1,5},{5... | collective-permute-start | bytes 270344 | tf_op jit(solution)/shard_map/ppermute | solution.py:516
  7.5 6.6 %copy-start = (f32[40,20,256]{2,0,1:T(8,128)S(1)}, f32[40,20,256]{2,0,1:T(8,128)}, u32[]{:S(2)}) copy-start(f32[40,20,256]{2,0,1:T(8,128)} %param.14) | copy-start | bytes 2457604
  9.5 5.4 %copy-start.1 = (f32[40]{0:T(128)S(1)}, f32[40]{0:T(128)}, u32[]{:S(2)}) copy-start(f32[40]{0:T(128)} %refs_8_.11) | copy-start | bytes 484
  10.5 7.9 %collective-permute-start.1 = (bf16[144,640]{1,0:T(8,128)(2,1)S(1)}, bf16[144,640]{1,0:T(8,128)(2,1)S(1)}, u32[]{:S(2)}, u32[]{:S(2)}) collective-permute-start(bf16[144,640]{1,0:T(8,128)(2,1)S(1)} %get-tuple-element.57), channel_id=1, source_target_pairs={{0,4},{4,0},{8,12},{12,8},{16,20},{20,16},{24,28},{28,24},{1,5},{5... | collective-permute-start | bytes 552968 | tf_op jit(solution)/shard_map/ppermute | solution.py:516
  10.6 7.8 %collective-permute-start.2 = (bf16[144,640]{1,0:T(8,128)(2,1)S(1)}, bf16[144,640]{1,0:T(8,128)(2,1)S(1)}, u32[]{:S(2)}, u32[]{:S(2)}) collective-permute-start(bf16[144,640]{1,0:T(8,128)(2,1)S(1)} %get-tuple-element.58.refs_7_), channel_id=1, source_target_pairs={{0,8},{4,12},{8,0},{12,4},{16,24},{20,28},{24,16},{28,20},{1,9},{5... | collective-permute-start | bytes 552968 | tf_op jit(solution)/shard_map/ppermute | solution.py:516
  11.7 9.8 %collective-permute-start.3 = (bf16[144,640]{1,0:T(8,128)(2,1)S(1)}, bf16[144,640]{1,0:T(8,128)(2,1)S(1)}, u32[]{:S(2)}, u32[]{:S(2)}) collective-permute-start(bf16[144,640]{1,0:T(8,128)(2,1)S(1)} %get-tuple-element.59), channel_id=1, source_target_pairs={{0,12},{4,8},{8,4},{12,0},{16,28},{20,24},{24,20},{28,16},{1,13},{... | collective-permute-start | bytes 552968 | tf_op jit(solution)/shard_map/ppermute | solution.py:516
  21.6 3.0 %copy-start.3 = (f32[2560]{0:T(1024)S(1)}, f32[2560]{0:T(1024)}, u32[]{:S(2)}) copy-start(f32[2560]{0:T(1024)} %param.16) | copy-start | bytes 30724
  23.1 13.4 %collective-permute-start.8 = (bf16[256,640]{1,0:T(8,128)(2,1)S(1)}, bf16[256,640]{1,0:T(8,128)(2,1)S(1)}, u32[]{:S(2)}, u32[]{:S(2)}) collective-permute-start(bf16[256,640]{1,0:T(8,128)(2,1)S(1)} %get-tuple-element.68), channel_id=1, source_target_pairs={{0,8},{4,12},{8,0},{12,4},{16,24},{20,28},{24,16},{28,20},{1,9},{5... | collective-permute-start | bytes 983048 | tf_op jit(solution)/shard_map/ppermute | solution.py:516
  23.5 16.1 %collective-permute-start.4 = (bf16[384,640]{1,0:T(8,128)(2,1)S(1)}, bf16[384,640]{1,0:T(8,128)(2,1)S(1)}, u32[]{:S(2)}, u32[]{:S(2)}) collective-permute-start(bf16[384,640]{1,0:T(8,128)(2,1)S(1)} %get-tuple-element.63), channel_id=1, source_target_pairs={{0,4},{4,0},{8,12},{12,8},{16,20},{20,16},{24,28},{28,24},{1,5},{5... | collective-permute-start | bytes 1474568 | tf_op jit(solution)/shard_map/ppermute | solution.py:516
  26.4 8.4 %collective-permute-start.6 = (bf16[128,640]{1,0:T(8,128)(2,1)S(1)}, bf16[128,640]{1,0:T(8,128)(2,1)S(1)}, u32[]{:S(2)}, u32[]{:S(2)}) collective-permute-start(bf16[128,640]{1,0:T(8,128)(2,1)S(1)} %get-tuple-element.62.refs_8_.refs_9_), channel_id=1, source_target_pairs={{0,16},{4,20},{8,24},{12,28},{16,0},{20,4},{24,8},{28,12},{1,17},{... | collective-permute-start | bytes 491528 | tf_op jit(solution)/shard_map/ppermute | solution.py:516
  27.8 5.5 %copy-start.2 = (bf16[256,2560]{1,0:T(8,128)(2,1)S(1)}, bf16[256,2560]{1,0:T(8,128)(2,1)}, u32[]{:S(2)}) copy-start(bf16[256,2560]{1,0:T(8,128)(2,1)} %refs_8_.15) | copy-start | bytes 3932164
  27.9 13.0 %collective-permute-start.5 = (bf16[128,640]{1,0:T(8,128)(2,1)S(1)}, bf16[128,640]{1,0:T(8,128)(2,1)S(1)}, u32[]{:S(2)}, u32[]{:S(2)}) collective-permute-start(bf16[128,640]{1,0:T(8,128)(2,1)S(1)} %get-tuple-element.64.refs_7_), channel_id=1, source_target_pairs={{0,12},{4,8},{16,28},{20,24},{1,13},{5,9},{17,29},{21,25},{2,14},{... | collective-permute-start | bytes 491528 | tf_op jit(solution)/shard_map/ppermute | solution.py:516
  34.8 6.5 %collective-permute-start.7 = (bf16[128,640]{1,0:T(8,128)(2,1)S(1)}, bf16[128,640]{1,0:T(8,128)(2,1)S(1)}, u32[]{:S(2)}, u32[]{:S(2)}) collective-permute-start(bf16[128,640]{1,0:T(8,128)(2,1)S(1)} %collective-permute-done.6.refs_12_), channel_id=1, source_target_pairs={{0,12},{4,8},{8,4},{12,0},{16,28},{20,24},{24,20},{28,16},{1,13},{... | collective-permute-start | bytes 491528 | tf_op jit(solution)/shard_map/ppermute | solution.py:516
  36.5 6.3 %collective-permute-start.9 = (bf16[128,640]{1,0:T(8,128)(2,1)S(1)}, bf16[128,640]{1,0:T(8,128)(2,1)S(1)}, u32[]{:S(2)}, u32[]{:S(2)}) collective-permute-start(bf16[128,640]{1,0:T(8,128)(2,1)S(1)} %collective-permute-done.6.refs_12_), channel_id=1, source_target_pairs={{0,4},{4,0},{8,12},{12,8},{16,20},{20,16},{24,28},{28,24},{1,5},{5... | collective-permute-start | bytes 491528 | tf_op jit(solution)/shard_map/ppermute | solution.py:516
  36.5 6.5 %collective-permute-start.10 = (bf16[128,640]{1,0:T(8,128)(2,1)S(1)}, bf16[128,640]{1,0:T(8,128)(2,1)S(1)}, u32[]{:S(2)}, u32[]{:S(2)}) collective-permute-start(bf16[128,640]{1,0:T(8,128)(2,1)S(1)} %collective-permute-done.6.refs_12_), channel_id=1, source_target_pairs={{0,8},{4,12},{8,0},{12,4},{16,24},{20,28},{24,16},{28,20},{1,9},{5... | collective-permute-start | bytes 491528 | tf_op jit(solution)/shard_map/ppermute | solution.py:516
